TPU v7x, 32 devices: a whole 2x2x4 slice. The times are simulated.
32 devices in a mesh: teacher: 4 (over x, core), vocab: 8 (over z, y).
Axes of the slice: x: 2, y: 2, z: 4, core: 2. Of those that a mesh axis runs over, the one named last changes fastest.
Arguments:
- teacher_hidden: bfloat16 [4, 128, 2048], P('teacher', 'vocab'), may hold values from -32 to 32
- teacher_head: bfloat16 [2048, 16384], P('teacher', 'vocab'), may hold values from -1 to 1
- student_hidden: bfloat16 [128, 2048], P(None, 'teacher'), may hold values from -32 to 32
- student_head: bfloat16 [2048, 16384], P('teacher', 'vocab'), may hold values from -1 to 1
- labels: int32 [128], P('teacher'), may hold values from 0 to 16383
Outputs:
- ce_matrix: float32 [128, 4, 4], P('teacher')
- agreement: float32 [128, 4], P('teacher')
- student_grad: float32 [2048, 16384], P('teacher', 'vocab')
All inputs are finite; a program needn't handle non-finite values.
Results may differ from a plain program's by a relative error of at most 0.0065.
Values may be sent and summed in bfloat16 or wider, within the bound.
No kernel may reach another device: no remote copies, remote signals or barrier semaphores. Data moves between devices by JAX's collectives and lax.ppermute only.
A program may use at most 64 MiB of HBM per device.

v0:
```python
import jax
import jax.numpy as jnp
from jax import lax
from jax.sharding import PartitionSpec as P

HARD_SHARE = 0.3


def teacher_normalizer(logits):
    highest = lax.pmax(jnp.max(logits, axis=1), "vocab")
    summed = lax.psum(jnp.sum(jnp.exp(logits - highest[:, None]), axis=1), "vocab")
    return highest + jnp.log(summed)


def student_normalizer(logits):
    highest = lax.pmax(jnp.max(logits, axis=1), "vocab")
    summed = lax.psum(jnp.sum(jnp.exp(logits - highest[:, None]), axis=1), "vocab")
    return highest + jnp.log(summed)


def student_scores(student_hidden, student_head):
    return lax.psum_scatter(
        jnp.dot(student_hidden, student_head, preferred_element_type=jnp.float32),
        "teacher",
        scatter_dimension=0,
        tiled=True,
    )


def on_device(teacher_hidden, teacher_head, student_hidden, student_head, labels):
    teachers = lax.axis_size("teacher")
    block_rows = student_hidden.shape[0] // teachers
    shard_width = teacher_head.shape[1]
    gathered = lax.all_gather(teacher_hidden, "vocab", axis=1, tiled=True)
    flat_rows = gathered[0]
    columns = flat_rows
    logits = jnp.dot(
        columns,
        lax.all_gather(teacher_head, "teacher", axis=0, tiled=True),
        preferred_element_type=jnp.float32,
    )
    log_norm = teacher_normalizer(logits)
    log_prob = (logits - log_norm[:, None]).astype(jnp.bfloat16)
    exchanged = lax.all_to_all(log_prob[None], "teacher", split_axis=1, concat_axis=0, tiled=True)
    teacher_prob = jnp.exp(exchanged.astype(jnp.float32)).astype(jnp.bfloat16)
    cross_local = -jnp.einsum(
        "itv,jtv->tij", teacher_prob, exchanged, preferred_element_type=jnp.float32
    )
    cross_matrix = lax.psum(cross_local, "vocab")
    disagree = jnp.mean(cross_matrix, axis=1)
    inverse = 1.0 / (1.0 + disagree)
    weights = inverse / jnp.sum(inverse, axis=1, keepdims=True)
    soft_mix = jnp.sum(weights.T[:, :, None] * teacher_prob.astype(jnp.float32), axis=0)
    col_offset = lax.axis_index("vocab") * shard_width
    columns = lax.broadcasted_iota(jnp.int32, (block_rows, shard_width), 1) + col_offset
    onehot = (columns == labels[:, None]).astype(jnp.float32)
    target = (1.0 - HARD_SHARE) * soft_mix + HARD_SHARE * onehot
    student_logits = student_scores(student_hidden, student_head)
    student_norm = student_normalizer(student_logits)
    student_prob = jnp.exp(student_logits - student_norm[:, None])
    residual = (student_prob - target).astype(jnp.bfloat16)
    student_grad = lax.dot_general(
        student_hidden,
        lax.all_gather(residual, "teacher", axis=0, tiled=True),
        (((0,), (0,)), ((), ())),
        preferred_element_type=jnp.float32,
    )
    return (cross_matrix, weights * teachers, student_grad)


def solution(mesh):
    return jax.shard_map(
        on_device,
        mesh=mesh,
        in_specs=(
            P("teacher", "vocab", None),
            P("teacher", "vocab"),
            P(None, "teacher"),
            P("teacher", "vocab"),
            P("teacher"),
        ),
        out_specs=(P("teacher", None, None), P("teacher", None), P("teacher", "vocab")),
        check_vma=False,
    )
```

profile of v0, /device:TPU:0, one launch (start us, length us, event | category | flops | bytes accessed | tf_op | source)
XLA Modules:
  0.0 229.7 jit_solution(2376637356905215207)
XLA Ops:
  7.2 0.0 copy-start
  7.2 0.0 copy-start.4
  7.2 0.0 reduce-scatter.2.cloned.1.call-start
  7.2 1.5 copy-done
  8.8 2.3 %fusion.6 = f32[128,2048]{1,0:T(8,128)} fusion(bf16[128,512]{1,0:T(8,128)(2,1)} %param.7, bf16[512,2048]{1,0:T(8,128)(2,1)S(1)} %copy-done), kind=kOutput, calls=%fused_computation.22 | convolution fusion | flops 268435456 | bytes 3276800 | tf_op jit(solution)/shard_map/dot_general | solution.py:23
  11.1 0.0 reduce-scatter.2.cloned.1.call-update
  11.1 0.0 all-gather.2.cloned.1.call-start
  11.2 0.7 all-gather.2.cloned.1.call-update
  11.9 0.0 copy-done.4
  11.9 35.2 %all_gather.9 = bf16[1,128,2048]{2,1,0:T(8,128)(2,1)} all-gather(bf16[1,16,2048]{2,1,0:T(8,128)(2,1)S(1)} %copy-done.4), channel_id=1, replica_groups=mesh['teacher'=4,'vocab'=8] {'vocab'}, dimensions={1}, use_global_device_ids=true | all-gather | bytes 589824 | tf_op jit(solution)/shard_map/all_gather | solution.py:34
  47.1 0.0 reduce-scatter.2.cloned.1.call-done
  47.1 1.1 reduce_max.19
  48.2 50.6 %all-gather.2.cloned.1.call-done = bf16[2048,2048]{1,0:T(8,128)(2,1)} async-done(((bf16[512,2048]{1,0:T(8,128)(2,1)}), bf16[2048,2048]{1,0:T(8,128)(2,1)}) %all-gather.2.cloned.1.call-update) | async-done | bytes 8388624 | tf_op jit(solution)/shard_map/all_gather | solution.py:39
  98.8 4.9 %fusion.5 = (f32[128]{0:T(128)S(1)}, f32[128,2048]{1,0:T(8,128)S(1)}) fusion(bf16[2048,2048]{1,0:T(8,128)(2,1)} %all-gather.2.cloned.1.call-done, bf16[1,128,2048]{2,1,0:T(8,128)(2,1)} %all_gather.9), kind=kOutput, calls=%fused_computation.20 | convolution fusion | flops 1074003840 | bytes 9961984 | tf_op jit(solution)/shard_map/dot_general | solution.py:37
  103.7 0.0 copy-start.1
  103.7 21.5 %all-reduce.1 = (f32[128]{0:T(128)S(1)}, f32[32]{0:T(128)S(1)}) all-reduce(f32[128]{0:T(128)S(1)} %get-tuple-element.18, f32[32]{0:T(128)S(1)} %reduce_max.19), channel_id=1, replica_groups=mesh['teacher'=4,'vocab'=8] {'vocab'}, use_global_device_ids=true, to_apply=%region_1.0 | all-reduce | flops 160 | bytes 1280 | tf_op jit(solution)/shard_map/pmax | solution.py:10
  125.2 0.3 exponential_reduce_fusion
  125.5 17.1 %psum.21 = f32[128]{0:T(128)S(1)} all-reduce(f32[128]{0:T(128)S(1)} %exponential_reduce_fusion), channel_id=1, replica_groups=mesh['teacher'=4,'vocab'=8] {'vocab'}, use_global_device_ids=true, to_apply=%region_3.0 | all-reduce | flops 128 | bytes 1024 | tf_op jit(solution)/shard_map/psum | solution.py:11
  142.7 0.1 fusion
  142.8 0.8 copy.30
  143.6 0.5 broadcast.52
  144.1 4.5 %reduce = bf16[128,2048]{1,0:T(8,128)(2,1)} reduce(bf16[128,1,2048]{2,1,0:T(2,128)(2,1)S(1)} %bitcast.22, bf16[]{:T(256)} %broadcast.52), dimensions={1}, to_apply=%bitcast.20.reduce_sub_computation | reduce | bytes 1048578
  148.6 2.2 reshape.19
  150.9 4.1 %all-to-all-start = ((bf16[4,2,32768]{2,1,0:T(2,128)(2,1)}), bf16[4,2,32768]{2,1,0:T(2,128)(2,1)}, u32[]{:S(2)}, u32[]{:S(2)}) async-start(bf16[4,2,32768]{2,1,0:T(2,128)(2,1)} %reshape.19), calls=%async_computation | async-start | bytes 1048576 | tf_op jit(solution)/shard_map/all_to_all | solution.py:44
  155.0 0.0 copy-done.1
  155.0 0.2 exponential_reduce_fusion.1
  155.2 0.0 copy-start.3
  155.2 8.7 %all-to-all-done = bf16[4,2,32768]{2,1,0:T(2,128)(2,1)} async-done(((bf16[4,2,32768]{2,1,0:T(2,128)(2,1)}), bf16[4,2,32768]{2,1,0:T(2,128)(2,1)}, u32[]{:S(2)}, u32[]{:S(2)}) %all-to-all-start) | async-done | bytes 524320 | tf_op jit(solution)/shard_map/all_to_all | solution.py:44
  163.9 2.2 reshape.20
  166.1 0.3 copy.23
  166.4 0.0 copy-start.2
  166.4 0.8 copy-done.2
  167.2 0.8 convolution_negate_fusion
  168.1 35.8 %all-reduce = (f32[32,4,4]{2,1,0:T(4,128)S(1)}, f32[32]{0:T(128)S(1)}) all-reduce(f32[32,4,4]{2,1,0:T(4,128)S(1)} %convolution_negate_fusion, f32[32]{0:T(128)S(1)} %exponential_reduce_fusion.1), channel_id=1, replica_groups=mesh['teacher'=4,'vocab'=8] {'vocab'}, use_global_device_ids=true, to_apply=%region_4.0 | all-reduce | flops 544 | bytes 4352 | tf_op jit(solution)/shard_map/psum | solution.py:49
  203.8 0.7 copy.20
  204.6 0.1 divide_reduce_fusion
  204.7 0.1 fusion.4
  204.8 0.7 copy.21
  205.4 2.0 multiply_reduce_fusion
  207.5 0.8 subtract_convert_fusion.1
  208.3 6.5 %all_gather.11 = bf16[128,2048]{1,0:T(8,128)(2,1)S(1)} all-gather(bf16[32,2048]{1,0:T(8,128)(2,1)S(1)} %subtract_convert_fusion.1), channel_id=1, replica_groups=mesh['teacher'=4,'vocab'=8] {'teacher'}, dimensions={0}, use_global_device_ids=true | all-gather | bytes 655360 | tf_op jit(solution)/shard_map/all_gather | solution.py:64
  214.8 0.0 copy-done.3
  214.8 2.7 %convolution_bitcast_fusion = f32[512,2048]{0,1:T(8,128)} fusion(bf16[128,2048]{1,0:T(8,128)(2,1)S(1)} %all_gather.11, bf16[128,512]{1,0:T(8,128)(2,1)S(1)} %copy-done.3), kind=kOutput, calls=%fused_computation | convolution fusion | flops 268435456 | bytes 4849664 | tf_op jit(solution)/shard_map/dot_general | solution.py:62
  217.5 5.3 %copy.22 = f32[512,2048]{1,0:T(8,128)} copy(f32[512,2048]{0,1:T(8,128)} %convolution_bitcast_fusion) | data formatting | bytes 8388608
  (4 shorter events, 0.1 us)
Async XLA Ops:
  7.2 1.6 copy-start
  7.2 4.7 %copy-start.4 = (bf16[1,16,2048]{2,1,0:T(8,128)(2,1)S(1)}, bf16[1,16,2048]{2,1,0:T(8,128)(2,1)}, u32[]{:S(2)}) copy-start(bf16[1,16,2048]{2,1,0:T(8,128)(2,1)} %param.5) | copy-start | bytes 196612
  7.2 39.9 %reduce-scatter.2.cloned.1.call-start = ((), (), s32[]{:S(2)}) async-start(), calls=%async_computation.3 | async-start | bytes 1310720 | tf_op jit(solution)/shard_map/reduce_scatter | solution.py:22
  11.1 87.7 %all-gather.2.cloned.1.call-start = ((), (), s32[]{:S(2)}) async-start(), calls=%async_computation.2 | async-start | bytes 10485760 | tf_op jit(solution)/shard_map/all_gather | solution.py:39
  103.7 51.3 %copy-start.1 = (f32[32,2048]{1,0:T(8,128)S(1)}, f32[32,2048]{1,0:T(8,128)}, u32[]{:S(2)}) copy-start(f32[32,2048]{1,0:T(8,128)} %reduce-scatter.2.cloned.1.call-done) | copy-start | bytes 786436
  150.9 13.0 %all-to-all-start = ((bf16[4,2,32768]{2,1,0:T(2,128)(2,1)}), bf16[4,2,32768]{2,1,0:T(2,128)(2,1)}, u32[]{:S(2)}, u32[]{:S(2)}) async-start(bf16[4,2,32768]{2,1,0:T(2,128)(2,1)} %reshape.19), calls=%async_computation | async-start | bytes 1048576 | tf_op jit(solution)/shard_map/all_to_all | solution.py:44
  155.2 59.6 %copy-start.3 = (bf16[128,512]{1,0:T(8,128)(2,1)S(1)}, bf16[128,512]{1,0:T(8,128)(2,1)}, u32[]{:S(2)}) copy-start(bf16[128,512]{1,0:T(8,128)(2,1)} %param.7) | copy-start | bytes 393220
  166.4 0.8 copy-start.2
Sparse Core Ops, SparseCore 0:
  11.2 27.5 reduce-scatter.1
  40.5 58.2 all-gather.1
where the time goes:
time: 230 us
  blocking collectives  116 us (50%)
  waiting for transfers between devices  59.9 us (26%)
  local copies, waits for them, and re-layouts  15.1 us (7%)
  between operations  14.2 us (6%)
  matrix products  10.7 us (5%)
  other arithmetic  9.36 us (4%)
  starting transfers between devices  4.2 us (2%)
    all_gather x1, waiting for transfers between devices, on_device(): lax.all_gather(teacher_head, 'teacher', axis=0, tiled=True)  50.6 us
    psum x1, blocking collectives, on_device(): cross_matrix = lax.psum(cross_local, 'vocab')  35.8 us
    all_gather x1, blocking collectives, on_device(): gathered = lax.all_gather(teacher_hidden, 'vocab', axis=1, tiled=True)  35.2 us
    pmax x1, blocking collectives, teacher_normalizer(): highest = lax.pmax(jnp.max(logits, axis=1), 'vocab')  21.5 us
    psum x1, blocking collectives, teacher_normalizer(): lax.psum(jnp.sum(jnp.exp(logits - highest[:, None]), axis=1), 'vocab')  17.1 us
    unnamed x17, local copies, waits for them, and re-layouts  14.3 us
    all_to_all x1, waiting for transfers between devices, on_device(): lax.all_to_all(log_prob[None], 'teacher', split_axis=1, concat_axis=0, ti...  8.65 us
    all_gather x1, blocking collectives, on_device(): lax.all_gather(residual, 'teacher', axis=0, tiled=True)  6.51 us
  transfers between devices with their start and end apart: 3, of which 2 were waited for; matrix products, arithmetic and copies ran while one was open for 1% of the time, Pallas kernels for 0%

commit v1 on v0

v1 whole, which is shorter than its diff:
```python
import functools

import jax
import jax.numpy as jnp
from jax import lax
from jax.experimental import pallas as pl
from jax.experimental.pallas import tpu as pltpu
from jax.sharding import PartitionSpec as P

HARD_SHARE = 0.3
LANES = 128


def swap(value, axis, mask):
    count = lax.axis_size(axis)
    return lax.ppermute(value, axis, [(i, i ^ mask) for i in range(count)])


def call(body, outs, args, grid=None, in_specs=None, out_specs=None, scratch=(), flops=0, moved=0):
    extra = {} if grid is None else {"grid": grid}
    if in_specs is not None:
        extra["in_specs"] = in_specs
    if out_specs is not None:
        extra["out_specs"] = out_specs
    return pl.pallas_call(
        body,
        out_shape=outs,
        scratch_shapes=list(scratch),
        compiler_params=pltpu.CompilerParams(vmem_limit_bytes=48 * 1024 * 1024),
        cost_estimate=pl.CostEstimate(flops=flops, bytes_accessed=moved, transcendentals=0),
        **extra,
    )(*args)


def partial_body(hidden_ref, own_ref, sib_ref, out_ref):
    half = own_ref.shape[0]
    out_ref[...] = jnp.dot(
        hidden_ref[:, :half], own_ref[...], preferred_element_type=jnp.float32
    ) + jnp.dot(hidden_ref[:, half:], sib_ref[...], preferred_element_type=jnp.float32)


def stats_body(kept_ref, came_ref, student_ref, logits_ref, lse_ref, mean_ref):
    teachers, rows, _ = kept_ref.shape
    lane = lax.broadcasted_iota(jnp.int32, (rows, LANES), 1)
    lse = jnp.zeros((rows, LANES), jnp.float32)
    mean = jnp.zeros((rows, LANES), jnp.float32)
    tops = []
    for i in range(teachers):
        value = kept_ref[i] + came_ref[i].astype(jnp.float32)
        logits_ref[i] = value
        tops.append(jnp.max(value, axis=1, keepdims=True))
    for i in range(teachers):
        weight = jnp.exp(logits_ref[i] - tops[i])
        total = jnp.sum(weight, axis=1, keepdims=True)
        group = (lane >= i * teachers) & (lane < (i + 1) * teachers)
        lse = jnp.where(group, tops[i] + jnp.log(total), lse)
        for j in range(teachers):
            local = jnp.sum(weight * (logits_ref[j] - tops[j]), axis=1, keepdims=True) / total + tops[j]
            mean = jnp.where(lane == i * teachers + j, local, mean)
    value = student_ref[...]
    top = jnp.max(value, axis=1, keepdims=True)
    total = jnp.sum(jnp.exp(value - top), axis=1, keepdims=True)
    lse_ref[...] = jnp.where(lane == teachers * teachers, top + jnp.log(total), lse)
    mean_ref[...] = mean


def merge(lse, mean, other_lse, other_mean):
    high = jnp.maximum(lse, other_lse)
    low = jnp.minimum(lse, other_lse)
    both = high + jnp.log1p(jnp.exp(low - high))
    return both, jnp.exp(lse - both) * mean + jnp.exp(other_lse - both) * other_mean


def residual_body(logits_ref, student_ref, lse_ref, mean_ref, label_ref, cross_ref, agree_ref, residual_ref):
    teachers, rows, width = logits_ref.shape
    lane = lax.broadcasted_iota(jnp.int32, (rows, LANES), 1)
    lse, mean = lse_ref[...], mean_ref[...]
    norms = [lse[:, i * teachers : i * teachers + 1] for i in range(teachers)]
    cross = jnp.zeros((rows, LANES), jnp.float32)
    inverse = []
    for j in range(teachers):
        spread = jnp.zeros((rows, 1), jnp.float32)
        for i in range(teachers):
            at = i * teachers + j
            entry = norms[j] - mean[:, at : at + 1]
            cross = jnp.where(lane == at, entry, cross)
            spread = spread + entry
        inverse.append(1.0 / (1.0 + spread * (1.0 / teachers)))
    cross_ref[...] = cross
    total = inverse[0]
    for i in range(1, teachers):
        total = total + inverse[i]
    weights = [value / total for value in inverse]
    agree = jnp.zeros((rows, LANES), jnp.float32)
    for i in range(teachers):
        agree = jnp.where(lane == i, weights[i] * teachers, agree)
    agree_ref[...] = agree
    at = teachers * teachers
    target = jnp.where(
        lax.broadcasted_iota(jnp.int32, (rows, width), 1) == label_ref[...], HARD_SHARE, 0.0
    )
    for i in range(teachers):
        log_prob = (logits_ref[i] - norms[i]).astype(jnp.bfloat16).astype(jnp.float32)
        prob = jnp.exp(log_prob).astype(jnp.bfloat16).astype(jnp.float32)
        target = target + ((1.0 - HARD_SHARE) * weights[i]) * prob
    prob = jnp.exp(student_ref[...] - lse[:, at : at + 1])
    residual_ref[...] = (prob - target).astype(jnp.bfloat16)


def grad_body(hidden_ref, residual_ref, out_ref):
    out_ref[...] = jnp.dot(hidden_ref[...], residual_ref[...], preferred_element_type=jnp.float32)


def fast(teacher_hidden, teacher_head, student_hidden, student_head, labels):
    teachers = lax.axis_size("teacher")
    shards = lax.axis_size("vocab")
    chips = teachers // 2
    rows, width = teacher_head.shape
    tokens = student_hidden.shape[0]
    piece = tokens // shards // 2
    block = tokens // teachers
    x = lax.axis_index("teacher") // 2
    core = lax.axis_index("teacher") % 2
    f32 = jnp.float32

    sib_head = swap(teacher_head, "teacher", 1)
    sib_labels = swap(labels, "teacher", 1)

    ordered = student_hidden.reshape(chips, shards // chips, 2, piece, rows).transpose(0, 2, 1, 3, 4)
    ordered = ordered.reshape(tokens, rows)
    student = lax.psum_scatter(
        jnp.dot(ordered, student_head, preferred_element_type=f32), "teacher", scatter_dimension=0, tiled=True
    )
    ordered_t = ordered.T

    mine = teacher_hidden[0].reshape(2, piece, chips, 2, rows)
    parts = []
    for to in range(teachers):
        half = mine[to % 2, :, to // 2]
        parts.append(jnp.concatenate([half[:, to % 2], half[:, 1 - to % 2]], axis=1))
    spread = jnp.broadcast_to(jnp.stack(parts)[:, None], (teachers, shards, piece, 2 * rows))
    spread = spread.reshape(teachers * shards, piece, 2 * rows)
    came = lax.all_to_all(spread, ("teacher", "vocab"), 0, 0, tiled=True)
    came = came.reshape(teachers * shards * piece, 2 * rows)

    step = min(width, 512)
    partial = call(
        partial_body,
        jax.ShapeDtypeStruct((came.shape[0], width), f32),
        (came, teacher_head, sib_head),
        grid=(width // step,),
        in_specs=[
            pl.BlockSpec(came.shape, lambda i: (0, 0)),
            pl.BlockSpec((rows, step), lambda i: (0, i)),
            pl.BlockSpec((rows, step), lambda i: (0, i)),
        ],
        out_specs=pl.BlockSpec((came.shape[0], step), lambda i: (0, i)),
        flops=2 * came.shape[0] * 2 * rows * width,
        moved=4 * rows * width,
    )
    partial = partial.reshape(teachers, chips, block, width)
    kept = lax.dynamic_index_in_dim(partial, x, 1, keepdims=False)
    sent = lax.dynamic_index_in_dim(partial, 1 - x, 1, keepdims=False).astype(jnp.float16)
    other = swap(sent, "teacher", 2).astype(f32)

    flat = jax.ShapeDtypeStruct((block, LANES), f32)
    logits, lse, mean = call(
        stats_body,
        (jax.ShapeDtypeStruct((teachers, block, width), f32), flat, flat),
        (kept, other, student),
    )
    mask = 1
    while mask < shards:
        both = swap(jnp.stack([lse, mean]), "vocab", mask)
        lse, mean = merge(lse, mean, both[0], both[1])
        mask *= 2

    pair = jnp.where(core == 0, jnp.stack([labels, sib_labels]), jnp.stack([sib_labels, labels]))
    chosen = lax.dynamic_index_in_dim(
        pair.reshape(shards // chips, 2, piece), core, 1, keepdims=False
    ).reshape(block, 1)
    local_label = chosen - lax.axis_index("vocab") * width
    cross, agree, residual = call(
        residual_body,
        (flat, flat, jax.ShapeDtypeStruct((block, width), jnp.bfloat16)),
        (logits, student, lse, mean, local_label),
    )
    gathered = lax.all_gather(residual, "teacher", axis=0, tiled=True)
    grad = call(
        grad_body,
        jax.ShapeDtypeStruct((rows, width), f32),
        (ordered_t, gathered),
        grid=(width // step,),
        in_specs=[
            pl.BlockSpec((rows, tokens), lambda i: (0, 0)),
            pl.BlockSpec((tokens, step), lambda i: (0, i)),
        ],
        out_specs=pl.BlockSpec((rows, step), lambda i: (0, i)),
        flops=2 * rows * tokens * width,
        moved=4 * rows * width,
    )

    small = jnp.concatenate([cross[:, : teachers * teachers], agree[:, :teachers]], axis=1)
    sib_small = swap(small, "teacher", 1)
    lead = jnp.where(core == 0, small, sib_small).reshape(2, shards // chips // 2, piece, -1)
    trail = jnp.where(core == 0, sib_small, small).reshape(2, shards // chips // 2, piece, -1)
    lead = lax.dynamic_index_in_dim(lead, core, 0, keepdims=False)
    trail = lax.dynamic_index_in_dim(trail, core, 0, keepdims=False)
    small = jnp.stack([lead, trail], axis=1).reshape(block, -1)
    cross = small[:, : teachers * teachers].reshape(block, teachers, teachers)
    return cross, small[:, teachers * teachers :], grad


def normalizer(logits):
    highest = lax.pmax(jnp.max(logits, axis=1), "vocab")
    summed = lax.psum(jnp.sum(jnp.exp(logits - highest[:, None]), axis=1), "vocab")
    return highest + jnp.log(summed)


def general(teacher_hidden, teacher_head, student_hidden, student_head, labels):
    teachers = lax.axis_size("teacher")
    block_rows = student_hidden.shape[0] // teachers
    shard_width = teacher_head.shape[1]
    gathered = lax.all_gather(teacher_hidden, "vocab", axis=1, tiled=True)
    logits = jnp.dot(
        gathered[0],
        lax.all_gather(teacher_head, "teacher", axis=0, tiled=True),
        preferred_element_type=jnp.float32,
    )
    log_prob = (logits - normalizer(logits)[:, None]).astype(jnp.bfloat16)
    exchanged = lax.all_to_all(log_prob[None], "teacher", split_axis=1, concat_axis=0, tiled=True)
    teacher_prob = jnp.exp(exchanged.astype(jnp.float32)).astype(jnp.bfloat16)
    cross_local = -jnp.einsum("itv,jtv->tij", teacher_prob, exchanged, preferred_element_type=jnp.float32)
    cross_matrix = lax.psum(cross_local, "vocab")
    inverse = 1.0 / (1.0 + jnp.mean(cross_matrix, axis=1))
    weights = inverse / jnp.sum(inverse, axis=1, keepdims=True)
    soft_mix = jnp.sum(weights.T[:, :, None] * teacher_prob.astype(jnp.float32), axis=0)
    col_offset = lax.axis_index("vocab") * shard_width
    columns = lax.broadcasted_iota(jnp.int32, (block_rows, shard_width), 1) + col_offset
    onehot = (columns == labels[:, None]).astype(jnp.float32)
    target = (1.0 - HARD_SHARE) * soft_mix + HARD_SHARE * onehot
    student_logits = lax.psum_scatter(
        jnp.dot(student_hidden, student_head, preferred_element_type=jnp.float32),
        "teacher",
        scatter_dimension=0,
        tiled=True,
    )
    student_prob = jnp.exp(student_logits - normalizer(student_logits)[:, None])
    residual = (student_prob - target).astype(jnp.bfloat16)
    student_grad = lax.dot_general(
        student_hidden,
        lax.all_gather(residual, "teacher", axis=0, tiled=True),
        (((0,), (0,)), ((), ())),
        preferred_element_type=jnp.float32,
    )
    return (cross_matrix, weights * teachers, student_grad)


def solution(mesh):
    body = fast if mesh.shape["teacher"] == 4 and mesh.shape["vocab"] == 8 else general
    return jax.shard_map(
        body,
        mesh=mesh,
        in_specs=(
            P("teacher", "vocab", None),
            P("teacher", "vocab"),
            P(None, "teacher"),
            P("teacher", "vocab"),
            P("teacher"),
        ),
        out_specs=(P("teacher", None, None), P("teacher", None), P("teacher", "vocab")),
        check_vma=False,
    )
```

time: 230 us -> 94.5 us (0.41)
  blocking collectives: 116 us -> 7.43 us
  waiting for transfers between devices: 59.9 us -> 38.3 us
  Pallas kernels: 0 us -> 8.42 us
  matrix products: 10.7 us -> 2.37 us
  other arithmetic: 9.36 us -> 1.56 us
  starting transfers between devices: 4.2 us -> 10.6 us
  local copies, waits for them, and re-layouts: 15.1 us -> 11 us
    psum x2 -> x0, blocking collectives: 52.9 us -> none  [the longest x1 35.8 us: on_device(): cross_matrix = lax.psum(cross_local, 'vocab')]
    all_gather x1 -> x0, waiting for transfers between devices: 50.6 us -> none  [on_device(): lax.all_gather(teacher_head, 'teacher', axis=0, tiled=True)]
    all_gather x2 -> x1, blocking collectives: 41.8 us -> 7.43 us  [fast(): gathered = lax.all_gather(residual, 'teacher', axis=0, tiled=True)]
    ppermute x0 -> x7, waiting for transfers between devices: none -> 21.9 us  [swap(): return lax.ppermute(value, axis, [(i, i ^ mask) for i in range(count)])]
    pmax x1 -> x0, blocking collectives: 21.5 us -> none  [teacher_normalizer(): highest = lax.pmax(jnp.max(logits, axis=1), 'vocab')]
    pallas_call x0 -> x4, Pallas kernels: none -> 8.42 us  [call(): pl.pallas_call(body, out_shape=outs, scratch_shapes=list(scratch), compil...]
    dot_general x4 -> x1, matrix products: 10.7 us -> 2.37 us  [fast(): jnp.dot(ordered, student_head, preferred_element_type=f32)]
    unnamed x17 -> x19, local copies, waits for them, and re-layouts: 14.3 us -> 6.62 us
  transfers between devices with their start and end apart: 3 -> 9, of which waited for: 2 -> 5; matrix products, arithmetic and copies ran while one was open for 1% -> 8% of each run, Pallas kernels for 0% -> 7%
where the time goes in v1:
time: 94.5 us; the launch traced here: 94 us
  waiting for transfers between devices  38.3 us (41%)
  between operations  14.3 us (15%)
  local copies, waits for them, and re-layouts  11 us (12%)
  starting transfers between devices  10.6 us (11%)
  Pallas kernels  8.42 us (9%)
  blocking collectives  7.43 us (8%)
  matrix products  2.37 us (3%)
  other arithmetic  1.56 us (2%)
    ppermute x7, waiting for transfers between devices, swap(): return lax.ppermute(value, axis, [(i, i ^ mask) for i in range(count)])  21.9 us
    all_to_all x1, waiting for transfers between devices, fast(): came = lax.all_to_all(spread, ('teacher', 'vocab'), 0, 0, tiled=True)  16.3 us
    pallas_call x4, Pallas kernels, call(): pl.pallas_call(body, out_shape=outs, scratch_shapes=list(scratch), compil...  8.42 us
    all_gather x1, blocking collectives, fast(): gathered = lax.all_gather(residual, 'teacher', axis=0, tiled=True)  7.43 us
    all_to_all x1, starting transfers between devices, fast(): came = lax.all_to_all(spread, ('teacher', 'vocab'), 0, 0, tiled=True)  6.94 us
    unnamed x19, local copies, waits for them, and re-layouts  6.62 us
    ppermute x7, starting transfers between devices, swap(): return lax.ppermute(value, axis, [(i, i ^ mask) for i in range(count)])  3.64 us
    dot_general x1, matrix products, fast(): jnp.dot(ordered, student_head, preferred_element_type=f32)  2.37 us
  transfers between devices with their start and end apart: 9, of which 5 were waited for; matrix products, arithmetic and copies ran while one was open for 8% of the time, Pallas kernels for 7%

profile of v1, /device:TPU:0, one launch (start us, length us, event | category | flops | bytes accessed | tf_op | source)
XLA Modules:
  0.0 94.0 jit_solution(8395549888782152384)
XLA Ops:
  7.2 0.0 copy-start
  7.2 0.0 reduce-scatter.2.cloned.1.call-start
  7.2 0.5 collective-permute-start
  7.7 1.6 %copy.17 = bf16[2,2,4,8,512]{4,3,2,1,0:T(8,128)(2,1)} copy(bf16[2,2,4,8,512]{4,3,1,2,0:T(8,128)(2,1)} %bitcast.139) | data formatting | bytes 262144 | tf_op jit(solution)/shard_map/transpose | solution.py:129
  9.4 2.4 %fusion.9 = f32[128,2048]{1,0:T(8,128)} fusion(bf16[128,512]{1,0:T(8,128)(2,1)} %bitcast.24, bf16[512,2048]{1,0:T(8,128)(2,1)S(1)} %copy-done), kind=kOutput, calls=%fused_computation.48 | convolution fusion | flops 268435456 | bytes 3276800 | tf_op jit(solution)/shard_map/dot_general | solution.py:132
  11.7 0.0 reduce-scatter.2.cloned.1.call-update
  11.8 0.0 copy-done.7
  11.9 0.9 broadcast_in_dim.2
  12.7 6.9 %all-to-all-start = ((bf16[32,8,1024]{2,1,0:T(8,128)(2,1)}), bf16[32,8,1024]{2,1,0:T(8,128)(2,1)S(1)}, u32[]{:S(2)}, u32[]{:S(2)}) async-start(bf16[32,8,1024]{2,1,0:T(8,128)(2,1)} %bitcast.17), calls=%async_computation | async-start | bytes 1048576 | tf_op jit(solution)/shard_map/all_to_all | solution.py:143
  19.7 16.3 %all-to-all-done = bf16[32,8,1024]{2,1,0:T(8,128)(2,1)S(1)} async-done(((bf16[32,8,1024]{2,1,0:T(8,128)(2,1)}), bf16[32,8,1024]{2,1,0:T(8,128)(2,1)S(1)}, u32[]{:S(2)}, u32[]{:S(2)}) %all-to-all-start) | async-done | bytes 524320 | tf_op jit(solution)/shard_map/all_to_all | solution.py:143
  36.0 0.0 collective-permute-done.sib_ref
  36.0 1.6 %copy-done.2 = bf16[512,2048]{1,0:T(8,128)(2,1)S(1)} copy-done((bf16[512,2048]{1,0:T(8,128)(2,1)S(1)}, bf16[512,2048]{1,0:T(8,128)(2,1)}, u32[]{:S(2)}) %copy-start.2) | copy-done | bytes 2097176
  37.6 3.7 %shard_map.76 = f32[256,2048]{1,0:T(8,128)S(1)} custom-call(bf16[256,1024]{1,0:T(8,128)(2,1)S(1)} %bitcast.127, bf16[512,2048]{1,0:T(8,128)(2,1)S(1)} %copy-done.2, bf16[512,2048]{1,0:T(8,128)(2,1)} %collective-permute-done.sib_ref), custom_call_target="tpu_custom_call" | custom-call | flops 1073741824 | bytes 4194304 | tf_op jit(solution)/shard_map/pallas_call | solution.py:25
  41.3 1.1 %fusion = (f16[4,32,2048]{2,1,0:T(8,128)(2,1)S(1)}, f32[4,32,2048]{2,1,0:T(8,128)}) fusion(f32[4,2,32,2048]{3,2,1,0:T(8,128)S(1)} %bitcast.126, s32[]{:T(128)S(6)} %select_n.53, s32[]{:T(128)S(6)} %select_n.52), kind=kLoop, calls=%fused_computation.2 | loop fusion | flops 262144 | bytes 3670024 | tf_op jit(solution)/shard_map/convert_element_type | solution.py:163
  42.5 0.6 collective-permute-start.1
  43.0 12.9 %collective-permute-done.1 = f16[4,32,2048]{2,1,0:T(8,128)(2,1)S(1)} collective-permute-done((f16[4,32,2048]{2,1,0:T(8,128)(2,1)S(1)}, f16[4,32,2048]{2,1,0:T(8,128)(2,1)S(1)}, u32[]{:S(2)}, u32[]{:S(2)}) %collective-permute-start.1) | collective-permute-done | bytes 524320 | tf_op jit(solution)/shard_map/ppermute | solution.py:16
  56.0 0.1 convert_element_type.11.came_ref
  56.1 0.0 reduce-scatter.2.cloned.1.call-done.student_ref
  56.1 0.0 copy-start.1
  56.1 1.2 %copy-done.1 = f32[4,32,2048]{2,1,0:T(8,128)S(1)} copy-done((f32[4,32,2048]{2,1,0:T(8,128)S(1)}, f32[4,32,2048]{2,1,0:T(8,128)}, u32[]{:S(2)}) %copy-start.1) | copy-done | bytes 1048600
  57.3 0.9 %copy-done.5 = f32[32,2048]{1,0:T(8,128)S(1)} copy-done((f32[32,2048]{1,0:T(8,128)S(1)}, f32[32,2048]{1,0:T(8,128)}, u32[]{:S(2)}) %copy-start.5) | copy-done | bytes 262168
  58.3 0.7 shard_map.77
  59.0 0.0 copy-start.3
  59.0 1.0 %copy-done.3 = f32[4,32,2048]{2,1,0:T(8,128)} copy-done((f32[4,32,2048]{2,1,0:T(8,128)}, f32[4,32,2048]{2,1,0:T(8,128)S(1)}, u32[]{:S(2)}) %copy-start.3) | copy-done | bytes 1048600
  60.0 1.3 %collective-permute-start.2 = (f32[2,32,128]{2,1,0:T(8,128)S(1)}, f32[2,32,128]{2,1,0:T(8,128)S(1)}, u32[]{:S(2)}, u32[]{:S(2)}) collective-permute-start(f32[2,32,128]{2,1,0:T(8,128)S(1)} %pad_maximum_fusion.1), channel_id=1, source_target_pairs={{0,1},{1,0},{2,3},{3,2},{4,5},{5,4},{6,7},{7,6},{8,9},{9,8},{10,11... | collective-permute-start | bytes 98312 | tf_op jit(solution)/shard_map/ppermute | solution.py:16
  61.2 2.6 %collective-permute-done.2 = f32[2,32,128]{2,1,0:T(8,128)S(1)} collective-permute-done((f32[2,32,128]{2,1,0:T(8,128)S(1)}, f32[2,32,128]{2,1,0:T(8,128)S(1)}, u32[]{:S(2)}, u32[]{:S(2)}) %collective-permute-start.2) | collective-permute-done | bytes 32800 | tf_op jit(solution)/shard_map/ppermute | solution.py:16
  63.9 1.2 %collective-permute-start.3 = (f32[2,32,128]{2,1,0:T(8,128)S(1)}, f32[2,32,128]{2,1,0:T(8,128)S(1)}, u32[]{:S(2)}, u32[]{:S(2)}) collective-permute-start(f32[2,32,128]{2,1,0:T(8,128)S(1)} %pad_maximum_fusion.2), channel_id=1, source_target_pairs={{0,2},{1,3},{2,0},{3,1},{4,6},{5,7},{6,4},{7,5},{8,10},{9,11},{10,... | collective-permute-start | bytes 98312 | tf_op jit(solution)/shard_map/ppermute | solution.py:16
  65.1 0.0 collective-permute-start.5
  65.1 1.0 %copy.21 = bf16[128,512]{0,1:T(8,128)(2,1)S(1)} copy(bf16[128,512]{1,0:T(8,128)(2,1)} %bitcast.24) | data formatting | bytes 262144 | tf_op jit(solution)/shard_map/reshape | solution.py:130
  66.2 1.7 %collective-permute-done.3 = f32[2,32,128]{2,1,0:T(8,128)S(1)} collective-permute-done((f32[2,32,128]{2,1,0:T(8,128)S(1)}, f32[2,32,128]{2,1,0:T(8,128)S(1)}, u32[]{:S(2)}, u32[]{:S(2)}) %collective-permute-start.3) | collective-permute-done | bytes 32800 | tf_op jit(solution)/shard_map/ppermute | solution.py:16
  67.9 0.1 fusion.4
  68.0 0.1 collective-permute-start.4
  68.0 0.0 collective-permute-done.5
  68.1 0.1 select_n.56
  68.2 0.1 sub.56.label_ref
  68.3 4.6 %collective-permute-done.4 = f32[2,32,128]{2,1,0:T(8,128)S(1)} collective-permute-done((f32[2,32,128]{2,1,0:T(8,128)S(1)}, f32[2,32,128]{2,1,0:T(8,128)S(1)}, u32[]{:S(2)}, u32[]{:S(2)}) %collective-permute-start.4) | collective-permute-done | bytes 32800 | tf_op jit(solution)/shard_map/ppermute | solution.py:16
  72.9 0.0 copy-start.4
  72.9 1.2 %copy-done.4 = f32[4,32,2048]{2,1,0:T(8,128)S(1)} copy-done((f32[4,32,2048]{2,1,0:T(8,128)S(1)}, f32[4,32,2048]{2,1,0:T(8,128)}, u32[]{:S(2)}) %copy-start.4) | copy-done | bytes 1048600
  74.1 1.1 %shard_map.78 = (f32[32,128]{1,0:T(8,128)S(1)}, f32[32,128]{1,0:T(8,128)S(1)}, bf16[32,2048]{1,0:T(8,128)(2,1)S(1)}) custom-call(f32[4,32,2048]{2,1,0:T(8,128)S(1)} %copy-done.4, f32[32,2048]{1,0:T(8,128)S(1)} %copy-done.6, f32[32,128]{1,0:T(8,128)S(1)} %get-tuple-element.30.lse_ref, f32[32,128]{1,0:T(8,128)S(1)} %get-tuple-element.29.mean_ref, ...), custom_call_target="tpu_custom_call" | custom-call | tf_op jit(solution)/shard_map/pallas_call | solution.py:25
  75.3 0.1 pad_maximum_fusion.4
  75.4 0.0 collective-permute-start.6
  75.4 7.4 %all_gather.3.residual_ref = bf16[128,2048]{1,0:T(8,128)(2,1)S(1)} all-gather(bf16[32,2048]{1,0:T(8,128)(2,1)S(1)} %get-tuple-element.14), channel_id=1, replica_groups=mesh['teacher'=4,'vocab'=8] {'teacher'}, dimensions={0}, use_global_device_ids=true | all-gather | bytes 655360 | tf_op jit(solution)/shard_map/all_gather | solution.py:188
  82.8 2.9 %shard_map.79 = f32[512,2048]{1,0:T(8,128)} custom-call(bf16[512,128]{1,0:T(8,128)(2,1)S(1)} %bitcast.128, bf16[128,2048]{1,0:T(8,128)(2,1)S(1)} %all_gather.3.residual_ref), custom_call_target="tpu_custom_call" | custom-call | flops 268435456 | bytes 4194304 | tf_op jit(solution)/shard_map/pallas_call | solution.py:25
  85.7 0.0 collective-permute-done.6
  85.7 0.1 broadcast_select_fusion.1
  85.8 0.1 slice.107
  85.9 0.7 copy.20
  86.5 0.7 copy.22
  (27 shorter events, 0.2 us)
Async XLA Ops:
  7.2 2.2 %copy-start = (bf16[512,2048]{1,0:T(8,128)(2,1)S(1)}, bf16[512,2048]{1,0:T(8,128)(2,1)}, u32[]{:S(2)}) copy-start(bf16[512,2048]{1,0:T(8,128)(2,1)} %param.8) | copy-start | bytes 6291460
  7.2 48.9 %reduce-scatter.2.cloned.1.call-start = ((), (), s32[]{:S(2)}) async-start(), calls=%async_computation.2 | async-start | bytes 1310720 | tf_op jit(solution)/shard_map/reduce_scatter | solution.py:131
  7.2 28.8 %collective-permute-start = (bf16[512,2048]{1,0:T(8,128)(2,1)}, bf16[512,2048]{1,0:T(8,128)(2,1)}, u32[]{:S(2)}, u32[]{:S(2)}) collective-permute-start(bf16[512,2048]{1,0:T(8,128)(2,1)} %own_ref.1), channel_id=1, source_target_pairs={{0,8},{8,0},{16,24},{24,16},{1,9},{9,1},{17,25},{25,17},{2,10},{10... | collective-permute-start | bytes 6291464 | tf_op jit(solution)/shard_map/ppermute | solution.py:16
  9.4 2.4 %copy-start.7 = (bf16[1,16,2048]{2,1,0:T(8,128)(2,1)S(1)}, bf16[1,16,2048]{2,1,0:T(8,128)(2,1)}, u32[]{:S(2)}) copy-start(bf16[1,16,2048]{2,1,0:T(8,128)(2,1)} %param.5) | copy-start | bytes 196612
  12.7 23.3 %all-to-all-start = ((bf16[32,8,1024]{2,1,0:T(8,128)(2,1)}), bf16[32,8,1024]{2,1,0:T(8,128)(2,1)S(1)}, u32[]{:S(2)}, u32[]{:S(2)}) async-start(bf16[32,8,1024]{2,1,0:T(8,128)(2,1)} %bitcast.17), calls=%async_computation | async-start | bytes 1048576 | tf_op jit(solution)/shard_map/all_to_all | solution.py:143
  36.0 1.6 %copy-start.2 = (bf16[512,2048]{1,0:T(8,128)(2,1)S(1)}, bf16[512,2048]{1,0:T(8,128)(2,1)}, u32[]{:S(2)}) copy-start(bf16[512,2048]{1,0:T(8,128)(2,1)} %own_ref.1) | copy-start | bytes 6291460
  42.5 22.6 %copy-start.8 = (s32[32]{0:T(128)S(1)}, s32[32]{0:T(128)}, u32[]{:S(2)}) copy-start(s32[32]{0:T(128)} %param.9) | copy-start | bytes 388
  42.5 13.5 %collective-permute-start.1 = (f16[4,32,2048]{2,1,0:T(8,128)(2,1)S(1)}, f16[4,32,2048]{2,1,0:T(8,128)(2,1)S(1)}, u32[]{:S(2)}, u32[]{:S(2)}) collective-permute-start(f16[4,32,2048]{2,1,0:T(8,128)(2,1)S(1)} %get-tuple-element.23), channel_id=1, source_target_pairs={{0,16},{8,24},{16,0},{24,8},{1,17},{9,25},{17,1},{25,9},{2,18},{10... | collective-permute-start | bytes 1572872 | tf_op jit(solution)/shard_map/ppermute | solution.py:16
  56.1 1.2 %copy-start.1 = (f32[4,32,2048]{2,1,0:T(8,128)S(1)}, f32[4,32,2048]{2,1,0:T(8,128)}, u32[]{:S(2)}) copy-start(f32[4,32,2048]{2,1,0:T(8,128)} %get-tuple-element.24.kept_ref) | copy-start | bytes 3145732
  57.3 0.9 %copy-start.5 = (f32[32,2048]{1,0:T(8,128)S(1)}, f32[32,2048]{1,0:T(8,128)}, u32[]{:S(2)}) copy-start(f32[32,2048]{1,0:T(8,128)} %reduce-scatter.2.cloned.1.call-done.student_ref) | copy-start | bytes 786436
  58.3 14.6 %copy-start.6 = (f32[32,2048]{1,0:T(8,128)S(1)}, f32[32,2048]{1,0:T(8,128)}, u32[]{:S(2)}) copy-start(f32[32,2048]{1,0:T(8,128)} %reduce-scatter.2.cloned.1.call-done.student_ref) | copy-start | bytes 786436
  59.0 1.0 %copy-start.3 = (f32[4,32,2048]{2,1,0:T(8,128)}, f32[4,32,2048]{2,1,0:T(8,128)S(1)}, u32[]{:S(2)}) copy-start(f32[4,32,2048]{2,1,0:T(8,128)S(1)} %get-tuple-element.9.logits_ref) | copy-start | bytes 3145732
  60.0 3.9 %collective-permute-start.2 = (f32[2,32,128]{2,1,0:T(8,128)S(1)}, f32[2,32,128]{2,1,0:T(8,128)S(1)}, u32[]{:S(2)}, u32[]{:S(2)}) collective-permute-start(f32[2,32,128]{2,1,0:T(8,128)S(1)} %pad_maximum_fusion.1), channel_id=1, source_target_pairs={{0,1},{1,0},{2,3},{3,2},{4,5},{5,4},{6,7},{7,6},{8,9},{9,8},{10,11... | collective-permute-start | bytes 98312 | tf_op jit(solution)/shard_map/ppermute | solution.py:16
  63.9 4.0 %collective-permute-start.3 = (f32[2,32,128]{2,1,0:T(8,128)S(1)}, f32[2,32,128]{2,1,0:T(8,128)S(1)}, u32[]{:S(2)}, u32[]{:S(2)}) collective-permute-start(f32[2,32,128]{2,1,0:T(8,128)S(1)} %pad_maximum_fusion.2), channel_id=1, source_target_pairs={{0,2},{1,3},{2,0},{3,1},{4,6},{5,7},{6,4},{7,5},{8,10},{9,11},{10,... | collective-permute-start | bytes 98312 | tf_op jit(solution)/shard_map/ppermute | solution.py:16
  65.1 2.9 %collective-permute-start.5 = (s32[32]{0:T(128)S(1)}, s32[32]{0:T(128)S(1)}, u32[]{:S(2)}, u32[]{:S(2)}) collective-permute-start(s32[32]{0:T(128)S(1)} %copy-done.8), channel_id=1, source_target_pairs={{0,8},{8,0},{16,24},{24,16},{1,9},{9,1},{17,25},{25,17},{2,10},{10... | collective-permute-start | bytes 392 | tf_op jit(solution)/shard_map/ppermute | solution.py:16
  68.0 4.9 %collective-permute-start.4 = (f32[2,32,128]{2,1,0:T(8,128)S(1)}, f32[2,32,128]{2,1,0:T(8,128)S(1)}, u32[]{:S(2)}, u32[]{:S(2)}) collective-permute-start(f32[2,32,128]{2,1,0:T(8,128)S(1)} %pad_maximum_fusion.3), channel_id=1, source_target_pairs={{0,4},{1,5},{2,6},{3,7},{4,0},{5,1},{6,2},{7,3},{8,12},{9,13},{10,... | collective-permute-start | bytes 98312 | tf_op jit(solution)/shard_map/ppermute | solution.py:16
  72.9 1.2 %copy-start.4 = (f32[4,32,2048]{2,1,0:T(8,128)S(1)}, f32[4,32,2048]{2,1,0:T(8,128)}, u32[]{:S(2)}) copy-start(f32[4,32,2048]{2,1,0:T(8,128)} %copy-done.3) | copy-start | bytes 3145732
  75.4 10.3 %collective-permute-start.6 = (f32[32,20]{1,0:T(8,128)S(1)}, f32[32,20]{1,0:T(8,128)S(1)}, u32[]{:S(2)}, u32[]{:S(2)}) collective-permute-start(f32[32,20]{1,0:T(8,128)S(1)} %pad_maximum_fusion.4), channel_id=1, source_target_pairs={{0,8},{8,0},{16,24},{24,16},{1,9},{9,1},{17,25},{25,17},{2,10},{10... | collective-permute-start | bytes 7688 | tf_op jit(solution)/shard_map/ppermute | solution.py:16
Sparse Core Ops, SparseCore 0:
  11.9 28.1 reduce-scatter.1

commit v2 on v1

--- a/solution.py
+++ b/solution.py
@@ -26,27 +26,39 @@
         body,
         out_shape=outs,
         scratch_shapes=list(scratch),
-        compiler_params=pltpu.CompilerParams(vmem_limit_bytes=48 * 1024 * 1024),
+        compiler_params=pltpu.CompilerParams(vmem_limit_bytes=16 * 1024 * 1024),
         cost_estimate=pl.CostEstimate(flops=flops, bytes_accessed=moved, transcendentals=0),
         **extra,
     )(*args)
 
 
-def partial_body(hidden_ref, own_ref, sib_ref, out_ref):
-    half = own_ref.shape[0]
-    out_ref[...] = jnp.dot(
-        hidden_ref[:, :half], own_ref[...], preferred_element_type=jnp.float32
-    ) + jnp.dot(hidden_ref[:, half:], sib_ref[...], preferred_element_type=jnp.float32)
-
-
-def stats_body(kept_ref, came_ref, student_ref, logits_ref, lse_ref, mean_ref):
+VMEM = pl.BlockSpec(memory_space=pltpu.VMEM)
+SMEM = pl.BlockSpec(memory_space=pltpu.SMEM)
+
+
+def partial_body(step, which_ref, hidden_ref, own_ref, sib_ref, out_ref):
+    teachers, _, block, depth = hidden_ref.shape
+    half = depth // 2
+    which = which_ref[0]
+    rows = jnp.concatenate([hidden_ref[i, which] for i in range(teachers)], axis=0)
+
+    @pl.loop(0, own_ref.shape[1] // step)
+    def _(at):
+        columns = pl.ds(pl.multiple_of(at * step, step), step)
+        value = jnp.dot(rows[:, :half], own_ref[:, columns], preferred_element_type=jnp.float32)
+        value += jnp.dot(rows[:, half:], sib_ref[:, columns], preferred_element_type=jnp.float32)
+        for i in range(teachers):
+            out_ref[i, :, columns] = value[i * block : (i + 1) * block]
+
+
+def stats_body(kept_ref, came_ref, student_ref, logits_ref, stats_ref):
     teachers, rows, _ = kept_ref.shape
     lane = lax.broadcasted_iota(jnp.int32, (rows, LANES), 1)
     lse = jnp.zeros((rows, LANES), jnp.float32)
     mean = jnp.zeros((rows, LANES), jnp.float32)
     tops = []
     for i in range(teachers):
-        value = kept_ref[i] + came_ref[i].astype(jnp.float32)
+        value = kept_ref[i] + came_ref[i]
         logits_ref[i] = value
         tops.append(jnp.max(value, axis=1, keepdims=True))
     for i in range(teachers):
@@ -60,42 +72,41 @@
     value = student_ref[...]
     top = jnp.max(value, axis=1, keepdims=True)
     total = jnp.sum(jnp.exp(value - top), axis=1, keepdims=True)
-    lse_ref[...] = jnp.where(lane == teachers * teachers, top + jnp.log(total), lse)
-    mean_ref[...] = mean
-
-
-def merge(lse, mean, other_lse, other_mean):
-    high = jnp.maximum(lse, other_lse)
-    low = jnp.minimum(lse, other_lse)
+    stats_ref[0] = jnp.where(lane == teachers * teachers, top + jnp.log(total), lse)
+    stats_ref[1] = mean
+
+
+def merge(one, two):
+    high = jnp.maximum(one[0], two[0])
+    low = jnp.minimum(one[0], two[0])
     both = high + jnp.log1p(jnp.exp(low - high))
-    return both, jnp.exp(lse - both) * mean + jnp.exp(other_lse - both) * other_mean
-
-
-def residual_body(logits_ref, student_ref, lse_ref, mean_ref, label_ref, cross_ref, agree_ref, residual_ref):
+    return jnp.stack([both, jnp.exp(one[0] - both) * one[1] + jnp.exp(two[0] - both) * two[1]])
+
+
+def residual_body(logits_ref, student_ref, stats_ref, label_ref, small_ref, residual_ref):
     teachers, rows, width = logits_ref.shape
     lane = lax.broadcasted_iota(jnp.int32, (rows, LANES), 1)
-    lse, mean = lse_ref[...], mean_ref[...]
+    lse, mean = stats_ref[0], stats_ref[1]
     norms = [lse[:, i * teachers : i * teachers + 1] for i in range(teachers)]
-    cross = jnp.zeros((rows, LANES), jnp.float32)
+    small = jnp.zeros((rows, LANES), jnp.float32)
     inverse = []
     for j in range(teachers):
         spread = jnp.zeros((rows, 1), jnp.float32)
         for i in range(teachers):
             at = i * teachers + j
             entry = norms[j] - mean[:, at : at + 1]
-            cross = jnp.where(lane == at, entry, cross)
+            small = jnp.where(lane == at, entry, small)
             spread = spread + entry
         inverse.append(1.0 / (1.0 + spread * (1.0 / teachers)))
-    cross_ref[...] = cross
     total = inverse[0]
     for i in range(1, teachers):
         total = total + inverse[i]
     weights = [value / total for value in inverse]
-    agree = jnp.zeros((rows, LANES), jnp.float32)
-    for i in range(teachers):
-        agree = jnp.where(lane == i, weights[i] * teachers, agree)
-    agree_ref[...] = agree
     at = teachers * teachers
+    for i in range(teachers):
+        small = jnp.where(lane == at + i, weights[i] * teachers, small)
+    square = jnp.concatenate([small, jnp.zeros((LANES - rows, LANES), jnp.float32)], axis=0)
+    small_ref[...] = square.T[: small_ref.shape[0]]
     target = jnp.where(
         lax.broadcasted_iota(jnp.int32, (rows, width), 1) == label_ref[...], HARD_SHARE, 0.0
     )
@@ -123,16 +134,6 @@
     core = lax.axis_index("teacher") % 2
     f32 = jnp.float32
 
-    sib_head = swap(teacher_head, "teacher", 1)
-    sib_labels = swap(labels, "teacher", 1)
-
-    ordered = student_hidden.reshape(chips, shards // chips, 2, piece, rows).transpose(0, 2, 1, 3, 4)
-    ordered = ordered.reshape(tokens, rows)
-    student = lax.psum_scatter(
-        jnp.dot(ordered, student_head, preferred_element_type=f32), "teacher", scatter_dimension=0, tiled=True
-    )
-    ordered_t = ordered.T
-
     mine = teacher_hidden[0].reshape(2, piece, chips, 2, rows)
     parts = []
     for to in range(teachers):
@@ -141,38 +142,54 @@
     spread = jnp.broadcast_to(jnp.stack(parts)[:, None], (teachers, shards, piece, 2 * rows))
     spread = spread.reshape(teachers * shards, piece, 2 * rows)
     came = lax.all_to_all(spread, ("teacher", "vocab"), 0, 0, tiled=True)
-    came = came.reshape(teachers * shards * piece, 2 * rows)
+    came = came.reshape(teachers, chips, block, 2 * rows)
+
+    student_hidden, student_head, teacher_head, labels, _ = lax.optimization_barrier(
+        (student_hidden, student_head, teacher_head, labels, spread)
+    )
+    sib_head = swap(teacher_head, "teacher", 1)
+    sib_labels = swap(labels, "teacher", 1)
+    ordered = student_hidden.reshape(chips, shards // chips, 2, piece, rows).transpose(0, 2, 1, 3, 4)
+    ordered = ordered.reshape(tokens, rows)
+    student = jnp.dot(ordered, student_head, preferred_element_type=f32).reshape(chips, 2, block, width)
+    student_own = lax.dynamic_index_in_dim(student, core, 1, keepdims=False)
+    student_sib = lax.dynamic_index_in_dim(student, 1 - core, 1, keepdims=False)
+    student = student_own + swap(student_sib, "teacher", 1)
+    student_own = lax.dynamic_index_in_dim(student, x, 0, keepdims=False)
+    student_far = lax.dynamic_index_in_dim(student, 1 - x, 0, keepdims=False)
+    student = student_own + swap(student_far, "teacher", 2)
+    ordered_t = ordered.T
 
     step = min(width, 512)
-    partial = call(
-        partial_body,
-        jax.ShapeDtypeStruct((came.shape[0], width), f32),
-        (came, teacher_head, sib_head),
-        grid=(width // step,),
-        in_specs=[
-            pl.BlockSpec(came.shape, lambda i: (0, 0)),
-            pl.BlockSpec((rows, step), lambda i: (0, i)),
-            pl.BlockSpec((rows, step), lambda i: (0, i)),
-        ],
-        out_specs=pl.BlockSpec((came.shape[0], step), lambda i: (0, i)),
-        flops=2 * came.shape[0] * 2 * rows * width,
-        moved=4 * rows * width,
-    )
-    partial = partial.reshape(teachers, chips, block, width)
-    kept = lax.dynamic_index_in_dim(partial, x, 1, keepdims=False)
-    sent = lax.dynamic_index_in_dim(partial, 1 - x, 1, keepdims=False).astype(jnp.float16)
+
+    def partial(which):
+        return call(
+            functools.partial(partial_body, step),
+            jax.ShapeDtypeStruct((teachers, block, width), f32),
+            (which.reshape(1).astype(jnp.int32), came, teacher_head, sib_head),
+            in_specs=[SMEM, VMEM, VMEM, VMEM],
+            out_specs=VMEM,
+            flops=2 * teachers * block * 2 * rows * width,
+            moved=4 * rows * width,
+        )
+
+    sent = partial(1 - x).astype(jnp.float16)
     other = swap(sent, "teacher", 2).astype(f32)
-
-    flat = jax.ShapeDtypeStruct((block, LANES), f32)
-    logits, lse, mean = call(
+    kept = partial(x)
+
+    logits, stats = call(
         stats_body,
-        (jax.ShapeDtypeStruct((teachers, block, width), f32), flat, flat),
+        (
+            jax.ShapeDtypeStruct((teachers, block, width), f32),
+            jax.ShapeDtypeStruct((2, block, LANES), f32),
+        ),
         (kept, other, student),
+        in_specs=[VMEM] * 3,
+        out_specs=(VMEM, VMEM),
     )
     mask = 1
     while mask < shards:
-        both = swap(jnp.stack([lse, mean]), "vocab", mask)
-        lse, mean = merge(lse, mean, both[0], both[1])
+        stats = merge(stats, swap(stats, "vocab", mask))
         mask *= 2
 
     pair = jnp.where(core == 0, jnp.stack([labels, sib_labels]), jnp.stack([sib_labels, labels]))
@@ -180,10 +197,16 @@
         pair.reshape(shards // chips, 2, piece), core, 1, keepdims=False
     ).reshape(block, 1)
     local_label = chosen - lax.axis_index("vocab") * width
-    cross, agree, residual = call(
+    entries = teachers * teachers + teachers
+    small, residual = call(
         residual_body,
-        (flat, flat, jax.ShapeDtypeStruct((block, width), jnp.bfloat16)),
-        (logits, student, lse, mean, local_label),
+        (
+            jax.ShapeDtypeStruct((-(-entries // 8) * 8, LANES), f32),
+            jax.ShapeDtypeStruct((block, width), jnp.bfloat16),
+        ),
+        (logits, student, stats, local_label),
+        in_specs=[VMEM] * 4,
+        out_specs=(VMEM, VMEM),
     )
     gathered = lax.all_gather(residual, "teacher", axis=0, tiled=True)
     grad = call(
@@ -200,15 +223,15 @@
         moved=4 * rows * width,
     )
 
-    small = jnp.concatenate([cross[:, : teachers * teachers], agree[:, :teachers]], axis=1)
+    small = small[:, :block]
     sib_small = swap(small, "teacher", 1)
-    lead = jnp.where(core == 0, small, sib_small).reshape(2, shards // chips // 2, piece, -1)
-    trail = jnp.where(core == 0, sib_small, small).reshape(2, shards // chips // 2, piece, -1)
-    lead = lax.dynamic_index_in_dim(lead, core, 0, keepdims=False)
-    trail = lax.dynamic_index_in_dim(trail, core, 0, keepdims=False)
-    small = jnp.stack([lead, trail], axis=1).reshape(block, -1)
-    cross = small[:, : teachers * teachers].reshape(block, teachers, teachers)
-    return cross, small[:, teachers * teachers :], grad
+    first = jnp.where(core == 0, small, sib_small).reshape(-1, 2, shards // chips // 2, piece)
+    second = jnp.where(core == 0, sib_small, small).reshape(-1, 2, shards // chips // 2, piece)
+    first = jnp.where(core == 0, first[:, 0], first[:, 1])
+    second = jnp.where(core == 0, second[:, 0], second[:, 1])
+    small = jnp.stack([first, second], axis=2).reshape(-1, block)
+    cross = small[: teachers * teachers].T.reshape(block, teachers, teachers)
+    return cross, small[teachers * teachers : entries].T, grad
 
 
 def normalizer(logits):

time: 94.5 us -> 78.9 us (0.83)
  between operations: 14.3 us -> 0.96 us
  waiting for transfers between devices: 38.3 us -> 30.8 us
  other arithmetic: 1.56 us -> 4.48 us
  starting transfers between devices: 10.6 us -> 12.9 us
  Pallas kernels: 8.42 us -> 10.4 us
  matrix products: 2.37 us -> 1.35 us
    ppermute x7 -> x9, waiting for transfers between devices: 21.9 us -> 17.7 us  [swap(): return lax.ppermute(value, axis, [(i, i ^ mask) for i in range(count)])]
    all_to_all x1, waiting for transfers between devices: 16.3 us -> 13.2 us  [fast(): came = lax.all_to_all(spread, ('teacher', 'vocab'), 0, 0, tiled=True)]
    add x2 -> x5, other arithmetic: 0.08 us -> 2.33 us  [the longest x1 1.26 us: fast(): student = student_own + swap(student_sib, 'teacher', 1)]
    pallas_call x4 -> x5, Pallas kernels: 8.42 us -> 10.4 us  [call(): pl.pallas_call(body, out_shape=outs, scratch_shapes=list(scratch), compil...]
    ppermute x7 -> x9, starting transfers between devices: 3.64 us -> 5.57 us  [swap(): return lax.ppermute(value, axis, [(i, i ^ mask) for i in range(count)])]
    transpose x1, local copies, waits for them, and re-layouts: 1.61 us -> 0.01 us  [fast(): student_hidden.reshape(chips, shards // chips, 2, piece, rows)]
    convert_element_type x1, other arithmetic: 0.07 us -> 1.11 us  [fast(): other = swap(sent, 'teacher', 2).astype(f32)]
    dot_general x1, matrix products: 2.37 us -> 1.35 us  [fast(): jnp.dot(ordered, student_head, preferred_element_type=f32)]
  transfers between devices with their start and end apart: 9 -> 10, of which waited for: 5 -> 5; matrix products, arithmetic and copies ran while one was open for 8% -> 6% of each run, Pallas kernels for 7% -> 11%
where the time goes in v2:
time: 78.9 us; the launch traced here: 78.4 us
  waiting for transfers between devices  30.8 us (39%)
  starting transfers between devices  12.9 us (16%)
  Pallas kernels  10.4 us (13%)
  local copies, waits for them, and re-layouts  10.1 us (13%)
  blocking collectives  7.43 us (9%)
  other arithmetic  4.48 us (6%)
  matrix products  1.35 us (2%)
  between operations  0.96 us (1%)
    ppermute x9, waiting for transfers between devices, swap(): return lax.ppermute(value, axis, [(i, i ^ mask) for i in range(count)])  17.7 us
    all_to_all x1, waiting for transfers between devices, fast(): came = lax.all_to_all(spread, ('teacher', 'vocab'), 0, 0, tiled=True)  13.2 us
    pallas_call x5, Pallas kernels, call(): pl.pallas_call(body, out_shape=outs, scratch_shapes=list(scratch), compil...  10.4 us
    all_gather x1, blocking collectives, fast(): gathered = lax.all_gather(residual, 'teacher', axis=0, tiled=True)  7.43 us
    all_to_all x1, starting transfers between devices, fast(): came = lax.all_to_all(spread, ('teacher', 'vocab'), 0, 0, tiled=True)  7.3 us
    unnamed x16, local copies, waits for them, and re-layouts  6.35 us
    ppermute x9, starting transfers between devices, swap(): return lax.ppermute(value, axis, [(i, i ^ mask) for i in range(count)])  5.57 us
  transfers between devices with their start and end apart: 10, of which 5 were waited for; matrix products, arithmetic and copies ran while one was open for 6% of the time, Pallas kernels for 11%

profile of v2, /device:TPU:0, one launch (start us, length us, event | category | flops | bytes accessed | tf_op | source)
XLA Modules:
  0.0 78.4 jit_solution(2041166980993612947)
XLA Ops:
  0.6 0.0 copy-start
  0.6 0.9 %slice_bitcast_fusion.3 = (bf16[8,2,512]{2,0,1:T(8,128)(2,1)S(1)}, bf16[8,2,512]{2,0,1:T(8,128)(2,1)S(1)}, bf16[8,2,512]{2,0,1:T(8,128)(2,1)S(1)}, bf16[8,2,512]{2,0,1:T(8,128)(2,1)S(1)}) fusion(bf16[2,8,2,2,512]{4,1,3,2,0:T(8,128)(2,1)} %bitcast.81), kind=kLoop, calls=%fused_computation.22 | loop fusion | bytes 131072 | tf_op jit(solution)/shard_map/squeeze | solution.py:140
  1.7 0.9 %broadcast_in_dim.2 = bf16[4,8,8,1024]{3,2,1,0:T(8,128)(2,1)} broadcast(bf16[4,8,1024]{2,1,0:T(8,128)(2,1)S(1)} %pad_maximum_fusion), dimensions={0,2,3} | broadcast | bytes 589824 | tf_op jit(solution)/shard_map/broadcast_in_dim | solution.py:142
  2.5 0.5 collective-permute-start
  3.0 1.3 %fusion = f32[2,2,32,2048]{3,2,1,0:T(8,128)S(1)} fusion(bf16[512,2048]{1,0:T(8,128)(2,1)S(1)} %copy-done, bf16[2,2,4,8,512]{4,3,1,2,0:T(8,128)(2,1)} %bitcast.76), kind=kOutput, calls=%fused_computation | convolution fusion | flops 268435456 | bytes 3276800 | tf_op jit(solution)/shard_map/dot_general | solution.py:154
  4.3 0.0 copy-start.5
  4.3 1.0 %copy-done.5 = f32[2,2,32,2048]{3,2,1,0:T(8,128)} copy-done((f32[2,2,32,2048]{3,2,1,0:T(8,128)}, f32[2,2,32,2048]{3,2,1,0:T(8,128)S(1)}, u32[]{:S(2)}) %copy-start.5) | copy-done | bytes 1048600
  5.3 0.1 collective-permute-start.2
  5.4 7.3 %all-to-all-start = ((bf16[32,8,1024]{2,1,0:T(8,128)(2,1)}), bf16[32,8,1024]{2,1,0:T(8,128)(2,1)S(1)}, u32[]{:S(2)}, u32[]{:S(2)}) async-start(bf16[32,8,1024]{2,1,0:T(8,128)(2,1)} %bitcast.18), calls=%async_computation | async-start | bytes 1048576 | tf_op jit(solution)/shard_map/all_to_all | solution.py:144
  12.8 1.3 %bitcast_add_fusion = f32[2,32,2048]{2,1,0:T(8,128)S(1)} fusion(f32[2,32,2048]{2,1,0:T(8,128)} %collective-permute-done.2, f32[2,2,32,2048]{3,2,1,0:T(8,128)} %copy-done.5, s32[]{:T(128)S(6)} %select_n.87), kind=kLoop, calls=%fused_computation.2 | loop fusion | flops 131072 | bytes 1572868 | tf_op jit(solution)/shard_map/add | solution.py:157
  14.1 1.8 %collective-permute-start.3 = (f32[32,2048]{1,0:T(8,128)S(1)}, f32[32,2048]{1,0:T(8,128)}, u32[]{:S(2)}, u32[]{:S(2)}) collective-permute-start(f32[32,2048]{1,0:T(8,128)S(1)} %dynamic-slice_bitcast_fusion.1), channel_id=1, source_target_pairs={{0,16},{8,24},{16,0},{24,8},{1,17},{9,25},{17,1},{25,9},{2,18},{10... | collective-permute-start | bytes 786440 | tf_op jit(solution)/shard_map/ppermute | solution.py:16
  15.9 13.2 %all-to-all-done = bf16[32,8,1024]{2,1,0:T(8,128)(2,1)S(1)} async-done(((bf16[32,8,1024]{2,1,0:T(8,128)(2,1)}), bf16[32,8,1024]{2,1,0:T(8,128)(2,1)S(1)}, u32[]{:S(2)}, u32[]{:S(2)}) %all-to-all-start) | async-done | bytes 524320 | tf_op jit(solution)/shard_map/all_to_all | solution.py:144
  29.1 1.6 %copy-done.1 = bf16[512,2048]{1,0:T(8,128)(2,1)S(1)} copy-done((bf16[512,2048]{1,0:T(8,128)(2,1)S(1)}, bf16[512,2048]{1,0:T(8,128)(2,1)}, u32[]{:S(2)}) %copy-start.1) | copy-done | bytes 2097176
  30.7 2.9 %shard_map.77 = f32[4,32,2048]{2,1,0:T(8,128)S(1)} custom-call(s32[1]{0:T(128)} %bitcast.20.which_ref, bf16[4,2,32,1024]{3,2,1,0:T(8,128)(2,1)S(1)} %bitcast.72, bf16[512,2048]{1,0:T(8,128)(2,1)S(1)} %copy-done.1, bf16[512,2048]{1,0:T(8,128)(2,1)} %collective-permute-done.sib_ref), custom_call_target="tpu_custom_call" | custom-call | flops 536870912 | bytes 4194304 | tf_op jit(solution)/shard_map/pallas_call | solution.py:25
  33.6 0.9 %convert_element_type.6 = f16[4,32,2048]{2,1,0:T(8,128)(2,1)} convert(f32[4,32,2048]{2,1,0:T(8,128)S(1)} %shard_map.77) | non-fusion elementwise | flops 262144 | bytes 1572864 | tf_op jit(solution)/shard_map/convert_element_type | solution.py:176
  34.4 0.5 collective-permute-start.1
  35.0 1.0 %bitcast_add_fusion.1.student_ref = f32[32,2048]{1,0:T(8,128)S(1)} fusion(f32[32,2048]{1,0:T(8,128)} %collective-permute-done.3, f32[2,32,2048]{2,1,0:T(8,128)S(1)} %bitcast_add_fusion, s32[]{:T(128)S(6)} %select_n.89), kind=kLoop, calls=%fused_computation.4 | loop fusion | flops 65536 | bytes 786436 | tf_op jit(solution)/shard_map/add | solution.py:160
  36.0 0.0 copy-start.2
  36.0 1.6 %copy-done.2 = bf16[512,2048]{1,0:T(8,128)(2,1)S(1)} copy-done((bf16[512,2048]{1,0:T(8,128)(2,1)S(1)}, bf16[512,2048]{1,0:T(8,128)(2,1)}, u32[]{:S(2)}) %copy-start.2) | copy-done | bytes 2097176
  37.6 2.9 %shard_map.76.kept_ref = f32[4,32,2048]{2,1,0:T(8,128)S(1)} custom-call(s32[1]{0:T(128)} %bitcast.which_ref, bf16[4,2,32,1024]{3,2,1,0:T(8,128)(2,1)S(1)} %bitcast.73, bf16[512,2048]{1,0:T(8,128)(2,1)S(1)} %copy-done.2, bf16[512,2048]{1,0:T(8,128)(2,1)} %collective-permute-done.sib_ref), custom_call_target="tpu_custom_call" | custom-call | flops 536870912 | bytes 4194304 | tf_op jit(solution)/shard_map/pallas_call | solution.py:25
  40.4 0.0 copy-start.7
  40.4 0.0 copy-start.6
  40.5 7.8 %collective-permute-done.1 = f16[4,32,2048]{2,1,0:T(8,128)(2,1)} collective-permute-done((f16[4,32,2048]{2,1,0:T(8,128)(2,1)}, f16[4,32,2048]{2,1,0:T(8,128)(2,1)}, u32[]{:S(2)}, u32[]{:S(2)}) %collective-permute-start.1) | collective-permute-done | bytes 524320 | tf_op jit(solution)/shard_map/ppermute | solution.py:16
  48.3 1.1 %convert_element_type.7.came_ref = f32[4,32,2048]{2,1,0:T(8,128)S(1)} convert(f16[4,32,2048]{2,1,0:T(8,128)(2,1)} %collective-permute-done.1) | non-fusion elementwise | flops 262144 | bytes 1572864 | tf_op jit(solution)/shard_map/convert_element_type | solution.py:177
  49.4 0.7 shard_map.78
  50.1 0.0 copy-start.3
  50.1 1.0 %copy-done.3 = f32[4,32,2048]{2,1,0:T(8,128)} copy-done((f32[4,32,2048]{2,1,0:T(8,128)}, f32[4,32,2048]{2,1,0:T(8,128)S(1)}, u32[]{:S(2)}) %copy-start.3) | copy-done | bytes 1048600
  51.0 1.3 %collective-permute-start.4 = (f32[2,32,128]{2,1,0:T(8,128)S(1)}, f32[2,32,128]{2,1,0:T(8,128)S(1)}, u32[]{:S(2)}, u32[]{:S(2)}) collective-permute-start(f32[2,32,128]{2,1,0:T(8,128)S(1)} %get-tuple-element.15), channel_id=1, source_target_pairs={{0,1},{1,0},{2,3},{3,2},{4,5},{5,4},{6,7},{7,6},{8,9},{9,8},{10,11... | collective-permute-start | bytes 98312 | tf_op jit(solution)/shard_map/ppermute | solution.py:16
  52.3 2.6 %collective-permute-done.4 = f32[2,32,128]{2,1,0:T(8,128)S(1)} collective-permute-done((f32[2,32,128]{2,1,0:T(8,128)S(1)}, f32[2,32,128]{2,1,0:T(8,128)S(1)}, u32[]{:S(2)}, u32[]{:S(2)}) %collective-permute-start.4) | collective-permute-done | bytes 32800 | tf_op jit(solution)/shard_map/ppermute | solution.py:16
  55.0 1.2 %collective-permute-start.5 = (f32[2,32,128]{2,1,0:T(8,128)S(1)}, f32[2,32,128]{2,1,0:T(8,128)S(1)}, u32[]{:S(2)}, u32[]{:S(2)}) collective-permute-start(f32[2,32,128]{2,1,0:T(8,128)S(1)} %pad_maximum_fusion.1), channel_id=1, source_target_pairs={{0,2},{1,3},{2,0},{3,1},{4,6},{5,7},{6,4},{7,5},{8,10},{9,11},{10,... | collective-permute-start | bytes 98312 | tf_op jit(solution)/shard_map/ppermute | solution.py:16
  56.2 0.1 copy.39
  56.4 2.6 %collective-permute-done.5 = f32[2,32,128]{2,1,0:T(8,128)S(1)} collective-permute-done((f32[2,32,128]{2,1,0:T(8,128)S(1)}, f32[2,32,128]{2,1,0:T(8,128)S(1)}, u32[]{:S(2)}, u32[]{:S(2)}) %collective-permute-start.5) | collective-permute-done | bytes 32800 | tf_op jit(solution)/shard_map/ppermute | solution.py:16
  59.0 0.1 collective-permute-start.6
  59.1 0.1 select_n.93
  59.3 0.1 sub.85.label_ref
  59.3 4.6 %collective-permute-done.6 = f32[2,32,128]{2,1,0:T(8,128)S(1)} collective-permute-done((f32[2,32,128]{2,1,0:T(8,128)S(1)}, f32[2,32,128]{2,1,0:T(8,128)S(1)}, u32[]{:S(2)}, u32[]{:S(2)}) %collective-permute-start.6) | collective-permute-done | bytes 32800 | tf_op jit(solution)/shard_map/ppermute | solution.py:16
  64.0 0.0 copy-start.4
  64.0 1.2 %copy-done.4 = f32[4,32,2048]{2,1,0:T(8,128)S(1)} copy-done((f32[4,32,2048]{2,1,0:T(8,128)S(1)}, f32[4,32,2048]{2,1,0:T(8,128)}, u32[]{:S(2)}) %copy-start.4) | copy-done | bytes 1048600
  65.2 1.1 %shard_map.79 = (f32[24,128]{1,0:T(8,128)S(1)}, bf16[32,2048]{1,0:T(8,128)(2,1)S(1)}) custom-call(f32[4,32,2048]{2,1,0:T(8,128)S(1)} %copy-done.4, f32[32,2048]{1,0:T(8,128)S(1)} %bitcast_add_fusion.1.student_ref, f32[2,32,128]{2,1,0:T(8,128)S(1)} %pad_maximum_fusion.3.stats_ref, s32[32,1]{1,0:T(8,128)S(1)} %sub.85.label_ref), custom_call_target="tpu_custom_call" | custom-call | tf_op jit(solution)/shard_map/pallas_call | solution.py:25
  66.3 0.1 collective-permute-start.8
  66.4 7.4 %all_gather.3.residual_ref = bf16[128,2048]{1,0:T(8,128)(2,1)S(1)} all-gather(bf16[32,2048]{1,0:T(8,128)(2,1)S(1)} %get-tuple-element.18), channel_id=1, replica_groups=mesh['teacher'=4,'vocab'=8] {'teacher'}, dimensions={0}, use_global_device_ids=true | all-gather | bytes 655360 | tf_op jit(solution)/shard_map/all_gather | solution.py:211
  73.8 2.9 %shard_map.80 = f32[512,2048]{1,0:T(8,128)} custom-call(bf16[512,128]{1,0:T(8,128)(2,1)S(1)} %bitcast.74, bf16[128,2048]{1,0:T(8,128)(2,1)S(1)} %all_gather.3.residual_ref), custom_call_target="tpu_custom_call" | custom-call | flops 268435456 | bytes 4194304 | tf_op jit(solution)/shard_map/pallas_call | solution.py:25
  76.7 0.1 copy.34
  76.8 0.1 copy.33
  76.9 0.1 pad_maximum_fusion.4
  77.0 0.7 copy.36
  77.7 0.1 copy.37
  77.8 0.7 slice.123
  (33 shorter events, 0.3 us)
Async XLA Ops:
  0.6 2.3 %copy-start = (bf16[512,2048]{1,0:T(8,128)(2,1)S(1)}, bf16[512,2048]{1,0:T(8,128)(2,1)}, u32[]{:S(2)}) copy-start(bf16[512,2048]{1,0:T(8,128)(2,1)} %param.8) | copy-start | bytes 6291460
  2.5 26.6 %collective-permute-start = (bf16[512,2048]{1,0:T(8,128)(2,1)}, bf16[512,2048]{1,0:T(8,128)(2,1)}, u32[]{:S(2)}, u32[]{:S(2)}) collective-permute-start(bf16[512,2048]{1,0:T(8,128)(2,1)} %own_ref.1), channel_id=1, source_target_pairs={{0,8},{8,0},{16,24},{24,16},{1,9},{9,1},{17,25},{25,17},{2,10},{10... | collective-permute-start | bytes 6291464 | tf_op jit(solution)/shard_map/ppermute | solution.py:16
  4.3 1.0 %copy-start.5 = (f32[2,2,32,2048]{3,2,1,0:T(8,128)}, f32[2,2,32,2048]{3,2,1,0:T(8,128)S(1)}, u32[]{:S(2)}) copy-start(f32[2,2,32,2048]{3,2,1,0:T(8,128)S(1)} %fusion) | copy-start | bytes 3145732
  5.3 7.5 %collective-permute-start.2 = (f32[2,32,2048]{2,1,0:T(8,128)S(1)}, f32[2,32,2048]{2,1,0:T(8,128)}, u32[]{:S(2)}, u32[]{:S(2)}) collective-permute-start(f32[2,32,2048]{2,1,0:T(8,128)S(1)} %dynamic-slice_bitcast_fusion), channel_id=1, source_target_pairs={{0,8},{8,0},{16,24},{24,16},{1,9},{9,1},{17,25},{25,17},{2,10},{10... | collective-permute-start | bytes 1572872 | tf_op jit(solution)/shard_map/ppermute | solution.py:16
  5.4 23.7 %all-to-all-start = ((bf16[32,8,1024]{2,1,0:T(8,128)(2,1)}), bf16[32,8,1024]{2,1,0:T(8,128)(2,1)S(1)}, u32[]{:S(2)}, u32[]{:S(2)}) async-start(bf16[32,8,1024]{2,1,0:T(8,128)(2,1)} %bitcast.18), calls=%async_computation | async-start | bytes 1048576 | tf_op jit(solution)/shard_map/all_to_all | solution.py:144
  14.1 20.9 %collective-permute-start.3 = (f32[32,2048]{1,0:T(8,128)S(1)}, f32[32,2048]{1,0:T(8,128)}, u32[]{:S(2)}, u32[]{:S(2)}) collective-permute-start(f32[32,2048]{1,0:T(8,128)S(1)} %dynamic-slice_bitcast_fusion.1), channel_id=1, source_target_pairs={{0,16},{8,24},{16,0},{24,8},{1,17},{9,25},{17,1},{25,9},{2,18},{10... | collective-permute-start | bytes 786440 | tf_op jit(solution)/shard_map/ppermute | solution.py:16
  29.1 1.6 %copy-start.1 = (bf16[512,2048]{1,0:T(8,128)(2,1)S(1)}, bf16[512,2048]{1,0:T(8,128)(2,1)}, u32[]{:S(2)}) copy-start(bf16[512,2048]{1,0:T(8,128)(2,1)} %own_ref.1) | copy-start | bytes 6291460
  34.4 13.8 %collective-permute-start.1 = (f16[4,32,2048]{2,1,0:T(8,128)(2,1)}, f16[4,32,2048]{2,1,0:T(8,128)(2,1)}, u32[]{:S(2)}, u32[]{:S(2)}) collective-permute-start(f16[4,32,2048]{2,1,0:T(8,128)(2,1)} %convert_element_type.6), channel_id=1, source_target_pairs={{0,16},{8,24},{16,0},{24,8},{1,17},{9,25},{17,1},{25,9},{2,18},{10... | collective-permute-start | bytes 1572872 | tf_op jit(solution)/shard_map/ppermute | solution.py:16
  36.0 1.6 %copy-start.2 = (bf16[512,2048]{1,0:T(8,128)(2,1)S(1)}, bf16[512,2048]{1,0:T(8,128)(2,1)}, u32[]{:S(2)}) copy-start(bf16[512,2048]{1,0:T(8,128)(2,1)} %own_ref.1) | copy-start | bytes 6291460
  40.4 15.8 %copy-start.7 = (s32[32]{0:T(128)S(1)}, s32[32]{0:T(128)}, u32[]{:S(2)}) copy-start(s32[32]{0:T(128)} %param.9) | copy-start | bytes 388
  40.4 15.8 %copy-start.6 = (bf16[128,512]{1,0:T(8,128)(2,1)S(1)}, bf16[128,512]{1,0:T(8,128)(2,1)}, u32[]{:S(2)}) copy-start(bf16[128,512]{1,0:T(8,128)(2,1)} %param.7) | copy-start | bytes 393220
  50.1 1.0 %copy-start.3 = (f32[4,32,2048]{2,1,0:T(8,128)}, f32[4,32,2048]{2,1,0:T(8,128)S(1)}, u32[]{:S(2)}) copy-start(f32[4,32,2048]{2,1,0:T(8,128)S(1)} %get-tuple-element.14.logits_ref) | copy-start | bytes 3145732
  51.0 3.9 %collective-permute-start.4 = (f32[2,32,128]{2,1,0:T(8,128)S(1)}, f32[2,32,128]{2,1,0:T(8,128)S(1)}, u32[]{:S(2)}, u32[]{:S(2)}) collective-permute-start(f32[2,32,128]{2,1,0:T(8,128)S(1)} %get-tuple-element.15), channel_id=1, source_target_pairs={{0,1},{1,0},{2,3},{3,2},{4,5},{5,4},{6,7},{7,6},{8,9},{9,8},{10,11... | collective-permute-start | bytes 98312 | tf_op jit(solution)/shard_map/ppermute | solution.py:16
  55.0 4.0 %collective-permute-start.5 = (f32[2,32,128]{2,1,0:T(8,128)S(1)}, f32[2,32,128]{2,1,0:T(8,128)S(1)}, u32[]{:S(2)}, u32[]{:S(2)}) collective-permute-start(f32[2,32,128]{2,1,0:T(8,128)S(1)} %pad_maximum_fusion.1), channel_id=1, source_target_pairs={{0,2},{1,3},{2,0},{3,1},{4,6},{5,7},{6,4},{7,5},{8,10},{9,11},{10,... | collective-permute-start | bytes 98312 | tf_op jit(solution)/shard_map/ppermute | solution.py:16
  56.2 2.9 %collective-permute-start.7 = (s32[32]{0:T(128)S(1)}, s32[32]{0:T(128)S(1)}, u32[]{:S(2)}, u32[]{:S(2)}) collective-permute-start(s32[32]{0:T(128)S(1)} %copy-done.7), channel_id=1, source_target_pairs={{0,8},{8,0},{16,24},{24,16},{1,9},{9,1},{17,25},{25,17},{2,10},{10... | collective-permute-start | bytes 392 | tf_op jit(solution)/shard_map/ppermute | solution.py:16
  59.0 4.9 %collective-permute-start.6 = (f32[2,32,128]{2,1,0:T(8,128)S(1)}, f32[2,32,128]{2,1,0:T(8,128)S(1)}, u32[]{:S(2)}, u32[]{:S(2)}) collective-permute-start(f32[2,32,128]{2,1,0:T(8,128)S(1)} %pad_maximum_fusion.2), channel_id=1, source_target_pairs={{0,4},{1,5},{2,6},{3,7},{4,0},{5,1},{6,2},{7,3},{8,12},{9,13},{10,... | collective-permute-start | bytes 98312 | tf_op jit(solution)/shard_map/ppermute | solution.py:16
  64.0 1.2 %copy-start.4 = (f32[4,32,2048]{2,1,0:T(8,128)S(1)}, f32[4,32,2048]{2,1,0:T(8,128)}, u32[]{:S(2)}) copy-start(f32[4,32,2048]{2,1,0:T(8,128)} %copy-done.3) | copy-start | bytes 3145732
  66.3 10.4 %collective-permute-start.8 = (f32[24,32]{1,0:T(8,128)S(1)}, f32[24,32]{1,0:T(8,128)S(1)}, u32[]{:S(2)}, u32[]{:S(2)}) collective-permute-start(f32[24,32]{1,0:T(8,128)S(1)} %bitcast.75), channel_id=1, source_target_pairs={{0,8},{8,0},{16,24},{24,16},{1,9},{9,1},{17,25},{25,17},{2,10},{10... | collective-permute-start | bytes 9224 | tf_op jit(solution)/shard_map/ppermute | solution.py:16

commit v3 on v2

v3 whole, which is shorter than its diff:
```python
import functools

import jax
import jax.numpy as jnp
from jax import lax
from jax.experimental import pallas as pl
from jax.experimental.pallas import tpu as pltpu
from jax.sharding import PartitionSpec as P

HARD_SHARE = 0.3
LANES = 128


def swap(value, axis, mask):
    count = lax.axis_size(axis)
    return lax.ppermute(value, axis, [(i, i ^ mask) for i in range(count)])


def call(body, outs, args, grid=None, in_specs=None, out_specs=None, scratch=(), flops=0, moved=0, limit=16):
    extra = {} if grid is None else {"grid": grid}
    if in_specs is not None:
        extra["in_specs"] = in_specs
    if out_specs is not None:
        extra["out_specs"] = out_specs
    return pl.pallas_call(
        body,
        out_shape=outs,
        scratch_shapes=list(scratch),
        compiler_params=pltpu.CompilerParams(vmem_limit_bytes=limit * 1024 * 1024),
        cost_estimate=pl.CostEstimate(flops=flops, bytes_accessed=moved, transcendentals=0),
        **extra,
    )(*args)


VMEM = pl.BlockSpec(memory_space=pltpu.VMEM)


def split_body(hidden_ref, keep_ref, give_ref):
    piece = keep_ref.shape[0]
    core = lax.axis_index("teacher") % 2
    value = hidden_ref[...].astype(jnp.float32)
    low, high = value[:piece], value[piece:]
    keep_ref[...] = jnp.where(core == 0, low, high).astype(keep_ref.dtype)
    give_ref[...] = jnp.where(core == 0, high, low).astype(give_ref.dtype)


def halve_body(own_ref, sib_ref, keep_ref, give_ref):
    depth = keep_ref.shape[2]
    half = depth // 2
    x = lax.axis_index("teacher") // 2
    core = lax.axis_index("teacher") % 2
    own = own_ref[...].astype(jnp.float32)
    sib = sib_ref[...].astype(jnp.float32)
    for at, value in enumerate((jnp.where(core == 0, own, sib), jnp.where(core == 0, sib, own))):
        low, high = value[:, :depth], value[:, depth:]
        for ref, part in ((keep_ref, jnp.where(x == 0, low, high)), (give_ref, jnp.where(x == 0, high, low))):
            lead, trail = part[:, :half], part[:, half:]
            ref[at, :, :half] = jnp.where(core == 0, lead, trail).astype(ref.dtype)
            ref[at, :, half:] = jnp.where(core == 0, trail, lead).astype(ref.dtype)


def order_body(own_ref, far_ref, out_ref):
    x = lax.axis_index("teacher") // 2
    count = own_ref.shape[0]
    for i in range(count):
        out_ref[x * count + i] = own_ref[i]
        out_ref[(1 - x) * count + i] = far_ref[i]


def assemble_body(*refs):
    pieces, (away_ref, stay_ref, buf) = refs[:-3], refs[-3:]
    teachers, near = away_ref.shape[:2]
    x = lax.axis_index("teacher") // 2
    level = lax.axis_index("vocab") // 2
    for mask, piece_ref in enumerate(pieces):
        buf[level ^ mask] = piece_ref[...]
    for i in range(teachers):
        for j in range(near):
            away_ref[i, j] = buf[(1 - x) * near + j, i]
            stay_ref[i, j] = buf[x * near + j, i]


def partial_body(*refs):
    count = (len(refs) - 2) // 2
    hidden_refs, (own_ref, sib_ref), out_refs = refs[:count], refs[count : count + 2], refs[count + 2 :]
    half, width = own_ref.shape
    step = min(width, 512)
    rows = [ref[...] for ref in hidden_refs]
    rows = rows[0] if count == 1 else jnp.concatenate(rows, axis=0)
    for at in range(0, width, step):
        value = jnp.dot(rows[:, :half], own_ref[:, at : at + step], preferred_element_type=jnp.float32)
        value += jnp.dot(rows[:, half:], sib_ref[:, at : at + step], preferred_element_type=jnp.float32)
        value = value.reshape(count, *out_refs[0].shape[:2], step)
        for which, out_ref in enumerate(out_refs):
            out_ref[:, :, at : at + step] = value[which]


def student_body(hidden_ref, head_ref, keep_ref, give_ref, turned_ref):
    core = lax.axis_index("teacher") % 2
    chips, block, _ = keep_ref.shape
    value = jnp.dot(hidden_ref[...], head_ref[...], preferred_element_type=jnp.float32)
    near = 2
    piece = block // near // 2
    tall = hidden_ref[...].astype(jnp.float32)

    def place(x, level, side, c):
        return (((x * near + level) * 2 + side) * 2 + c) * piece

    for x in range(chips):
        for side in range(2):
            for level in range(near):
                low = value[place(x, level, side, 0) :][:piece]
                high = value[place(x, level, side, 1) :][:piece]
                to = (side * near + level) * piece
                keep_ref[x, to : to + piece] = jnp.where(core == 0, low, high)
                give_ref[x, to : to + piece] = jnp.where(core == 0, high, low)

    @pl.when(pl.program_id(0) == 0)
    def _():
        ordered = [
            tall[place(x, level, side, c) :][:piece]
            for x in range(chips)
            for c in range(2)
            for side in range(2)
            for level in range(near)
        ]
        turned_ref[...] = jnp.concatenate(ordered, axis=0).T.astype(turned_ref.dtype)


def sum_body(own_ref, sib_ref, keep_ref, give_ref):
    x = lax.axis_index("teacher") // 2
    keep_ref[...] = own_ref[x] + sib_ref[x]
    give_ref[...] = own_ref[1 - x] + sib_ref[1 - x]


def stats_body(part, logits_ref, student_ref, stats_ref):
    side = lax.axis_index("vocab") % 2
    teachers, rows, _ = logits_ref.shape
    lane = lax.broadcasted_iota(jnp.int32, (rows, LANES), 1)
    lse = jnp.zeros((rows, LANES), jnp.float32)
    mean = jnp.zeros((rows, LANES), jnp.float32)
    tops = [jnp.max(logits_ref[i], axis=1, keepdims=True) for i in range(teachers)]
    for i in range(teachers):
        weight = jnp.exp(logits_ref[i] - tops[i])
        total = jnp.sum(weight, axis=1, keepdims=True)
        group = (lane >= i * teachers) & (lane < (i + 1) * teachers)
        lse = jnp.where(group, tops[i] + jnp.log(total), lse)
        for j in range(teachers):
            local = jnp.sum(weight * (logits_ref[j] - tops[j]), axis=1, keepdims=True) / total + tops[j]
            mean = jnp.where(lane == i * teachers + j, local, mean)
    place = side if part == 0 else 1 - side
    value = student_ref[pl.ds(pl.multiple_of(place * rows, rows), rows)]
    top = jnp.max(value, axis=1, keepdims=True)
    total = jnp.sum(jnp.exp(value - top), axis=1, keepdims=True)
    stats_ref[0] = jnp.where(lane == teachers * teachers, top + jnp.log(total), lse)
    stats_ref[1] = mean


def merge(one, two):
    high = jnp.maximum(one[0], two[0])
    low = jnp.minimum(one[0], two[0])
    both = high + jnp.log1p(jnp.exp(low - high))
    return jnp.stack([both, jnp.exp(one[0] - both) * one[1] + jnp.exp(two[0] - both) * two[1]])


def residual_body(
    own_ref, other_ref, student_ref, stats_ref, label_ref, sib_label_ref, small_ref, residual_ref, weight_ref
):
    side = lax.axis_index("vocab") % 2
    core = lax.axis_index("teacher") % 2
    teachers, group, width = own_ref.shape
    rows = 2 * group
    lane = lax.broadcasted_iota(jnp.int32, (rows, LANES), 1)
    lse, mean = stats_ref[0], stats_ref[1]
    small = jnp.zeros((rows, LANES), jnp.float32)
    inverse = []
    for j in range(teachers):
        norm = lse[:, j * teachers : j * teachers + 1]
        spread = jnp.zeros((rows, 1), jnp.float32)
        for i in range(teachers):
            at = i * teachers + j
            entry = norm - mean[:, at : at + 1]
            small = jnp.where(lane == at, entry, small)
            spread = spread + entry
        inverse.append(1.0 / (1.0 + spread * (1.0 / teachers)))
    total = inverse[0]
    for i in range(1, teachers):
        total = total + inverse[i]
    at = teachers * teachers
    for i in range(teachers):
        small = jnp.where(lane == at + i, inverse[i] / total * teachers, small)
    weight_ref[...] = small
    square = jnp.concatenate([small, jnp.zeros((LANES - rows, LANES), jnp.float32)], axis=0)
    small_ref[...] = square.T[: small_ref.shape[0]]
    piece = rows // 4
    token = lax.broadcasted_iota(jnp.int32, (rows, rows), 0)
    source = lax.broadcasted_iota(jnp.int32, (rows, rows), 1)
    hit = source == token // (2 * piece) * (2 * piece) + core * piece + token % piece
    mine = token // piece % 2 == core
    label = jnp.where(hit, jnp.where(mine, label_ref[...], sib_label_ref[...]), 0)
    label = jnp.sum(label, axis=1, keepdims=True) - lax.axis_index("vocab") * width
    label_at = lambda place: jnp.where(place == 0, label[:group], label[group:])
    for part, logits_ref in enumerate((own_ref, other_ref)):
        place = side if part == 0 else 1 - side
        span = pl.ds(pl.multiple_of(place * group, group), group)
        norms = stats_ref[0, span]
        weights = weight_ref[span]
        target = jnp.where(
            lax.broadcasted_iota(jnp.int32, (group, width), 1) == label_at(place), HARD_SHARE, 0.0
        )
        for i in range(teachers):
            norm = norms[:, i * teachers : i * teachers + 1]
            log_prob = (logits_ref[i] - norm).astype(jnp.bfloat16).astype(jnp.float32)
            prob = jnp.exp(log_prob).astype(jnp.bfloat16).astype(jnp.float32)
            target = target + ((1.0 - HARD_SHARE) / teachers * weights[:, at + i : at + i + 1]) * prob
        prob = jnp.exp(student_ref[span] - norms[:, at : at + 1])
        residual_ref[span] = (prob - target).astype(jnp.bfloat16)


def grad_body(hidden_ref, residual_ref, small_ref, sib_ref, grad_ref, cross_ref, agree_ref):
    core = lax.axis_index("teacher") % 2
    grad_ref[...] = jnp.dot(hidden_ref[...], residual_ref[...], preferred_element_type=jnp.float32)

    @pl.when(pl.program_id(0) == 0)
    def _():
        block = cross_ref.shape[1]
        piece = block // 4
        source = lax.broadcasted_iota(jnp.int32, (LANES, block), 0)
        token = lax.broadcasted_iota(jnp.int32, (LANES, block), 1)
        hit = source == token // (2 * piece) * (2 * piece) + core * piece + token % piece
        mine = token // piece % 2 == core
        placed = sum(
            jnp.dot(
                ref[...],
                jnp.where(hit & which, 1.0, 0.0),
                preferred_element_type=jnp.float32,
                precision=lax.Precision.HIGHEST,
            )
            for ref, which in ((small_ref, mine), (sib_ref, jnp.logical_not(mine)))
        )
        count = cross_ref.shape[0]
        cross_ref[...] = placed[:count]
        agree_ref[...] = placed[count : count + agree_ref.shape[0]]


def fast(teacher_hidden, teacher_head, student_hidden, student_head, labels):
    teachers = lax.axis_size("teacher")
    shards = lax.axis_size("vocab")
    chips = teachers // 2
    rows, width = teacher_head.shape
    tokens = student_hidden.shape[0]
    near = shards // 2 // chips
    piece = tokens // shards // 2
    block = tokens // teachers
    group = block // 2
    f32 = jnp.float32
    kind = teacher_hidden.dtype
    shape = jax.ShapeDtypeStruct

    def local(body, outs, args, **extra):
        return call(body, outs, args, in_specs=[VMEM] * len(args), out_specs=(VMEM,) * len(outs), **extra)

    keep, give = local(split_body, (shape((piece, teachers * rows), kind),) * 2, (teacher_hidden[0],))
    sib = swap(give, "teacher", 1)
    teacher_head, labels, keep = lax.optimization_barrier((teacher_head, labels, keep))
    sib_head = swap(teacher_head, "teacher", 1)
    sib_labels = swap(labels, "teacher", 1)
    keep, give = local(halve_body, (shape((2, piece, 2 * rows), kind),) * 2, (keep, sib))
    student_hidden, student_head, keep = lax.optimization_barrier((student_hidden, student_head, keep))
    (part,) = local(
        order_body, (shape((teachers, piece, 2 * rows), kind),), (keep, swap(give, "teacher", 2))
    )
    parts = [part] + [swap(part, "vocab", 2 * mask) for mask in range(1, shards // 2)]
    away, stay = local(
        assemble_body,
        (shape((teachers, near, piece, 2 * rows), kind),) * 2,
        parts,
        scratch=[pltpu.VMEM((shards // 2, teachers, piece, 2 * rows), kind)],
    )
    away = away.reshape(teachers * group, 2 * rows)
    stay = stay.reshape(teachers * group, 2 * rows)

    step = min(width, 512)
    whole = lambda i: (0, 0)
    keep, give, turned = call(
        student_body,
        (shape((chips, block, width), f32),) * 2 + (shape((rows, tokens), student_hidden.dtype),),
        (student_hidden, student_head),
        grid=(width // step,),
        in_specs=[pl.BlockSpec((tokens, rows), whole), pl.BlockSpec((rows, step), lambda i: (0, i))],
        out_specs=(pl.BlockSpec((chips, block, step), lambda i: (0, 0, i)),) * 2
        + (pl.BlockSpec((rows, tokens), whole),),
        flops=2 * tokens * rows * width,
        moved=2 * rows * width,
    )
    keep, give = local(sum_body, (shape((block, width), f32),) * 2, (keep, swap(give, "teacher", 1)))
    student = keep + swap(give, "teacher", 2)

    flat = shape((teachers, group, width), f32)

    def partial(*hidden):
        return local(
            partial_body,
            (flat,) * len(hidden),
            (*hidden, teacher_head, sib_head),
            flops=2 * len(hidden) * teachers * group * 2 * rows * width,
            moved=4 * rows * width,
        )

    other_away = swap(away, "vocab", 1)
    other_stay = swap(stay, "vocab", 1)
    sent, kept = partial(away, stay)
    far = swap(sent.astype(jnp.float16), "teacher", 2)
    (other_sent,) = partial(other_away)
    other_far = swap(other_sent.astype(jnp.float16), "teacher", 2)
    (other_kept,) = partial(other_stay)

    logits = [kept + far.astype(f32), other_kept + other_far.astype(f32)]
    stats = [
        local(functools.partial(stats_body, at), (shape((2, group, LANES), f32),), (logits[at], student))[0]
        for at in range(2)
    ]
    side = lax.axis_index("vocab") % 2
    stats = jnp.where(side == 0, jnp.concatenate(stats, axis=1), jnp.concatenate(stats[::-1], axis=1))
    mask = 1
    while mask < shards:
        stats = merge(stats, swap(stats, "vocab", mask))
        mask *= 2

    entries = teachers * teachers + teachers
    small, residual = local(
        residual_body,
        (shape((-(-entries // 8) * 8, LANES), f32), shape((block, width), jnp.bfloat16)),
        (*logits, student, stats, labels.reshape(1, block), sib_labels.reshape(1, block)),
        scratch=[pltpu.VMEM((block, LANES), f32)],
    )
    sib_small = swap(small, "teacher", 1)
    gathered = lax.all_gather(residual, "teacher", axis=0, tiled=True)
    grad, cross, agree = call(
        grad_body,
        (
            shape((rows, width), f32),
            shape((teachers * teachers, block), f32),
            shape((teachers, block), f32),
        ),
        (turned, gathered, small, sib_small),
        grid=(width // step,),
        in_specs=[
            pl.BlockSpec((rows, tokens), whole),
            pl.BlockSpec((tokens, step), lambda i: (0, i)),
            pl.BlockSpec(small.shape, whole),
            pl.BlockSpec(small.shape, whole),
        ],
        out_specs=(
            pl.BlockSpec((rows, step), lambda i: (0, i)),
            pl.BlockSpec((teachers * teachers, block), whole),
            pl.BlockSpec((teachers, block), whole),
        ),
        flops=2 * rows * tokens * width,
        moved=4 * rows * width,
    )
    return cross.T.reshape(block, teachers, teachers), agree.T, grad


def normalizer(logits):
    highest = lax.pmax(jnp.max(logits, axis=1), "vocab")
    summed = lax.psum(jnp.sum(jnp.exp(logits - highest[:, None]), axis=1), "vocab")
    return highest + jnp.log(summed)


def general(teacher_hidden, teacher_head, student_hidden, student_head, labels):
    teachers = lax.axis_size("teacher")
    block_rows = student_hidden.shape[0] // teachers
    shard_width = teacher_head.shape[1]
    gathered = lax.all_gather(teacher_hidden, "vocab", axis=1, tiled=True)
    logits = jnp.dot(
        gathered[0],
        lax.all_gather(teacher_head, "teacher", axis=0, tiled=True),
        preferred_element_type=jnp.float32,
    )
    log_prob = (logits - normalizer(logits)[:, None]).astype(jnp.bfloat16)
    exchanged = lax.all_to_all(log_prob[None], "teacher", split_axis=1, concat_axis=0, tiled=True)
    teacher_prob = jnp.exp(exchanged.astype(jnp.float32)).astype(jnp.bfloat16)
    cross_local = -jnp.einsum("itv,jtv->tij", teacher_prob, exchanged, preferred_element_type=jnp.float32)
    cross_matrix = lax.psum(cross_local, "vocab")
    inverse = 1.0 / (1.0 + jnp.mean(cross_matrix, axis=1))
    weights = inverse / jnp.sum(inverse, axis=1, keepdims=True)
    soft_mix = jnp.sum(weights.T[:, :, None] * teacher_prob.astype(jnp.float32), axis=0)
    col_offset = lax.axis_index("vocab") * shard_width
    columns = lax.broadcasted_iota(jnp.int32, (block_rows, shard_width), 1) + col_offset
    onehot = (columns == labels[:, None]).astype(jnp.float32)
    target = (1.0 - HARD_SHARE) * soft_mix + HARD_SHARE * onehot
    student_logits = lax.psum_scatter(
        jnp.dot(student_hidden, student_head, preferred_element_type=jnp.float32),
        "teacher",
        scatter_dimension=0,
        tiled=True,
    )
    student_prob = jnp.exp(student_logits - normalizer(student_logits)[:, None])
    residual = (student_prob - target).astype(jnp.bfloat16)
    student_grad = lax.dot_general(
        student_hidden,
        lax.all_gather(residual, "teacher", axis=0, tiled=True),
        (((0,), (0,)), ((), ())),
        preferred_element_type=jnp.float32,
    )
    return (cross_matrix, weights * teachers, student_grad)


def solution(mesh):
    body = fast if mesh.shape["teacher"] == 4 and mesh.shape["vocab"] == 8 else general
    return jax.shard_map(
        body,
        mesh=mesh,
        in_specs=(
            P("teacher", "vocab", None),
            P("teacher", "vocab"),
            P(None, "teacher"),
            P("teacher", "vocab"),
            P("teacher"),
        ),
        out_specs=(P("teacher", None, None), P("teacher", None), P("teacher", "vocab")),
        check_vma=False,
    )
```

time: 78.9 us -> 69.6 us (0.88)
  starting transfers between devices: 12.9 us -> 19.9 us
  waiting for transfers between devices: 30.8 us -> 24.5 us
  local copies, waits for them, and re-layouts: 10.1 us -> 5.55 us
  other arithmetic: 4.48 us -> 2.25 us
  Pallas kernels: 10.4 us -> 8.81 us
  matrix products: 1.35 us -> 0 us
    ppermute x9 -> x17, starting transfers between devices: 5.57 us -> 19.9 us  [swap(): return lax.ppermute(value, axis, [(i, i ^ mask) for i in range(count)])]
    all_to_all x1 -> x0, waiting for transfers between devices: 13.2 us -> none  [fast(): came = lax.all_to_all(spread, ('teacher', 'vocab'), 0, 0, tiled=True)]
    all_to_all x1 -> x0, starting transfers between devices: 7.3 us -> none  [fast(): came = lax.all_to_all(spread, ('teacher', 'vocab'), 0, 0, tiled=True)]
    ppermute x9 -> x17, waiting for transfers between devices: 17.7 us -> 24.5 us  [swap(): return lax.ppermute(value, axis, [(i, i ^ mask) for i in range(count)])]
    convert_element_type x2, other arithmetic: 1.97 us -> 0.06 us  [the longest x1 0.03 us: fast(): far = swap(sent.astype(jnp.float16), 'teacher', 2)]
    pallas_call x5 -> x13, Pallas kernels: 10.4 us -> 8.81 us  [call(): pl.pallas_call(body, out_shape=outs, scratch_shapes=list(scratch), compil...]
    dot_general x1 -> x0, matrix products: 1.35 us -> none  [fast(): jnp.dot(ordered, student_head, preferred_element_type=f32)]
    squeeze x5 -> x0, local copies, waits for them, and re-layouts: 0.99 us -> none  [the longest x1 0.92 us: fast(): half = mine[to % 2, :, to // 2]]
  transfers between devices with their start and end apart: 10 -> 17, of which waited for: 5 -> 10; matrix products, arithmetic and copies ran while one was open for 6% -> 3% of each run, Pallas kernels for 11% -> 6%
where the time goes in v3:
time: 69.6 us; the launch traced here: 69.3 us
  waiting for transfers between devices  24.5 us (35%)
  starting transfers between devices  19.9 us (29%)
  Pallas kernels  8.81 us (13%)
  blocking collectives  7.43 us (11%)
  local copies, waits for them, and re-layouts  5.55 us (8%)
  other arithmetic  2.25 us (3%)
  between operations  0.85 us (1%)
    ppermute x17, waiting for transfers between devices, swap(): return lax.ppermute(value, axis, [(i, i ^ mask) for i in range(count)])  24.5 us
    ppermute x17, starting transfers between devices, swap(): return lax.ppermute(value, axis, [(i, i ^ mask) for i in range(count)])  19.9 us
    pallas_call x13, Pallas kernels, call(): pl.pallas_call(body, out_shape=outs, scratch_shapes=list(scratch), compil...  8.81 us
    all_gather x1, blocking collectives, fast(): gathered = lax.all_gather(residual, 'teacher', axis=0, tiled=True)  7.43 us
    unnamed x14, local copies, waits for them, and re-layouts  5.55 us
  transfers between devices with their start and end apart: 17, of which 10 were waited for; matrix products, arithmetic and copies ran while one was open for 3% of the time, Pallas kernels for 6%

profile of v3, /device:TPU:0, one launch (start us, length us, event | category | flops | bytes accessed | tf_op | source)
XLA Modules:
  0.0 69.3 jit_solution(6576272163376727780)
XLA Ops:
  0.6 0.0 copy-start
  0.7 1.0 %copy-done.5 = bf16[1,16,2048]{2,1,0:T(8,128)(2,1)S(1)} copy-done((bf16[1,16,2048]{2,1,0:T(8,128)(2,1)S(1)}, bf16[1,16,2048]{2,1,0:T(8,128)(2,1)}, u32[]{:S(2)}) %copy-start.5) | copy-done | bytes 65560
  1.6 0.5 collective-permute-start.5
  2.2 0.1 collective-permute-start
  2.2 3.7 %collective-permute-done.sib_ref = bf16[8,2048]{1,0:T(8,128)(2,1)S(1)} collective-permute-done((bf16[8,2048]{1,0:T(8,128)(2,1)S(1)}, bf16[8,2048]{1,0:T(8,128)(2,1)S(1)}, u32[]{:S(2)}, u32[]{:S(2)}) %collective-permute-start) | collective-permute-done | bytes 32800 | tf_op jit(solution)/shard_map/ppermute | solution.py:16
  5.9 0.0 copy-start.3
  6.0 1.6 %copy-done.3 = bf16[512,2048]{1,0:T(8,128)(2,1)S(1)} copy-done((bf16[512,2048]{1,0:T(8,128)(2,1)S(1)}, bf16[512,2048]{1,0:T(8,128)(2,1)}, u32[]{:S(2)}) %copy-start.3) | copy-done | bytes 2097176
  7.5 0.9 %copy-done.4 = bf16[128,512]{1,0:T(8,128)(2,1)S(1)} copy-done((bf16[128,512]{1,0:T(8,128)(2,1)S(1)}, bf16[128,512]{1,0:T(8,128)(2,1)}, u32[]{:S(2)}) %copy-start.4) | copy-done | bytes 131096
  8.4 1.3 %shard_map.78 = (f32[2,32,2048]{2,1,0:T(8,128)S(1)}, f32[2,32,2048]{2,1,0:T(8,128)S(1)}, bf16[512,128]{1,0:T(8,128)(2,1)S(1)}) custom-call(bf16[128,512]{1,0:T(8,128)(2,1)S(1)} %copy-done.4, bf16[512,2048]{1,0:T(8,128)(2,1)S(1)} %copy-done.3), custom_call_target="tpu_custom_call" | custom-call | flops 268435456 | bytes 2097152 | tf_op jit(solution)/shard_map/pallas_call | solution.py:25
  9.8 0.2 collective-permute-start.10
  10.0 2.8 %collective-permute-start.1 = (bf16[2,8,1024]{2,1,0:T(8,128)(2,1)S(1)}, bf16[2,8,1024]{2,1,0:T(8,128)(2,1)S(1)}, u32[]{:S(2)}, u32[]{:S(2)}) collective-permute-start(bf16[2,8,1024]{2,1,0:T(8,128)(2,1)S(1)} %get-tuple-element.35), channel_id=1, source_target_pairs={{0,16},{8,24},{16,0},{24,8},{1,17},{9,25},{17,1},{25,9},{2,18},{10... | collective-permute-start | bytes 98312 | tf_op jit(solution)/shard_map/ppermute | solution.py:16
  12.8 1.9 %collective-permute-done.1.far_ref = bf16[2,8,1024]{2,1,0:T(8,128)(2,1)S(1)} collective-permute-done((bf16[2,8,1024]{2,1,0:T(8,128)(2,1)S(1)}, bf16[2,8,1024]{2,1,0:T(8,128)(2,1)S(1)}, u32[]{:S(2)}, u32[]{:S(2)}) %collective-permute-start.1) | collective-permute-done | bytes 32800 | tf_op jit(solution)/shard_map/ppermute | solution.py:16
  14.7 4.2 %collective-permute-start.4 = (bf16[4,8,1024]{2,1,0:T(8,128)(2,1)S(1)}, bf16[4,8,1024]{2,1,0:T(8,128)(2,1)S(1)}, u32[]{:S(2)}, u32[]{:S(2)}) collective-permute-start(bf16[4,8,1024]{2,1,0:T(8,128)(2,1)S(1)} %shard_map.79.refs_0_), channel_id=1, source_target_pairs={{0,6},{1,7},{2,4},{3,5},{4,2},{5,3},{6,0},{7,1},{8,14},{9,15},{10,... | collective-permute-start | bytes 196616 | tf_op jit(solution)/shard_map/ppermute | solution.py:16
  18.9 0.6 collective-permute-start.2
  19.6 2.1 %collective-permute-done.4.refs_3_ = bf16[4,8,1024]{2,1,0:T(8,128)(2,1)S(1)} collective-permute-done((bf16[4,8,1024]{2,1,0:T(8,128)(2,1)S(1)}, bf16[4,8,1024]{2,1,0:T(8,128)(2,1)S(1)}, u32[]{:S(2)}, u32[]{:S(2)}) %collective-permute-start.4) | collective-permute-done | bytes 65568 | tf_op jit(solution)/shard_map/ppermute | solution.py:16
  21.6 2.7 %collective-permute-done.3.refs_2_ = bf16[4,8,1024]{2,1,0:T(8,128)(2,1)S(1)} collective-permute-done((bf16[4,8,1024]{2,1,0:T(8,128)(2,1)S(1)}, bf16[4,8,1024]{2,1,0:T(8,128)(2,1)S(1)}, u32[]{:S(2)}, u32[]{:S(2)}) %collective-permute-start.3) | collective-permute-done | bytes 65568 | tf_op jit(solution)/shard_map/ppermute | solution.py:16
  24.3 0.1 shard_map.80
  24.3 1.6 %collective-permute-start.8 = (bf16[64,1024]{1,0:T(8,128)(2,1)S(1)}, bf16[64,1024]{1,0:T(8,128)(2,1)S(1)}, u32[]{:S(2)}, u32[]{:S(2)}) collective-permute-start(bf16[64,1024]{1,0:T(8,128)(2,1)S(1)} %bitcast.11), channel_id=1, source_target_pairs={{0,1},{1,0},{2,3},{3,2},{4,5},{5,4},{6,7},{7,6},{8,9},{9,8},{10,11... | collective-permute-start | bytes 393224 | tf_op jit(solution)/shard_map/ppermute | solution.py:16
  25.9 0.1 shard_map.84
  26.0 1.6 %collective-permute-start.11 = (f32[32,2048]{1,0:T(8,128)S(1)}, f32[32,2048]{1,0:T(8,128)}, u32[]{:S(2)}, u32[]{:S(2)}) collective-permute-start(f32[32,2048]{1,0:T(8,128)S(1)} %get-tuple-element.44), channel_id=1, source_target_pairs={{0,16},{8,24},{16,0},{24,8},{1,17},{9,25},{17,1},{25,9},{2,18},{10... | collective-permute-start | bytes 786440 | tf_op jit(solution)/shard_map/ppermute | solution.py:16
  27.5 1.8 %collective-permute-done.8.refs_0_ = bf16[64,1024]{1,0:T(8,128)(2,1)S(1)} collective-permute-done((bf16[64,1024]{1,0:T(8,128)(2,1)S(1)}, bf16[64,1024]{1,0:T(8,128)(2,1)S(1)}, u32[]{:S(2)}, u32[]{:S(2)}) %collective-permute-start.8) | collective-permute-done | bytes 131104 | tf_op jit(solution)/shard_map/ppermute | solution.py:16
  29.4 0.8 %shard_map.83 = f32[4,16,2048]{2,1,0:T(8,128)S(1)} custom-call(bf16[64,1024]{1,0:T(8,128)(2,1)S(1)} %collective-permute-done.8.refs_0_, bf16[512,2048]{1,0:T(8,128)(2,1)S(1)} %copy-done, bf16[512,2048]{1,0:T(8,128)(2,1)S(1)} %collective-permute-done.5.refs_3_.refs_2_), custom_call_target="tpu_custom_call" | custom-call | flops 268435456 | bytes 4194304 | tf_op jit(solution)/shard_map/pallas_call | solution.py:25
  30.2 0.5 copy-done.1
  30.7 1.6 %collective-permute-start.9 = (f16[4,16,2048]{2,1,0:T(8,128)(2,1)S(1)}, f16[4,16,2048]{2,1,0:T(8,128)(2,1)}, u32[]{:S(2)}, u32[]{:S(2)}) collective-permute-start(f16[4,16,2048]{2,1,0:T(8,128)(2,1)S(1)} %convert_element_type.14), channel_id=1, source_target_pairs={{0,16},{8,24},{16,0},{24,8},{1,17},{9,25},{17,1},{25,9},{2,18},{10... | collective-permute-start | bytes 786440 | tf_op jit(solution)/shard_map/ppermute | solution.py:16
  32.3 1.5 %collective-permute-start.7 = (bf16[64,1024]{1,0:T(8,128)(2,1)S(1)}, bf16[64,1024]{1,0:T(8,128)(2,1)S(1)}, u32[]{:S(2)}, u32[]{:S(2)}) collective-permute-start(bf16[64,1024]{1,0:T(8,128)(2,1)S(1)} %bitcast.9), channel_id=1, source_target_pairs={{0,1},{1,0},{2,3},{3,2},{4,5},{5,4},{6,7},{7,6},{8,9},{9,8},{10,11... | collective-permute-start | bytes 393224 | tf_op jit(solution)/shard_map/ppermute | solution.py:16
  33.8 0.5 collective-permute-done.11
  34.4 1.0 %add.51.student_ref = f32[32,2048]{1,0:T(8,128)S(1)} add(f32[32,2048]{1,0:T(8,128)S(1)} %get-tuple-element.43, f32[32,2048]{1,0:T(8,128)} %collective-permute-done.11) | non-fusion elementwise | flops 65536 | bytes 786432 | tf_op jit(solution)/shard_map/add | solution.py:297
  35.3 0.0 copy-start.2
  35.3 1.6 %copy-done.2 = bf16[512,2048]{1,0:T(8,128)(2,1)S(1)} copy-done((bf16[512,2048]{1,0:T(8,128)(2,1)S(1)}, bf16[512,2048]{1,0:T(8,128)(2,1)}, u32[]{:S(2)}) %copy-start.2) | copy-done | bytes 2097176
  36.9 0.7 %shard_map.81 = (f32[4,16,2048]{2,1,0:T(8,128)S(1)}, f32[4,16,2048]{2,1,0:T(8,128)S(1)}) custom-call(bf16[64,1024]{1,0:T(8,128)(2,1)S(1)} %bitcast.12, bf16[64,1024]{1,0:T(8,128)(2,1)S(1)} %bitcast.10, bf16[512,2048]{1,0:T(8,128)(2,1)S(1)} %copy-done, bf16[512,2048]{1,0:T(8,128)(2,1)S(1)} %copy-done.2), custom_call_target="tpu_custom_call" | custom-call | flops 536870912 | bytes 4194304 | tf_op jit(solution)/shard_map/pallas_call | solution.py:25
  37.7 1.6 %collective-permute-start.6 = (f16[4,16,2048]{2,1,0:T(8,128)(2,1)S(1)}, f16[4,16,2048]{2,1,0:T(8,128)(2,1)S(1)}, u32[]{:S(2)}, u32[]{:S(2)}) collective-permute-start(f16[4,16,2048]{2,1,0:T(8,128)(2,1)S(1)} %convert_element_type.12), channel_id=1, source_target_pairs={{0,16},{8,24},{16,0},{24,8},{1,17},{9,25},{17,1},{25,9},{2,18},{10... | collective-permute-start | bytes 786440 | tf_op jit(solution)/shard_map/ppermute | solution.py:16
  39.3 0.8 %shard_map.82 = f32[4,16,2048]{2,1,0:T(8,128)S(1)} custom-call(bf16[64,1024]{1,0:T(8,128)(2,1)S(1)} %collective-permute-done.7.refs_0_, bf16[512,2048]{1,0:T(8,128)(2,1)S(1)} %copy-done, bf16[512,2048]{1,0:T(8,128)(2,1)S(1)} %copy-done.2), custom_call_target="tpu_custom_call" | custom-call | flops 268435456 | bytes 4194304 | tf_op jit(solution)/shard_map/pallas_call | solution.py:25
  40.1 0.0 copy-start.6
  40.1 1.0 %convert_add_fusion.logits_ref.other_ref = f32[4,16,2048]{2,1,0:T(8,128)S(1)} fusion(f32[4,16,2048]{2,1,0:T(8,128)S(1)} %shard_map.82, f16[4,16,2048]{2,1,0:T(8,128)(2,1)} %collective-permute-done.9), kind=kLoop, calls=%fused_computation | loop fusion | flops 262144 | bytes 1310720 | tf_op jit(solution)/shard_map/add | solution.py:318
  41.2 0.4 shard_map.86
  41.6 2.6 %collective-permute-done.6 = f16[4,16,2048]{2,1,0:T(8,128)(2,1)S(1)} collective-permute-done((f16[4,16,2048]{2,1,0:T(8,128)(2,1)S(1)}, f16[4,16,2048]{2,1,0:T(8,128)(2,1)S(1)}, u32[]{:S(2)}, u32[]{:S(2)}) %collective-permute-start.6) | collective-permute-done | bytes 262176 | tf_op jit(solution)/shard_map/ppermute | solution.py:16
  44.1 0.1 convert_add_fusion.1.logits_ref.own_ref
  44.2 0.4 shard_map.85
  44.6 0.2 collective-permute-start.12
  44.9 3.7 %collective-permute-done.12 = f32[2,32,128]{2,1,0:T(8,128)S(1)} collective-permute-done((f32[2,32,128]{2,1,0:T(8,128)S(1)}, f32[2,32,128]{2,1,0:T(8,128)S(1)}, u32[]{:S(2)}, u32[]{:S(2)}) %collective-permute-start.12) | collective-permute-done | bytes 32800 | tf_op jit(solution)/shard_map/ppermute | solution.py:16
  48.6 0.9 %collective-permute-start.13 = (f32[2,32,128]{2,1,0:T(8,128)S(1)}, f32[2,32,128]{2,1,0:T(8,128)S(1)}, u32[]{:S(2)}, u32[]{:S(2)}) collective-permute-start(f32[2,32,128]{2,1,0:T(8,128)S(1)} %pad_maximum_fusion), channel_id=1, source_target_pairs={{0,2},{1,3},{2,0},{3,1},{4,6},{5,7},{6,4},{7,5},{8,10},{9,11},{10,... | collective-permute-start | bytes 98312 | tf_op jit(solution)/shard_map/ppermute | solution.py:16
  49.6 3.1 %collective-permute-done.13 = f32[2,32,128]{2,1,0:T(8,128)S(1)} collective-permute-done((f32[2,32,128]{2,1,0:T(8,128)S(1)}, f32[2,32,128]{2,1,0:T(8,128)S(1)}, u32[]{:S(2)}, u32[]{:S(2)}) %collective-permute-start.13) | collective-permute-done | bytes 32800 | tf_op jit(solution)/shard_map/ppermute | solution.py:16
  52.7 2.4 %collective-permute-start.14 = (f32[2,32,128]{2,1,0:T(8,128)S(1)}, f32[2,32,128]{2,1,0:T(8,128)S(1)}, u32[]{:S(2)}, u32[]{:S(2)}) collective-permute-start(f32[2,32,128]{2,1,0:T(8,128)S(1)} %pad_maximum_fusion.1), channel_id=1, source_target_pairs={{0,4},{1,5},{2,6},{3,7},{4,0},{5,1},{6,2},{7,3},{8,12},{9,13},{10,... | collective-permute-start | bytes 98312 | tf_op jit(solution)/shard_map/ppermute | solution.py:16
  55.1 2.5 %collective-permute-done.14 = f32[2,32,128]{2,1,0:T(8,128)S(1)} collective-permute-done((f32[2,32,128]{2,1,0:T(8,128)S(1)}, f32[2,32,128]{2,1,0:T(8,128)S(1)}, u32[]{:S(2)}, u32[]{:S(2)}) %collective-permute-start.14) | collective-permute-done | bytes 32800 | tf_op jit(solution)/shard_map/ppermute | solution.py:16
  57.6 1.0 %shard_map.87 = (f32[24,128]{1,0:T(8,128)S(1)}, bf16[32,2048]{1,0:T(8,128)(2,1)S(1)}) custom-call(f32[4,16,2048]{2,1,0:T(8,128)S(1)} %convert_add_fusion.1.logits_ref.own_ref, f32[4,16,2048]{2,1,0:T(8,128)S(1)} %convert_add_fusion.logits_ref.other_ref, f32[32,2048]{1,0:T(8,128)S(1)} %add.51.student_ref, f32[2,32,128]{2,1,0:T(8,128)S(1)} %pad_maximum_fusion.2.stats_ref, ...), custom_call_target="tpu_custom_call" | custom-call | tf_op jit(solution)/shard_map/pallas_call | solution.py:25
  58.6 0.1 collective-permute-start.16
  58.7 7.4 %all_gather.3.residual_ref = bf16[128,2048]{1,0:T(8,128)(2,1)S(1)} all-gather(bf16[32,2048]{1,0:T(8,128)(2,1)S(1)} %get-tuple-element.46), channel_id=1, replica_groups=mesh['teacher'=4,'vocab'=8] {'teacher'}, dimensions={0}, use_global_device_ids=true | all-gather | bytes 655360 | tf_op jit(solution)/shard_map/all_gather | solution.py:338
  66.2 3.1 %shard_map.88 = (f32[512,2048]{1,0:T(8,128)}, f32[16,32]{1,0:T(8,128)}, f32[4,32]{1,0:T(4,128)}) custom-call(bf16[512,128]{1,0:T(8,128)(2,1)S(1)} %get-tuple-element.33.hidden_ref, bf16[128,2048]{1,0:T(8,128)(2,1)S(1)} %all_gather.3.residual_ref, f32[24,128]{1,0:T(8,128)S(1)} %get-tuple-element.47.small_ref, f32[24,128]{1,0:T(8,128)S(1)} %collective-permute-done.16.sib_ref), custom_call_target="tpu_custom_call" | custom-call | flops 268435456 | bytes 4194304 | tf_op jit(solution)/shard_map/pallas_call | solution.py:25
  (26 shorter events, 0.2 us)
Async XLA Ops:
  0.6 28.7 %copy-start = (bf16[512,2048]{1,0:T(8,128)(2,1)S(1)}, bf16[512,2048]{1,0:T(8,128)(2,1)}, u32[]{:S(2)}) copy-start(bf16[512,2048]{1,0:T(8,128)(2,1)} %refs_1_.1) | copy-start | bytes 6291460
  0.6 1.0 %copy-start.5 = (bf16[1,16,2048]{2,1,0:T(8,128)(2,1)S(1)}, bf16[1,16,2048]{2,1,0:T(8,128)(2,1)}, u32[]{:S(2)}) copy-start(bf16[1,16,2048]{2,1,0:T(8,128)(2,1)} %param.5) | copy-start | bytes 196612
  1.6 27.7 %collective-permute-start.5 = (bf16[512,2048]{1,0:T(8,128)(2,1)}, bf16[512,2048]{1,0:T(8,128)(2,1)S(1)}, u32[]{:S(2)}, u32[]{:S(2)}) collective-permute-start(bf16[512,2048]{1,0:T(8,128)(2,1)} %refs_1_.1), channel_id=1, source_target_pairs={{0,8},{8,0},{16,24},{24,16},{1,9},{9,1},{17,25},{25,17},{2,10},{10... | collective-permute-start | bytes 6291464 | tf_op jit(solution)/shard_map/ppermute | solution.py:16
  2.2 3.8 %collective-permute-start = (bf16[8,2048]{1,0:T(8,128)(2,1)S(1)}, bf16[8,2048]{1,0:T(8,128)(2,1)S(1)}, u32[]{:S(2)}, u32[]{:S(2)}) collective-permute-start(bf16[8,2048]{1,0:T(8,128)(2,1)S(1)} %get-tuple-element.29), channel_id=1, source_target_pairs={{0,8},{8,0},{16,24},{24,16},{1,9},{9,1},{17,25},{25,17},{2,10},{10... | collective-permute-start | bytes 98312 | tf_op jit(solution)/shard_map/ppermute | solution.py:16
  5.9 1.6 %copy-start.3 = (bf16[512,2048]{1,0:T(8,128)(2,1)S(1)}, bf16[512,2048]{1,0:T(8,128)(2,1)}, u32[]{:S(2)}) copy-start(bf16[512,2048]{1,0:T(8,128)(2,1)} %head_ref) | copy-start | bytes 6291460
  7.5 0.9 %copy-start.4 = (bf16[128,512]{1,0:T(8,128)(2,1)S(1)}, bf16[128,512]{1,0:T(8,128)(2,1)}, u32[]{:S(2)}) copy-start(bf16[128,512]{1,0:T(8,128)(2,1)} %hidden_ref) | copy-start | bytes 393220
  9.8 16.1 %collective-permute-start.10 = (f32[2,32,2048]{2,1,0:T(8,128)S(1)}, f32[2,32,2048]{2,1,0:T(8,128)S(1)}, u32[]{:S(2)}, u32[]{:S(2)}) collective-permute-start(f32[2,32,2048]{2,1,0:T(8,128)S(1)} %get-tuple-element.42), channel_id=1, source_target_pairs={{0,8},{8,0},{16,24},{24,16},{1,9},{9,1},{17,25},{25,17},{2,10},{10... | collective-permute-start | bytes 1572872 | tf_op jit(solution)/shard_map/ppermute | solution.py:16
  10.0 4.7 %collective-permute-start.1 = (bf16[2,8,1024]{2,1,0:T(8,128)(2,1)S(1)}, bf16[2,8,1024]{2,1,0:T(8,128)(2,1)S(1)}, u32[]{:S(2)}, u32[]{:S(2)}) collective-permute-start(bf16[2,8,1024]{2,1,0:T(8,128)(2,1)S(1)} %get-tuple-element.35), channel_id=1, source_target_pairs={{0,16},{8,24},{16,0},{24,8},{1,17},{9,25},{17,1},{25,9},{2,18},{10... | collective-permute-start | bytes 98312 | tf_op jit(solution)/shard_map/ppermute | solution.py:16
  14.7 6.9 %collective-permute-start.4 = (bf16[4,8,1024]{2,1,0:T(8,128)(2,1)S(1)}, bf16[4,8,1024]{2,1,0:T(8,128)(2,1)S(1)}, u32[]{:S(2)}, u32[]{:S(2)}) collective-permute-start(bf16[4,8,1024]{2,1,0:T(8,128)(2,1)S(1)} %shard_map.79.refs_0_), channel_id=1, source_target_pairs={{0,6},{1,7},{2,4},{3,5},{4,2},{5,3},{6,0},{7,1},{8,14},{9,15},{10,... | collective-permute-start | bytes 196616 | tf_op jit(solution)/shard_map/ppermute | solution.py:16
  18.9 5.4 %collective-permute-start.3 = (bf16[4,8,1024]{2,1,0:T(8,128)(2,1)S(1)}, bf16[4,8,1024]{2,1,0:T(8,128)(2,1)S(1)}, u32[]{:S(2)}, u32[]{:S(2)}) collective-permute-start(bf16[4,8,1024]{2,1,0:T(8,128)(2,1)S(1)} %shard_map.79.refs_0_), channel_id=1, source_target_pairs={{0,4},{1,5},{2,6},{3,7},{4,0},{5,1},{6,2},{7,3},{8,12},{9,13},{10,... | collective-permute-start | bytes 196616 | tf_op jit(solution)/shard_map/ppermute | solution.py:16
  18.9 5.4 %collective-permute-start.2 = (bf16[4,8,1024]{2,1,0:T(8,128)(2,1)S(1)}, bf16[4,8,1024]{2,1,0:T(8,128)(2,1)S(1)}, u32[]{:S(2)}, u32[]{:S(2)}) collective-permute-start(bf16[4,8,1024]{2,1,0:T(8,128)(2,1)S(1)} %shard_map.79.refs_0_), channel_id=1, source_target_pairs={{0,2},{1,3},{2,0},{3,1},{4,6},{5,7},{6,4},{7,5},{8,10},{9,11},{10,... | collective-permute-start | bytes 196616 | tf_op jit(solution)/shard_map/ppermute | solution.py:16
  24.3 5.0 %collective-permute-start.8 = (bf16[64,1024]{1,0:T(8,128)(2,1)S(1)}, bf16[64,1024]{1,0:T(8,128)(2,1)S(1)}, u32[]{:S(2)}, u32[]{:S(2)}) collective-permute-start(bf16[64,1024]{1,0:T(8,128)(2,1)S(1)} %bitcast.11), channel_id=1, source_target_pairs={{0,1},{1,0},{2,3},{3,2},{4,5},{5,4},{6,7},{7,6},{8,9},{9,8},{10,11... | collective-permute-start | bytes 393224 | tf_op jit(solution)/shard_map/ppermute | solution.py:16
  26.0 8.4 %collective-permute-start.11 = (f32[32,2048]{1,0:T(8,128)S(1)}, f32[32,2048]{1,0:T(8,128)}, u32[]{:S(2)}, u32[]{:S(2)}) collective-permute-start(f32[32,2048]{1,0:T(8,128)S(1)} %get-tuple-element.44), channel_id=1, source_target_pairs={{0,16},{8,24},{16,0},{24,8},{1,17},{9,25},{17,1},{25,9},{2,18},{10... | collective-permute-start | bytes 786440 | tf_op jit(solution)/shard_map/ppermute | solution.py:16
  29.4 1.3 %copy-start.1 = (bf16[512,2048]{1,0:T(8,128)(2,1)}, bf16[512,2048]{1,0:T(8,128)(2,1)S(1)}, u32[]{:S(2)}) copy-start(bf16[512,2048]{1,0:T(8,128)(2,1)S(1)} %collective-permute-done.5.refs_3_.refs_2_) | copy-start | bytes 6291460
  30.7 9.4 %collective-permute-start.9 = (f16[4,16,2048]{2,1,0:T(8,128)(2,1)S(1)}, f16[4,16,2048]{2,1,0:T(8,128)(2,1)}, u32[]{:S(2)}, u32[]{:S(2)}) collective-permute-start(f16[4,16,2048]{2,1,0:T(8,128)(2,1)S(1)} %convert_element_type.14), channel_id=1, source_target_pairs={{0,16},{8,24},{16,0},{24,8},{1,17},{9,25},{17,1},{25,9},{2,18},{10... | collective-permute-start | bytes 786440 | tf_op jit(solution)/shard_map/ppermute | solution.py:16
  32.3 7.0 %collective-permute-start.7 = (bf16[64,1024]{1,0:T(8,128)(2,1)S(1)}, bf16[64,1024]{1,0:T(8,128)(2,1)S(1)}, u32[]{:S(2)}, u32[]{:S(2)}) collective-permute-start(bf16[64,1024]{1,0:T(8,128)(2,1)S(1)} %bitcast.9), channel_id=1, source_target_pairs={{0,1},{1,0},{2,3},{3,2},{4,5},{5,4},{6,7},{7,6},{8,9},{9,8},{10,11... | collective-permute-start | bytes 393224 | tf_op jit(solution)/shard_map/ppermute | solution.py:16
  35.3 1.6 %copy-start.2 = (bf16[512,2048]{1,0:T(8,128)(2,1)S(1)}, bf16[512,2048]{1,0:T(8,128)(2,1)}, u32[]{:S(2)}) copy-start(bf16[512,2048]{1,0:T(8,128)(2,1)} %copy-done.1) | copy-start | bytes 6291460
  37.7 6.4 %collective-permute-start.6 = (f16[4,16,2048]{2,1,0:T(8,128)(2,1)S(1)}, f16[4,16,2048]{2,1,0:T(8,128)(2,1)S(1)}, u32[]{:S(2)}, u32[]{:S(2)}) collective-permute-start(f16[4,16,2048]{2,1,0:T(8,128)(2,1)S(1)} %convert_element_type.12), channel_id=1, source_target_pairs={{0,16},{8,24},{16,0},{24,8},{1,17},{9,25},{17,1},{25,9},{2,18},{10... | collective-permute-start | bytes 786440 | tf_op jit(solution)/shard_map/ppermute | solution.py:16
  40.1 15.0 %copy-start.6 = (s32[32]{0:T(128)S(1)}, s32[32]{0:T(128)}, u32[]{:S(2)}) copy-start(s32[32]{0:T(128)} %param.9) | copy-start | bytes 388
  44.6 4.0 %collective-permute-start.12 = (f32[2,32,128]{2,1,0:T(8,128)S(1)}, f32[2,32,128]{2,1,0:T(8,128)S(1)}, u32[]{:S(2)}, u32[]{:S(2)}) collective-permute-start(f32[2,32,128]{2,1,0:T(8,128)S(1)} %maximum_select_fusion), channel_id=1, source_target_pairs={{0,1},{1,0},{2,3},{3,2},{4,5},{5,4},{6,7},{7,6},{8,9},{9,8},{10,11... | collective-permute-start | bytes 98312 | tf_op jit(solution)/shard_map/ppermute | solution.py:16
  48.6 4.0 %collective-permute-start.13 = (f32[2,32,128]{2,1,0:T(8,128)S(1)}, f32[2,32,128]{2,1,0:T(8,128)S(1)}, u32[]{:S(2)}, u32[]{:S(2)}) collective-permute-start(f32[2,32,128]{2,1,0:T(8,128)S(1)} %pad_maximum_fusion), channel_id=1, source_target_pairs={{0,2},{1,3},{2,0},{3,1},{4,6},{5,7},{6,4},{7,5},{8,10},{9,11},{10,... | collective-permute-start | bytes 98312 | tf_op jit(solution)/shard_map/ppermute | solution.py:16
  52.7 4.9 %collective-permute-start.14 = (f32[2,32,128]{2,1,0:T(8,128)S(1)}, f32[2,32,128]{2,1,0:T(8,128)S(1)}, u32[]{:S(2)}, u32[]{:S(2)}) collective-permute-start(f32[2,32,128]{2,1,0:T(8,128)S(1)} %pad_maximum_fusion.1), channel_id=1, source_target_pairs={{0,4},{1,5},{2,6},{3,7},{4,0},{5,1},{6,2},{7,3},{8,12},{9,13},{10,... | collective-permute-start | bytes 98312 | tf_op jit(solution)/shard_map/ppermute | solution.py:16
  55.1 2.5 %collective-permute-start.15 = (s32[32]{0:T(128)S(1)}, s32[32]{0:T(128)S(1)}, u32[]{:S(2)}, u32[]{:S(2)}) collective-permute-start(s32[32]{0:T(128)S(1)} %copy-done.6), channel_id=1, source_target_pairs={{0,8},{8,0},{16,24},{24,16},{1,9},{9,1},{17,25},{25,17},{2,10},{10... | collective-permute-start | bytes 392 | tf_op jit(solution)/shard_map/ppermute | solution.py:16
  58.6 7.5 %collective-permute-start.16 = (f32[24,128]{1,0:T(8,128)S(1)}, f32[24,128]{1,0:T(8,128)S(1)}, u32[]{:S(2)}, u32[]{:S(2)}) collective-permute-start(f32[24,128]{1,0:T(8,128)S(1)} %get-tuple-element.47.small_ref), channel_id=1, source_target_pairs={{0,8},{8,0},{16,24},{24,16},{1,9},{9,1},{17,25},{25,17},{2,10},{10... | collective-permute-start | bytes 36872 | tf_op jit(solution)/shard_map/ppermute | solution.py:16

commit v4 on v3

v4 whole, which is shorter than its diff:
```python
import functools

import jax
import jax.numpy as jnp
from jax import lax
from jax.experimental import pallas as pl
from jax.experimental.pallas import tpu as pltpu
from jax.sharding import PartitionSpec as P

HARD_SHARE = 0.3
LANES = 128
TOP = 32767.0


def swap(value, axis, mask):
    count = lax.axis_size(axis)
    return lax.ppermute(value, axis, [(i, i ^ mask) for i in range(count)])


def call(body, outs, args, limit=16, scratch=(), **extra):
    return pl.pallas_call(
        body,
        out_shape=outs,
        scratch_shapes=list(scratch),
        compiler_params=pltpu.CompilerParams(vmem_limit_bytes=limit * 1024 * 1024),
        cost_estimate=pl.CostEstimate(flops=1, bytes_accessed=1, transcendentals=0),
        **extra,
    )(*args)


VMEM = pl.BlockSpec(memory_space=pltpu.VMEM)


def split_body(own_ref, far_ref, keep_ref, give_ref):
    piece, depth = keep_ref.shape[1:]
    half = depth // 2
    x = lax.axis_index("teacher") // 2
    core = lax.axis_index("teacher") % 2
    own = own_ref[...].astype(jnp.float32)
    far = far_ref[...].astype(jnp.float32)
    for at, value in enumerate((jnp.where(x == 0, own, far), jnp.where(x == 0, far, own))):
        value = jnp.where(x == 0, value[:, :depth], value[:, depth:])
        low, high = value[:piece], value[piece:]
        for ref, part, mine in (
            (keep_ref, jnp.where(core == 0, low, high), core),
            (give_ref, jnp.where(core == 0, high, low), 1 - core),
        ):
            lead, trail = part[:, :half], part[:, half:]
            ref[at, :, :half] = jnp.where(mine == 0, lead, trail).astype(ref.dtype)
            ref[at, :, half:] = jnp.where(mine == 0, trail, lead).astype(ref.dtype)


def order_body(own_ref, sib_ref, out_ref):
    core = lax.axis_index("teacher") % 2
    for i in range(own_ref.shape[0]):
        out_ref[2 * i + core] = own_ref[i]
        out_ref[2 * i + 1 - core] = sib_ref[i]


def assemble_body(*refs):
    pieces, (away_ref, stay_ref, buf) = refs[:-3], refs[-3:]
    teachers, near = away_ref.shape[:2]
    x = lax.axis_index("teacher") // 2
    level = lax.axis_index("vocab") // 2
    for mask, piece_ref in enumerate(pieces):
        buf[level ^ mask] = piece_ref[...]
    for i in range(teachers):
        for j in range(near):
            away_ref[i, j] = buf[(1 - x) * near + j, i]
            stay_ref[i, j] = buf[x * near + j, i]


def encode(value, code_ref, at):
    width = value.shape[1]
    count = jnp.floor(jnp.max(jnp.abs(value), axis=1, keepdims=True) * 0.5) + 1.0
    code = jnp.floor(value * (TOP * 0.5 / count) + 0.5)
    code_ref[(*at, slice(None), slice(0, width))] = code.astype(jnp.int32).astype(code_ref.dtype)
    count = jnp.broadcast_to(count, (value.shape[0], LANES))
    code_ref[(*at, slice(None), slice(width, width + LANES))] = count.astype(jnp.int32).astype(code_ref.dtype)


def decode(code):
    code = code.astype(jnp.int32).astype(jnp.float32)
    width = code.shape[1] - LANES
    return code[:, :width] * (code[:, width : width + 1] * (2.0 / TOP))


def partial_body(code, *refs):
    count = (len(refs) - 2 - code) // 2
    hidden_refs, (own_ref, sib_ref), out_refs = refs[:count], refs[count : count + 2], refs[count + 2 :]
    if code:
        code_ref, out_refs = out_refs[0], (out_refs[-1], *out_refs[1:-1])
    half, width = own_ref.shape
    step = min(width, 512)
    rows = [ref[...] for ref in hidden_refs]
    rows = rows[0] if count == 1 else jnp.concatenate(rows, axis=0)
    for at in range(0, width, step):
        value = jnp.dot(rows[:, :half], own_ref[:, at : at + step], preferred_element_type=jnp.float32)
        value += jnp.dot(rows[:, half:], sib_ref[:, at : at + step], preferred_element_type=jnp.float32)
        value = value.reshape(count, *out_refs[0].shape[:2], step)
        for which, out_ref in enumerate(out_refs):
            out_ref[:, :, at : at + step] = value[which]
    if code:
        for i in range(code_ref.shape[0]):
            encode(out_refs[0][i], code_ref, (i,))


def student_body(hidden_ref, head_ref, keep_ref, *refs):
    give_refs, turned_ref = refs[:-1], refs[-1]
    core = lax.axis_index("teacher") % 2
    chips, block, width = keep_ref.shape
    step = give_refs[0].shape[2]
    near = 2
    piece = block // near // 2
    tall = hidden_ref[...].astype(jnp.float32)

    def place(x, level, side, c):
        return (((x * near + level) * 2 + side) * 2 + c) * piece

    ordered = [
        tall[place(x, level, side, c) :][:piece]
        for x in range(chips)
        for c in range(2)
        for side in range(2)
        for level in range(near)
    ]
    turned_ref[...] = jnp.concatenate(ordered, axis=0).T.astype(turned_ref.dtype)
    for at, give_ref in enumerate(give_refs):
        columns = slice(at * step, (at + 1) * step)
        value = jnp.dot(hidden_ref[...], head_ref[:, columns], preferred_element_type=jnp.float32)
        for x in range(chips):
            for side in range(2):
                for level in range(near):
                    low = value[place(x, level, side, 0) :][:piece]
                    high = value[place(x, level, side, 1) :][:piece]
                    to = (side * near + level) * piece
                    keep_ref[x, to : to + piece, columns] = jnp.where(core == 0, low, high)
                    give_ref[x, to : to + piece] = jnp.where(core == 0, high, low)


def sum_body(cuts, own_ref, *refs):
    sib_refs, (keep_ref, give_ref) = refs[:cuts], refs[cuts:]
    x = lax.axis_index("teacher") // 2
    keep_ref[...] = own_ref[x] + jnp.concatenate([ref[x] for ref in sib_refs], axis=1)
    encode(own_ref[1 - x] + jnp.concatenate([ref[1 - x] for ref in sib_refs], axis=1), give_ref, ())


def stats_body(part, kept_ref, came_ref, student_ref, far_ref, *refs):
    logits_ref, student_out_ref, stats_ref = refs[-3:]
    side = lax.axis_index("vocab") % 2
    teachers, rows, _ = logits_ref.shape
    for i in range(teachers):
        logits_ref[i] = kept_ref[i] + decode(came_ref[i])
    lane = lax.broadcasted_iota(jnp.int32, (rows, LANES), 1)
    lse = jnp.zeros((rows, LANES), jnp.float32)
    mean = jnp.zeros((rows, LANES), jnp.float32)
    tops = [jnp.max(logits_ref[i], axis=1, keepdims=True) for i in range(teachers)]
    for i in range(teachers):
        weight = jnp.exp(logits_ref[i] - tops[i])
        total = jnp.sum(weight, axis=1, keepdims=True)
        group = (lane >= i * teachers) & (lane < (i + 1) * teachers)
        lse = jnp.where(group, tops[i] + jnp.log(total), lse)
        for j in range(teachers):
            local = jnp.sum(weight * (logits_ref[j] - tops[j]), axis=1, keepdims=True) / total + tops[j]
            mean = jnp.where(lane == i * teachers + j, local, mean)
    place = side if part == 0 else 1 - side
    span = pl.ds(pl.multiple_of(place * rows, rows), rows)
    value = student_ref[span] + decode(far_ref[span])
    student_out_ref[...] = value
    top = jnp.max(value, axis=1, keepdims=True)
    total = jnp.sum(jnp.exp(value - top), axis=1, keepdims=True)
    lse = jnp.where(lane == teachers * teachers, top + jnp.log(total), lse)
    if part == 0:
        stats_ref[0] = lse
        stats_ref[1] = mean
    else:
        first_ref = refs[0]
        own = pl.ds(pl.multiple_of(side * rows, rows), rows)
        for at, value in enumerate((lse, mean)):
            stats_ref[at, own] = first_ref[at]
            stats_ref[at, span] = value


def merge(one, two):
    high = jnp.maximum(one[0], two[0])
    low = jnp.minimum(one[0], two[0])
    both = high + jnp.log1p(jnp.exp(low - high))
    return jnp.stack([both, jnp.exp(one[0] - both) * one[1] + jnp.exp(two[0] - both) * two[1]])


def residual_body(
    own_ref, other_ref, student_ref, other_student_ref, stats_ref, label_ref, sib_label_ref, small_ref, residual_ref, weight_ref
):
    side = lax.axis_index("vocab") % 2
    core = lax.axis_index("teacher") % 2
    teachers, group, width = own_ref.shape
    rows = 2 * group
    lane = lax.broadcasted_iota(jnp.int32, (rows, LANES), 1)
    lse, mean = stats_ref[0], stats_ref[1]
    small = jnp.zeros((rows, LANES), jnp.float32)
    inverse = []
    for j in range(teachers):
        norm = lse[:, j * teachers : j * teachers + 1]
        spread = jnp.zeros((rows, 1), jnp.float32)
        for i in range(teachers):
            at = i * teachers + j
            entry = norm - mean[:, at : at + 1]
            small = jnp.where(lane == at, entry, small)
            spread = spread + entry
        inverse.append(1.0 / (1.0 + spread * (1.0 / teachers)))
    total = inverse[0]
    for i in range(1, teachers):
        total = total + inverse[i]
    at = teachers * teachers
    for i in range(teachers):
        small = jnp.where(lane == at + i, inverse[i] / total * teachers, small)
    weight_ref[...] = small
    square = jnp.concatenate([small, jnp.zeros((LANES - rows, LANES), jnp.float32)], axis=0)
    small_ref[...] = square.T[: small_ref.shape[0]]
    piece = rows // 4
    token = lax.broadcasted_iota(jnp.int32, (rows, rows), 0)
    source = lax.broadcasted_iota(jnp.int32, (rows, rows), 1)
    hit = source == token // (2 * piece) * (2 * piece) + core * piece + token % piece
    mine = token // piece % 2 == core
    label = jnp.where(hit, jnp.where(mine, label_ref[...], sib_label_ref[...]), 0)
    label = jnp.sum(label, axis=1, keepdims=True) - lax.axis_index("vocab") * width
    label_at = lambda place: jnp.where(place == 0, label[:group], label[group:])
    for part, (logits_ref, value_ref) in enumerate(((own_ref, student_ref), (other_ref, other_student_ref))):
        place = side if part == 0 else 1 - side
        span = pl.ds(pl.multiple_of(place * group, group), group)
        norms = stats_ref[0, span]
        weights = weight_ref[span]
        target = jnp.where(
            lax.broadcasted_iota(jnp.int32, (group, width), 1) == label_at(place), HARD_SHARE, 0.0
        )
        for i in range(teachers):
            norm = norms[:, i * teachers : i * teachers + 1]
            log_prob = (logits_ref[i] - norm).astype(jnp.bfloat16).astype(jnp.float32)
            prob = jnp.exp(log_prob).astype(jnp.bfloat16).astype(jnp.float32)
            target = target + ((1.0 - HARD_SHARE) / teachers * weights[:, at + i : at + i + 1]) * prob
        prob = jnp.exp(value_ref[...] - norms[:, at : at + 1])
        residual_ref[span] = (prob - target).astype(jnp.bfloat16)


def grad_body(hidden_ref, residual_ref, small_ref, sib_ref, grad_ref, cross_ref, agree_ref, buf, sems):
    parts, step, _ = buf.shape
    copies = []
    for at in range(parts):
        rows = pl.ds(at * step, step)
        buf[at] = jnp.dot(hidden_ref[rows], residual_ref[...], preferred_element_type=jnp.float32)
        copies.append(pltpu.make_async_copy(buf.at[at], grad_ref.at[rows], sems.at[at]))
        copies[at].start()
    core = lax.axis_index("teacher") % 2
    block = cross_ref.shape[1]
    piece = block // 4
    source = lax.broadcasted_iota(jnp.int32, (LANES, block), 0)
    token = lax.broadcasted_iota(jnp.int32, (LANES, block), 1)
    hit = source == token // (2 * piece) * (2 * piece) + core * piece + token % piece
    mine = token // piece % 2 == core
    placed = sum(
        jnp.dot(
            ref[...],
            jnp.where(hit & which, 1.0, 0.0),
            preferred_element_type=jnp.float32,
            precision=lax.Precision.HIGHEST,
        )
        for ref, which in ((small_ref, mine), (sib_ref, jnp.logical_not(mine)))
    )
    count = cross_ref.shape[0]
    cross_ref[...] = placed[:count]
    agree_ref[...] = placed[count : count + agree_ref.shape[0]]
    for copy in copies:
        copy.wait()


def fast(teacher_hidden, teacher_head, student_hidden, student_head, labels):
    teachers = lax.axis_size("teacher")
    shards = lax.axis_size("vocab")
    chips = teachers // 2
    rows, width = teacher_head.shape
    tokens = student_hidden.shape[0]
    near = shards // 2 // chips
    piece = tokens // shards // 2
    block = tokens // teachers
    group = block // 2
    f32 = jnp.float32
    kind = teacher_hidden.dtype
    shape = jax.ShapeDtypeStruct

    any_place = pl.BlockSpec(memory_space=pl.ANY)

    def local(body, outs, args, after=(), specs=None, **extra):
        specs = [VMEM] * len(args) if specs is None else specs
        skip = len(after)
        return call(
            (lambda *refs: body(*refs[skip:])) if after else body,
            outs,
            (*after, *args),
            in_specs=[any_place] * skip + specs,
            out_specs=(VMEM,) * len(outs),
            **extra,
        )

    own = teacher_hidden[0]
    far = swap(own, "teacher", 2)
    keep, give = local(split_body, (shape((2, piece, 2 * rows), kind),) * 2, (own, far))
    split = keep
    (part,) = local(order_body, (shape((teachers, piece, 2 * rows), kind),), (keep, swap(give, "teacher", 1)))
    parts = [part] + [swap(part, "vocab", 2 * mask) for mask in range(1, shards // 2)]
    sib_head = swap(teacher_head, "teacher", 1)
    sib_labels = swap(labels, "teacher", 1)
    cuts = max(1, min(4, width // LANES))
    mine, *others, turned = local(
        student_body,
        (
            shape((chips, block, width), f32),
            *(shape((chips, block, width // cuts), f32),) * cuts,
            shape((rows, tokens), student_hidden.dtype),
        ),
        (student_hidden, student_head),
        after=(),
    )
    others = [swap(value, "teacher", 1) for value in others]
    coded = functools.partial(shape, dtype=jnp.int16)
    student, give = local(
        functools.partial(sum_body, cuts),
        (shape((block, width), f32), coded((block, width + LANES))),
        (mine, *others),
        after=(sib_head,),
    )
    student_far = swap(give, "teacher", 2)
    away, stay = local(
        assemble_body,
        (shape((teachers, near, piece, 2 * rows), kind),) * 2,
        parts,
        scratch=[pltpu.VMEM((shards // 2, teachers, piece, 2 * rows), kind)],
    )
    away = away.reshape(teachers * group, 2 * rows)
    stay = stay.reshape(teachers * group, 2 * rows)

    flat = shape((teachers, group, width), f32)

    def partial(outs, *hidden):
        code = outs[0].dtype == jnp.int16
        return local(
            functools.partial(partial_body, int(code)),
            outs,
            (*hidden, teacher_head, sib_head),
            scratch=[pltpu.VMEM(flat.shape, f32)] if code else (),
        )

    code = coded((teachers, group, width + LANES))
    sent, kept = partial((code, flat), away, stay)
    sent, away, stay = lax.optimization_barrier((sent, away, stay))
    far = swap(sent, "teacher", 2)
    other_away = swap(away, "vocab", 1)
    other_away, stay, student_far = lax.optimization_barrier((other_away, stay, student_far))
    other_stay = swap(stay, "vocab", 1)
    (other_sent,) = partial((code,), other_away)
    other_far = swap(other_sent, "teacher", 2)
    (other_kept,) = partial((flat,), other_stay)

    outs = (flat, shape((group, width), f32))
    logits, mine, first = local(
        functools.partial(stats_body, 0), (*outs, shape((2, group, LANES), f32)), (kept, far, student, student_far)
    )
    other_logits, others, stats = local(
        functools.partial(stats_body, 1),
        (*outs, shape((2, block, LANES), f32)),
        (other_kept, other_far, student, student_far, first),
    )
    mask = 1
    while mask < shards:
        stats = merge(stats, swap(stats, "vocab", mask))
        mask *= 2

    entries = teachers * teachers + teachers
    small, residual = local(
        residual_body,
        (shape((-(-entries // 8) * 8, LANES), f32), shape((block, width), jnp.bfloat16)),
        (logits, other_logits, mine, others, stats, labels.reshape(1, block), sib_labels.reshape(1, block)),
        scratch=[pltpu.VMEM((block, LANES), f32)],
    )
    sib_small = swap(small, "teacher", 1)
    gathered = lax.all_gather(residual, "teacher", axis=0, tiled=True)
    parts = 8 if rows % 8 == 0 else 1
    grad, cross, agree = call(
        grad_body,
        (shape((rows, width), f32), shape((teachers * teachers, block), f32), shape((teachers, block), f32)),
        (turned, gathered, small, sib_small),
        in_specs=[VMEM] * 4,
        out_specs=(pl.BlockSpec(memory_space=pl.ANY), VMEM, VMEM),
        scratch=[pltpu.VMEM((parts, rows // parts, width), f32), pltpu.SemaphoreType.DMA((parts,))],
    )
    return cross.T.reshape(block, teachers, teachers), agree.T, grad


def normalizer(logits):
    highest = lax.pmax(jnp.max(logits, axis=1), "vocab")
    summed = lax.psum(jnp.sum(jnp.exp(logits - highest[:, None]), axis=1), "vocab")
    return highest + jnp.log(summed)


def general(teacher_hidden, teacher_head, student_hidden, student_head, labels):
    teachers = lax.axis_size("teacher")
    block_rows = student_hidden.shape[0] // teachers
    shard_width = teacher_head.shape[1]
    gathered = lax.all_gather(teacher_hidden, "vocab", axis=1, tiled=True)
    logits = jnp.dot(
        gathered[0],
        lax.all_gather(teacher_head, "teacher", axis=0, tiled=True),
        preferred_element_type=jnp.float32,
    )
    log_prob = (logits - normalizer(logits)[:, None]).astype(jnp.bfloat16)
    exchanged = lax.all_to_all(log_prob[None], "teacher", split_axis=1, concat_axis=0, tiled=True)
    teacher_prob = jnp.exp(exchanged.astype(jnp.float32)).astype(jnp.bfloat16)
    cross_local = -jnp.einsum("itv,jtv->tij", teacher_prob, exchanged, preferred_element_type=jnp.float32)
    cross_matrix = lax.psum(cross_local, "vocab")
    inverse = 1.0 / (1.0 + jnp.mean(cross_matrix, axis=1))
    weights = inverse / jnp.sum(inverse, axis=1, keepdims=True)
    soft_mix = jnp.sum(weights.T[:, :, None] * teacher_prob.astype(jnp.float32), axis=0)
    col_offset = lax.axis_index("vocab") * shard_width
    columns = lax.broadcasted_iota(jnp.int32, (block_rows, shard_width), 1) + col_offset
    onehot = (columns == labels[:, None]).astype(jnp.float32)
    target = (1.0 - HARD_SHARE) * soft_mix + HARD_SHARE * onehot
    student_logits = lax.psum_scatter(
        jnp.dot(student_hidden, student_head, preferred_element_type=jnp.float32),
        "teacher",
        scatter_dimension=0,
        tiled=True,
    )
    student_prob = jnp.exp(student_logits - normalizer(student_logits)[:, None])
    residual = (student_prob - target).astype(jnp.bfloat16)
    student_grad = lax.dot_general(
        student_hidden,
        lax.all_gather(residual, "teacher", axis=0, tiled=True),
        (((0,), (0,)), ((), ())),
        preferred_element_type=jnp.float32,
    )
    return (cross_matrix, weights * teachers, student_grad)


def solution(mesh):
    body = fast if mesh.shape["teacher"] == 4 and mesh.shape["vocab"] == 8 else general
    return jax.shard_map(
        body,
        mesh=mesh,
        in_specs=(
            P("teacher", "vocab", None),
            P("teacher", "vocab"),
            P(None, "teacher"),
            P("teacher", "vocab"),
            P("teacher"),
        ),
        out_specs=(P("teacher", None, None), P("teacher", None), P("teacher", "vocab")),
        check_vma=False,
    )
```

time: 69.6 us -> 60.9 us (0.88)
  starting transfers between devices: 19.9 us -> 16.8 us
  local copies, waits for them, and re-layouts: 5.55 us -> 2.51 us
  other arithmetic: 2.25 us -> 0.1 us
    ppermute x17 -> x20, starting transfers between devices: 19.9 us -> 16.8 us  [swap(): return lax.ppermute(value, axis, [(i, i ^ mask) for i in range(count)])]
    unnamed x14 -> x10, local copies, waits for them, and re-layouts: 5.55 us -> 2.51 us
    add x3 -> x0, other arithmetic: 2.08 us -> none  [the longest x2 1.1 us: fast(): logits = [kept + far.astype(f32), other_kept + other_far.astype(f32)]]
    pallas_call x13 -> x12, Pallas kernels: 8.81 us -> 8.42 us  [call(): pl.pallas_call(body, out_shape=outs, scratch_shapes=list(scratch), compil...]
    ppermute x17 -> x20, waiting for transfers between devices: 24.5 us -> 24.6 us  [swap(): return lax.ppermute(value, axis, [(i, i ^ mask) for i in range(count)])]
  transfers between devices with their start and end apart: 17 -> 20, of which waited for: 10 -> 9; matrix products, arithmetic and copies ran while one was open for 3% -> 0% of each run, Pallas kernels for 6% -> 7%
where the time goes in v4:
time: 60.9 us; the launch traced here: 60.7 us
  waiting for transfers between devices  24.6 us (40%)
  starting transfers between devices  16.8 us (28%)
  Pallas kernels  8.42 us (14%)
  blocking collectives  7.43 us (12%)
  local copies, waits for them, and re-layouts  2.51 us (4%)
  between operations  0.83 us (1%)
    ppermute x20, waiting for transfers between devices, swap(): return lax.ppermute(value, axis, [(i, i ^ mask) for i in range(count)])  24.6 us
    ppermute x20, starting transfers between devices, swap(): return lax.ppermute(value, axis, [(i, i ^ mask) for i in range(count)])  16.8 us
    pallas_call x12, Pallas kernels, call(): pl.pallas_call(body, out_shape=outs, scratch_shapes=list(scratch), compil...  8.42 us
    all_gather x1, blocking collectives, fast(): gathered = lax.all_gather(residual, 'teacher', axis=0, tiled=True)  7.43 us
    unnamed x10, local copies, waits for them, and re-layouts  2.51 us
  transfers between devices with their start and end apart: 20, of which 9 were waited for; matrix products, arithmetic and copies ran while one was open for 0% of the time, Pallas kernels for 7%

profile of v4, /device:TPU:0, one launch (start us, length us, event | category | flops | bytes accessed | tf_op | source)
XLA Modules:
  0.0 60.7 jit_solution(16083306436350418365)
XLA Ops:
  0.6 0.5 collective-permute-start.5
  1.1 2.6 %collective-permute-start = (bf16[16,2048]{1,0:T(8,128)(2,1)}, bf16[16,2048]{1,0:T(8,128)(2,1)S(1)}, u32[]{:S(2)}, u32[]{:S(2)}) collective-permute-start(bf16[16,2048]{1,0:T(8,128)(2,1)} %bitcast.13), channel_id=1, source_target_pairs={{0,16},{8,24},{16,0},{24,8},{1,17},{9,25},{17,1},{25,9},{2,18},{10... | collective-permute-start | bytes 196616 | tf_op jit(solution)/shard_map/ppermute | solution.py:17
  3.7 1.6 %copy-done.1 = bf16[512,2048]{1,0:T(8,128)(2,1)S(1)} copy-done((bf16[512,2048]{1,0:T(8,128)(2,1)S(1)}, bf16[512,2048]{1,0:T(8,128)(2,1)}, u32[]{:S(2)}) %copy-start.1) | copy-done | bytes 2097176
  5.3 0.9 %copy-done.2 = bf16[128,512]{1,0:T(8,128)(2,1)S(1)} copy-done((bf16[128,512]{1,0:T(8,128)(2,1)S(1)}, bf16[128,512]{1,0:T(8,128)(2,1)}, u32[]{:S(2)}) %copy-start.2) | copy-done | bytes 131096
  6.2 0.5 shard_map.76
  6.7 0.0 copy-start
  6.7 0.2 collective-permute-start.7
  6.9 0.3 collective-permute-start.8
  7.3 0.2 collective-permute-start.9
  7.4 0.0 collective-permute-done.far_ref
  7.4 0.1 shard_map.77
  7.5 0.4 collective-permute-start.1
  7.9 0.9 %collective-permute-done.1.sib_ref = bf16[2,8,1024]{2,1,0:T(8,128)(2,1)S(1)} collective-permute-done((bf16[2,8,1024]{2,1,0:T(8,128)(2,1)S(1)}, bf16[2,8,1024]{2,1,0:T(8,128)(2,1)S(1)}, u32[]{:S(2)}, u32[]{:S(2)}) %collective-permute-start.1) | collective-permute-done | bytes 32800 | tf_op jit(solution)/shard_map/ppermute | solution.py:17
  8.8 0.3 collective-permute-start.10
  9.1 3.7 %collective-permute-start.4 = (bf16[4,8,1024]{2,1,0:T(8,128)(2,1)S(1)}, bf16[4,8,1024]{2,1,0:T(8,128)(2,1)S(1)}, u32[]{:S(2)}, u32[]{:S(2)}) collective-permute-start(bf16[4,8,1024]{2,1,0:T(8,128)(2,1)S(1)} %shard_map.78.refs_0_), channel_id=1, source_target_pairs={{0,6},{1,7},{2,4},{3,5},{4,2},{5,3},{6,0},{7,1},{8,14},{9,15},{10,... | collective-permute-start | bytes 196616 | tf_op jit(solution)/shard_map/ppermute | solution.py:17
  12.8 0.0 collective-permute-done.8.refs_3_
  12.8 0.8 %collective-permute-start.2 = (bf16[4,8,1024]{2,1,0:T(8,128)(2,1)S(1)}, bf16[4,8,1024]{2,1,0:T(8,128)(2,1)S(1)}, u32[]{:S(2)}, u32[]{:S(2)}) collective-permute-start(bf16[4,8,1024]{2,1,0:T(8,128)(2,1)S(1)} %shard_map.78.refs_0_), channel_id=1, source_target_pairs={{0,2},{1,3},{2,0},{3,1},{4,6},{5,7},{6,4},{7,5},{8,10},{9,11},{10,... | collective-permute-start | bytes 196616 | tf_op jit(solution)/shard_map/ppermute | solution.py:17
  13.6 0.0 collective-permute-done.10.refs_5_
  13.6 0.0 collective-permute-done.5.refs_3_.refs_0_.refs_2_
  13.6 0.2 shard_map.81
  13.8 0.8 %collective-permute-start.12 = (s16[32,2176]{1,0:T(8,128)(2,1)S(1)}, s16[32,2176]{1,0:T(8,128)(2,1)S(1)}, u32[]{:S(2)}, u32[]{:S(2)}) collective-permute-start(s16[32,2176]{1,0:T(8,128)(2,1)S(1)} %get-tuple-element.50), channel_id=1, source_target_pairs={{0,16},{8,24},{16,0},{24,8},{1,17},{9,25},{17,1},{25,9},{2,18},{10... | collective-permute-start | bytes 417800 | tf_op jit(solution)/shard_map/ppermute | solution.py:17
  14.6 0.8 %collective-permute-done.4.refs_3_ = bf16[4,8,1024]{2,1,0:T(8,128)(2,1)S(1)} collective-permute-done((bf16[4,8,1024]{2,1,0:T(8,128)(2,1)S(1)}, bf16[4,8,1024]{2,1,0:T(8,128)(2,1)S(1)}, u32[]{:S(2)}, u32[]{:S(2)}) %collective-permute-start.4) | collective-permute-done | bytes 65568 | tf_op jit(solution)/shard_map/ppermute | solution.py:17
  15.5 3.2 %collective-permute-done.3.refs_2_ = bf16[4,8,1024]{2,1,0:T(8,128)(2,1)S(1)} collective-permute-done((bf16[4,8,1024]{2,1,0:T(8,128)(2,1)S(1)}, bf16[4,8,1024]{2,1,0:T(8,128)(2,1)S(1)}, u32[]{:S(2)}, u32[]{:S(2)}) %collective-permute-start.3) | collective-permute-done | bytes 65568 | tf_op jit(solution)/shard_map/ppermute | solution.py:17
  18.7 0.1 shard_map.79
  18.8 0.9 %shard_map.80 = (s16[4,16,2176]{2,1,0:T(8,128)(2,1)S(1)}, f32[4,16,2048]{2,1,0:T(8,128)S(1)}) custom-call(bf16[64,1024]{1,0:T(8,128)(2,1)S(1)} %bitcast.11, bf16[64,1024]{1,0:T(8,128)(2,1)S(1)} %bitcast.9, bf16[512,2048]{1,0:T(8,128)(2,1)S(1)} %copy-done, bf16[512,2048]{1,0:T(8,128)(2,1)S(1)} %collective-permute-done.5.refs_3_.refs_0_.refs_2_), custom_call_target="tpu_custom_call" | custom-call | flops 1 | bytes 1 | tf_op jit(solution)/shard_map/pallas_call | solution.py:21
  19.7 1.6 %collective-permute-start.11 = (bf16[64,1024]{1,0:T(8,128)(2,1)S(1)}, bf16[64,1024]{1,0:T(8,128)(2,1)S(1)}, u32[]{:S(2)}, u32[]{:S(2)}) collective-permute-start(bf16[64,1024]{1,0:T(8,128)(2,1)S(1)} %bitcast.12), channel_id=1, source_target_pairs={{0,1},{1,0},{2,3},{3,2},{4,5},{5,4},{6,7},{7,6},{8,9},{9,8},{10,11... | collective-permute-start | bytes 393224 | tf_op jit(solution)/shard_map/ppermute | solution.py:17
  21.2 0.8 %collective-permute-start.6 = (s16[4,16,2176]{2,1,0:T(8,128)(2,1)S(1)}, s16[4,16,2176]{2,1,0:T(8,128)(2,1)S(1)}, u32[]{:S(2)}, u32[]{:S(2)}) collective-permute-start(s16[4,16,2176]{2,1,0:T(8,128)(2,1)S(1)} %get-tuple-element.41), channel_id=1, source_target_pairs={{0,16},{8,24},{16,0},{24,8},{1,17},{9,25},{17,1},{25,9},{2,18},{10... | collective-permute-start | bytes 835592 | tf_op jit(solution)/shard_map/ppermute | solution.py:17
  22.1 2.8 %collective-permute-done.11.refs_0_ = bf16[64,1024]{1,0:T(8,128)(2,1)S(1)} collective-permute-done((bf16[64,1024]{1,0:T(8,128)(2,1)S(1)}, bf16[64,1024]{1,0:T(8,128)(2,1)S(1)}, u32[]{:S(2)}, u32[]{:S(2)}) %collective-permute-start.11) | collective-permute-done | bytes 131104 | tf_op jit(solution)/shard_map/ppermute | solution.py:17
  24.8 0.0 collective-permute-done.12.far_ref
  24.8 1.0 %shard_map.84 = s16[4,16,2176]{2,1,0:T(8,128)(2,1)S(1)} custom-call(bf16[64,1024]{1,0:T(8,128)(2,1)S(1)} %collective-permute-done.11.refs_0_, bf16[512,2048]{1,0:T(8,128)(2,1)S(1)} %copy-done, bf16[512,2048]{1,0:T(8,128)(2,1)S(1)} %collective-permute-done.5.refs_3_.refs_0_.refs_2_), custom_call_target="tpu_custom_call" | custom-call | flops 1 | bytes 1 | tf_op jit(solution)/shard_map/pallas_call | solution.py:21
  25.9 0.9 %collective-permute-start.14 = (s16[4,16,2176]{2,1,0:T(8,128)(2,1)S(1)}, s16[4,16,2176]{2,1,0:T(8,128)(2,1)S(1)}, u32[]{:S(2)}, u32[]{:S(2)}) collective-permute-start(s16[4,16,2176]{2,1,0:T(8,128)(2,1)S(1)} %shard_map.84), channel_id=1, source_target_pairs={{0,16},{8,24},{16,0},{24,8},{1,17},{9,25},{17,1},{25,9},{2,18},{10... | collective-permute-start | bytes 835592 | tf_op jit(solution)/shard_map/ppermute | solution.py:17
  26.8 1.5 %collective-permute-start.13 = (bf16[64,1024]{1,0:T(8,128)(2,1)S(1)}, bf16[64,1024]{1,0:T(8,128)(2,1)S(1)}, u32[]{:S(2)}, u32[]{:S(2)}) collective-permute-start(bf16[64,1024]{1,0:T(8,128)(2,1)S(1)} %bitcast.10), channel_id=1, source_target_pairs={{0,1},{1,0},{2,3},{3,2},{4,5},{5,4},{6,7},{7,6},{8,9},{9,8},{10,11... | collective-permute-start | bytes 393224 | tf_op jit(solution)/shard_map/ppermute | solution.py:17
  28.3 3.4 %collective-permute-done.13.refs_0_ = bf16[64,1024]{1,0:T(8,128)(2,1)S(1)} collective-permute-done((bf16[64,1024]{1,0:T(8,128)(2,1)S(1)}, bf16[64,1024]{1,0:T(8,128)(2,1)S(1)}, u32[]{:S(2)}, u32[]{:S(2)}) %collective-permute-start.13) | collective-permute-done | bytes 131104 | tf_op jit(solution)/shard_map/ppermute | solution.py:17
  31.7 0.8 %shard_map.83.kept_ref = f32[4,16,2048]{2,1,0:T(8,128)S(1)} custom-call(bf16[64,1024]{1,0:T(8,128)(2,1)S(1)} %collective-permute-done.13.refs_0_, bf16[512,2048]{1,0:T(8,128)(2,1)S(1)} %copy-done, bf16[512,2048]{1,0:T(8,128)(2,1)S(1)} %collective-permute-done.5.refs_3_.refs_0_.refs_2_), custom_call_target="tpu_custom_call" | custom-call | flops 1 | bytes 1 | tf_op jit(solution)/shard_map/pallas_call | solution.py:21
  32.6 0.0 copy-start.4
  32.6 0.5 shard_map.82
  33.1 2.1 %collective-permute-done.14.came_ref = s16[4,16,2176]{2,1,0:T(8,128)(2,1)S(1)} collective-permute-done((s16[4,16,2176]{2,1,0:T(8,128)(2,1)S(1)}, s16[4,16,2176]{2,1,0:T(8,128)(2,1)S(1)}, u32[]{:S(2)}, u32[]{:S(2)}) %collective-permute-start.14) | collective-permute-done | bytes 278560 | tf_op jit(solution)/shard_map/ppermute | solution.py:17
  35.2 0.5 shard_map.85
  35.7 0.6 collective-permute-start.15
  36.2 3.4 %collective-permute-done.15 = f32[2,32,128]{2,1,0:T(8,128)S(1)} collective-permute-done((f32[2,32,128]{2,1,0:T(8,128)S(1)}, f32[2,32,128]{2,1,0:T(8,128)S(1)}, u32[]{:S(2)}, u32[]{:S(2)}) %collective-permute-start.15) | collective-permute-done | bytes 32800 | tf_op jit(solution)/shard_map/ppermute | solution.py:17
  39.7 0.8 %collective-permute-start.16 = (f32[2,32,128]{2,1,0:T(8,128)S(1)}, f32[2,32,128]{2,1,0:T(8,128)S(1)}, u32[]{:S(2)}, u32[]{:S(2)}) collective-permute-start(f32[2,32,128]{2,1,0:T(8,128)S(1)} %pad_maximum_fusion), channel_id=1, source_target_pairs={{0,2},{1,3},{2,0},{3,1},{4,6},{5,7},{6,4},{7,5},{8,10},{9,11},{10,... | collective-permute-start | bytes 98312 | tf_op jit(solution)/shard_map/ppermute | solution.py:17
  40.5 3.4 %collective-permute-done.16 = f32[2,32,128]{2,1,0:T(8,128)S(1)} collective-permute-done((f32[2,32,128]{2,1,0:T(8,128)S(1)}, f32[2,32,128]{2,1,0:T(8,128)S(1)}, u32[]{:S(2)}, u32[]{:S(2)}) %collective-permute-start.16) | collective-permute-done | bytes 32800 | tf_op jit(solution)/shard_map/ppermute | solution.py:17
  44.0 0.6 %collective-permute-start.17 = (f32[2,32,128]{2,1,0:T(8,128)S(1)}, f32[2,32,128]{2,1,0:T(8,128)S(1)}, u32[]{:S(2)}, u32[]{:S(2)}) collective-permute-start(f32[2,32,128]{2,1,0:T(8,128)S(1)} %pad_maximum_fusion.1), channel_id=1, source_target_pairs={{0,4},{1,5},{2,6},{3,7},{4,0},{5,1},{6,2},{7,3},{8,12},{9,13},{10,... | collective-permute-start | bytes 98312 | tf_op jit(solution)/shard_map/ppermute | solution.py:17
  44.6 4.5 %collective-permute-done.17 = f32[2,32,128]{2,1,0:T(8,128)S(1)} collective-permute-done((f32[2,32,128]{2,1,0:T(8,128)S(1)}, f32[2,32,128]{2,1,0:T(8,128)S(1)}, u32[]{:S(2)}, u32[]{:S(2)}) %collective-permute-start.17) | collective-permute-done | bytes 32800 | tf_op jit(solution)/shard_map/ppermute | solution.py:17
  49.2 1.0 %shard_map.86 = (f32[24,128]{1,0:T(8,128)S(1)}, bf16[32,2048]{1,0:T(8,128)(2,1)S(1)}) custom-call(f32[4,16,2048]{2,1,0:T(8,128)S(1)} %get-tuple-element.52.own_ref, f32[4,16,2048]{2,1,0:T(8,128)S(1)} %get-tuple-element.56.other_ref, f32[16,2048]{1,0:T(8,128)S(1)} %get-tuple-element.57.student_ref, f32[16,2048]{1,0:T(8,128)S(1)} %get-tuple-element.58.other_student_ref, ...), custom_call_target="tpu_custom_call" | custom-call | flops 1 | bytes 1 | tf_op jit(solution)/shard_map/pallas_call | solution.py:21
  50.2 0.1 collective-permute-start.19
  50.3 7.4 %all_gather.3.residual_ref = bf16[128,2048]{1,0:T(8,128)(2,1)S(1)} all-gather(bf16[32,2048]{1,0:T(8,128)(2,1)S(1)} %get-tuple-element.60), channel_id=1, replica_groups=mesh['teacher'=4,'vocab'=8] {'teacher'}, dimensions={0}, use_global_device_ids=true | all-gather | bytes 655360 | tf_op jit(solution)/shard_map/all_gather | solution.py:385
  57.7 3.0 %shard_map.87 = (f32[512,2048]{1,0:T(8,128)}, f32[16,32]{1,0:T(8,128)}, f32[4,32]{1,0:T(4,128)}) custom-call(bf16[512,128]{1,0:T(8,128)(2,1)S(1)} %get-tuple-element.34.hidden_ref, bf16[128,2048]{1,0:T(8,128)(2,1)S(1)} %all_gather.3.residual_ref, f32[24,128]{1,0:T(8,128)S(1)} %get-tuple-element.61.small_ref, f32[24,128]{1,0:T(8,128)S(1)} %collective-permute-done.19.sib_ref), custom_call_target="tpu_custom_call" | custom-call | flops 1 | bytes 1 | tf_op jit(solution)/shard_map/pallas_call | solution.py:21
  (21 shorter events, 0.1 us)
Async XLA Ops:
  0.6 13.0 %collective-permute-start.5 = (bf16[512,2048]{1,0:T(8,128)(2,1)}, bf16[512,2048]{1,0:T(8,128)(2,1)S(1)}, u32[]{:S(2)}, u32[]{:S(2)}) collective-permute-start(bf16[512,2048]{1,0:T(8,128)(2,1)} %refs_1_.3), channel_id=1, source_target_pairs={{0,8},{8,0},{16,24},{24,16},{1,9},{9,1},{17,25},{25,17},{2,10},{10... | collective-permute-start | bytes 6291464 | tf_op jit(solution)/shard_map/ppermute | solution.py:17
  1.1 6.3 %collective-permute-start = (bf16[16,2048]{1,0:T(8,128)(2,1)}, bf16[16,2048]{1,0:T(8,128)(2,1)S(1)}, u32[]{:S(2)}, u32[]{:S(2)}) collective-permute-start(bf16[16,2048]{1,0:T(8,128)(2,1)} %bitcast.13), channel_id=1, source_target_pairs={{0,16},{8,24},{16,0},{24,8},{1,17},{9,25},{17,1},{25,9},{2,18},{10... | collective-permute-start | bytes 196616 | tf_op jit(solution)/shard_map/ppermute | solution.py:17
  3.7 1.6 %copy-start.1 = (bf16[512,2048]{1,0:T(8,128)(2,1)S(1)}, bf16[512,2048]{1,0:T(8,128)(2,1)}, u32[]{:S(2)}) copy-start(bf16[512,2048]{1,0:T(8,128)(2,1)} %head_ref.1) | copy-start | bytes 6291460
  5.3 0.9 %copy-start.2 = (bf16[128,512]{1,0:T(8,128)(2,1)S(1)}, bf16[128,512]{1,0:T(8,128)(2,1)}, u32[]{:S(2)}) copy-start(bf16[128,512]{1,0:T(8,128)(2,1)} %hidden_ref.1) | copy-start | bytes 393220
  6.2 1.2 %copy-start.3 = (bf16[1,16,2048]{2,1,0:T(8,128)(2,1)S(1)}, bf16[1,16,2048]{2,1,0:T(8,128)(2,1)}, u32[]{:S(2)}) copy-start(bf16[1,16,2048]{2,1,0:T(8,128)(2,1)} %param.5) | copy-start | bytes 196612
  6.7 12.1 %copy-start = (bf16[512,2048]{1,0:T(8,128)(2,1)S(1)}, bf16[512,2048]{1,0:T(8,128)(2,1)}, u32[]{:S(2)}) copy-start(bf16[512,2048]{1,0:T(8,128)(2,1)} %refs_1_.3) | copy-start | bytes 6291460
  6.7 2.4 %collective-permute-start.7 = (f32[2,32,512]{2,1,0:T(8,128)S(1)}, f32[2,32,512]{2,1,0:T(8,128)S(1)}, u32[]{:S(2)}, u32[]{:S(2)}) collective-permute-start(f32[2,32,512]{2,1,0:T(8,128)S(1)} %get-tuple-element.43), channel_id=1, source_target_pairs={{0,8},{8,0},{16,24},{24,16},{1,9},{9,1},{17,25},{25,17},{2,10},{10... | collective-permute-start | bytes 393224 | tf_op jit(solution)/shard_map/ppermute | solution.py:17
  6.9 5.9 %collective-permute-start.8 = (f32[2,32,512]{2,1,0:T(8,128)S(1)}, f32[2,32,512]{2,1,0:T(8,128)S(1)}, u32[]{:S(2)}, u32[]{:S(2)}) collective-permute-start(f32[2,32,512]{2,1,0:T(8,128)S(1)} %get-tuple-element.44), channel_id=1, source_target_pairs={{0,8},{8,0},{16,24},{24,16},{1,9},{9,1},{17,25},{25,17},{2,10},{10... | collective-permute-start | bytes 393224 | tf_op jit(solution)/shard_map/ppermute | solution.py:17
  7.3 5.5 %collective-permute-start.9 = (f32[2,32,512]{2,1,0:T(8,128)S(1)}, f32[2,32,512]{2,1,0:T(8,128)S(1)}, u32[]{:S(2)}, u32[]{:S(2)}) collective-permute-start(f32[2,32,512]{2,1,0:T(8,128)S(1)} %get-tuple-element.45), channel_id=1, source_target_pairs={{0,8},{8,0},{16,24},{24,16},{1,9},{9,1},{17,25},{25,17},{2,10},{10... | collective-permute-start | bytes 393224 | tf_op jit(solution)/shard_map/ppermute | solution.py:17
  7.5 1.3 %collective-permute-start.1 = (bf16[2,8,1024]{2,1,0:T(8,128)(2,1)S(1)}, bf16[2,8,1024]{2,1,0:T(8,128)(2,1)S(1)}, u32[]{:S(2)}, u32[]{:S(2)}) collective-permute-start(bf16[2,8,1024]{2,1,0:T(8,128)(2,1)S(1)} %get-tuple-element.36), channel_id=1, source_target_pairs={{0,8},{8,0},{16,24},{24,16},{1,9},{9,1},{17,25},{25,17},{2,10},{10... | collective-permute-start | bytes 98312 | tf_op jit(solution)/shard_map/ppermute | solution.py:17
  8.8 4.8 %collective-permute-start.10 = (f32[2,32,512]{2,1,0:T(8,128)S(1)}, f32[2,32,512]{2,1,0:T(8,128)S(1)}, u32[]{:S(2)}, u32[]{:S(2)}) collective-permute-start(f32[2,32,512]{2,1,0:T(8,128)S(1)} %get-tuple-element.46), channel_id=1, source_target_pairs={{0,8},{8,0},{16,24},{24,16},{1,9},{9,1},{17,25},{25,17},{2,10},{10... | collective-permute-start | bytes 393224 | tf_op jit(solution)/shard_map/ppermute | solution.py:17
  9.1 6.3 %collective-permute-start.4 = (bf16[4,8,1024]{2,1,0:T(8,128)(2,1)S(1)}, bf16[4,8,1024]{2,1,0:T(8,128)(2,1)S(1)}, u32[]{:S(2)}, u32[]{:S(2)}) collective-permute-start(bf16[4,8,1024]{2,1,0:T(8,128)(2,1)S(1)} %shard_map.78.refs_0_), channel_id=1, source_target_pairs={{0,6},{1,7},{2,4},{3,5},{4,2},{5,3},{6,0},{7,1},{8,14},{9,15},{10,... | collective-permute-start | bytes 196616 | tf_op jit(solution)/shard_map/ppermute | solution.py:17
  12.8 5.9 %collective-permute-start.3 = (bf16[4,8,1024]{2,1,0:T(8,128)(2,1)S(1)}, bf16[4,8,1024]{2,1,0:T(8,128)(2,1)S(1)}, u32[]{:S(2)}, u32[]{:S(2)}) collective-permute-start(bf16[4,8,1024]{2,1,0:T(8,128)(2,1)S(1)} %shard_map.78.refs_0_), channel_id=1, source_target_pairs={{0,4},{1,5},{2,6},{3,7},{4,0},{5,1},{6,2},{7,3},{8,12},{9,13},{10,... | collective-permute-start | bytes 196616 | tf_op jit(solution)/shard_map/ppermute | solution.py:17
  12.8 5.9 %collective-permute-start.2 = (bf16[4,8,1024]{2,1,0:T(8,128)(2,1)S(1)}, bf16[4,8,1024]{2,1,0:T(8,128)(2,1)S(1)}, u32[]{:S(2)}, u32[]{:S(2)}) collective-permute-start(bf16[4,8,1024]{2,1,0:T(8,128)(2,1)S(1)} %shard_map.78.refs_0_), channel_id=1, source_target_pairs={{0,2},{1,3},{2,0},{3,1},{4,6},{5,7},{6,4},{7,5},{8,10},{9,11},{10,... | collective-permute-start | bytes 196616 | tf_op jit(solution)/shard_map/ppermute | solution.py:17
  13.8 11.0 %collective-permute-start.12 = (s16[32,2176]{1,0:T(8,128)(2,1)S(1)}, s16[32,2176]{1,0:T(8,128)(2,1)S(1)}, u32[]{:S(2)}, u32[]{:S(2)}) collective-permute-start(s16[32,2176]{1,0:T(8,128)(2,1)S(1)} %get-tuple-element.50), channel_id=1, source_target_pairs={{0,16},{8,24},{16,0},{24,8},{1,17},{9,25},{17,1},{25,9},{2,18},{10... | collective-permute-start | bytes 417800 | tf_op jit(solution)/shard_map/ppermute | solution.py:17
  19.7 5.2 %collective-permute-start.11 = (bf16[64,1024]{1,0:T(8,128)(2,1)S(1)}, bf16[64,1024]{1,0:T(8,128)(2,1)S(1)}, u32[]{:S(2)}, u32[]{:S(2)}) collective-permute-start(bf16[64,1024]{1,0:T(8,128)(2,1)S(1)} %bitcast.12), channel_id=1, source_target_pairs={{0,1},{1,0},{2,3},{3,2},{4,5},{5,4},{6,7},{7,6},{8,9},{9,8},{10,11... | collective-permute-start | bytes 393224 | tf_op jit(solution)/shard_map/ppermute | solution.py:17
  21.2 11.3 %collective-permute-start.6 = (s16[4,16,2176]{2,1,0:T(8,128)(2,1)S(1)}, s16[4,16,2176]{2,1,0:T(8,128)(2,1)S(1)}, u32[]{:S(2)}, u32[]{:S(2)}) collective-permute-start(s16[4,16,2176]{2,1,0:T(8,128)(2,1)S(1)} %get-tuple-element.41), channel_id=1, source_target_pairs={{0,16},{8,24},{16,0},{24,8},{1,17},{9,25},{17,1},{25,9},{2,18},{10... | collective-permute-start | bytes 835592 | tf_op jit(solution)/shard_map/ppermute | solution.py:17
  25.9 9.3 %collective-permute-start.14 = (s16[4,16,2176]{2,1,0:T(8,128)(2,1)S(1)}, s16[4,16,2176]{2,1,0:T(8,128)(2,1)S(1)}, u32[]{:S(2)}, u32[]{:S(2)}) collective-permute-start(s16[4,16,2176]{2,1,0:T(8,128)(2,1)S(1)} %shard_map.84), channel_id=1, source_target_pairs={{0,16},{8,24},{16,0},{24,8},{1,17},{9,25},{17,1},{25,9},{2,18},{10... | collective-permute-start | bytes 835592 | tf_op jit(solution)/shard_map/ppermute | solution.py:17
  26.8 5.0 %collective-permute-start.13 = (bf16[64,1024]{1,0:T(8,128)(2,1)S(1)}, bf16[64,1024]{1,0:T(8,128)(2,1)S(1)}, u32[]{:S(2)}, u32[]{:S(2)}) collective-permute-start(bf16[64,1024]{1,0:T(8,128)(2,1)S(1)} %bitcast.10), channel_id=1, source_target_pairs={{0,1},{1,0},{2,3},{3,2},{4,5},{5,4},{6,7},{7,6},{8,9},{9,8},{10,11... | collective-permute-start | bytes 393224 | tf_op jit(solution)/shard_map/ppermute | solution.py:17
  32.6 12.0 %copy-start.4 = (s32[32]{0:T(128)S(1)}, s32[32]{0:T(128)}, u32[]{:S(2)}) copy-start(s32[32]{0:T(128)} %param.9) | copy-start | bytes 388
  35.7 4.0 %collective-permute-start.15 = (f32[2,32,128]{2,1,0:T(8,128)S(1)}, f32[2,32,128]{2,1,0:T(8,128)S(1)}, u32[]{:S(2)}, u32[]{:S(2)}) collective-permute-start(f32[2,32,128]{2,1,0:T(8,128)S(1)} %get-tuple-element.59), channel_id=1, source_target_pairs={{0,1},{1,0},{2,3},{3,2},{4,5},{5,4},{6,7},{7,6},{8,9},{9,8},{10,11... | collective-permute-start | bytes 98312 | tf_op jit(solution)/shard_map/ppermute | solution.py:17
  39.7 4.2 %collective-permute-start.16 = (f32[2,32,128]{2,1,0:T(8,128)S(1)}, f32[2,32,128]{2,1,0:T(8,128)S(1)}, u32[]{:S(2)}, u32[]{:S(2)}) collective-permute-start(f32[2,32,128]{2,1,0:T(8,128)S(1)} %pad_maximum_fusion), channel_id=1, source_target_pairs={{0,2},{1,3},{2,0},{3,1},{4,6},{5,7},{6,4},{7,5},{8,10},{9,11},{10,... | collective-permute-start | bytes 98312 | tf_op jit(solution)/shard_map/ppermute | solution.py:17
  44.0 5.2 %collective-permute-start.17 = (f32[2,32,128]{2,1,0:T(8,128)S(1)}, f32[2,32,128]{2,1,0:T(8,128)S(1)}, u32[]{:S(2)}, u32[]{:S(2)}) collective-permute-start(f32[2,32,128]{2,1,0:T(8,128)S(1)} %pad_maximum_fusion.1), channel_id=1, source_target_pairs={{0,4},{1,5},{2,6},{3,7},{4,0},{5,1},{6,2},{7,3},{8,12},{9,13},{10,... | collective-permute-start | bytes 98312 | tf_op jit(solution)/shard_map/ppermute | solution.py:17
  44.6 4.6 %collective-permute-start.18 = (s32[32]{0:T(128)S(1)}, s32[32]{0:T(128)S(1)}, u32[]{:S(2)}, u32[]{:S(2)}) collective-permute-start(s32[32]{0:T(128)S(1)} %copy-done.4), channel_id=1, source_target_pairs={{0,8},{8,0},{16,24},{24,16},{1,9},{9,1},{17,25},{25,17},{2,10},{10... | collective-permute-start | bytes 392 | tf_op jit(solution)/shard_map/ppermute | solution.py:17
  50.2 7.5 %collective-permute-start.19 = (f32[24,128]{1,0:T(8,128)S(1)}, f32[24,128]{1,0:T(8,128)S(1)}, u32[]{:S(2)}, u32[]{:S(2)}) collective-permute-start(f32[24,128]{1,0:T(8,128)S(1)} %get-tuple-element.61.small_ref), channel_id=1, source_target_pairs={{0,8},{8,0},{16,24},{24,16},{1,9},{9,1},{17,25},{25,17},{2,10},{10... | collective-permute-start | bytes 36872 | tf_op jit(solution)/shard_map/ppermute | solution.py:17

commit v5 on v4

--- a/solution.py
+++ b/solution.py
@@ -162,7 +162,7 @@
         lse = jnp.where(group, tops[i] + jnp.log(total), lse)
         for j in range(teachers):
             local = jnp.sum(weight * (logits_ref[j] - tops[j]), axis=1, keepdims=True) / total + tops[j]
-            mean = jnp.where(lane == i * teachers + j, local, mean)
+            mean = jnp.where(lane == LANES // 2 + i * teachers + j, local, mean)
     place = side if part == 0 else 1 - side
     span = pl.ds(pl.multiple_of(place * rows, rows), rows)
     value = student_ref[span] + decode(far_ref[span])
@@ -170,22 +170,24 @@
     top = jnp.max(value, axis=1, keepdims=True)
     total = jnp.sum(jnp.exp(value - top), axis=1, keepdims=True)
     lse = jnp.where(lane == teachers * teachers, top + jnp.log(total), lse)
+    value = jnp.where(lane < LANES // 2, lse, mean)
     if part == 0:
-        stats_ref[0] = lse
-        stats_ref[1] = mean
+        stats_ref[...] = value
     else:
-        first_ref = refs[0]
-        own = pl.ds(pl.multiple_of(side * rows, rows), rows)
-        for at, value in enumerate((lse, mean)):
-            stats_ref[at, own] = first_ref[at]
-            stats_ref[at, span] = value
-
-
-def merge(one, two):
-    high = jnp.maximum(one[0], two[0])
-    low = jnp.minimum(one[0], two[0])
-    both = high + jnp.log1p(jnp.exp(low - high))
-    return jnp.stack([both, jnp.exp(one[0] - both) * one[1] + jnp.exp(two[0] - both) * two[1]])
+        stats_ref[pl.ds(pl.multiple_of(side * rows, rows), rows)] = refs[0][...]
+        stats_ref[span] = value
+
+
+def merge_body(one_ref, two_ref, out_ref):
+    half = LANES // 2
+    first = lax.broadcasted_iota(jnp.int32, one_ref.shape, 1) < half
+    one, two = one_ref[...], two_ref[...]
+    one_lse = jnp.where(first, one, pltpu.roll(one, half, 1))
+    two_lse = jnp.where(first, two, pltpu.roll(two, half, 1))
+    high = jnp.maximum(one_lse, two_lse)
+    both = high + jnp.log(1.0 + jnp.exp(jnp.minimum(one_lse, two_lse) - high))
+    mean = jnp.exp(one_lse - both) * one + jnp.exp(two_lse - both) * two
+    out_ref[...] = jnp.where(first, both, mean)
 
 
 def residual_body(
@@ -196,7 +198,7 @@
     teachers, group, width = own_ref.shape
     rows = 2 * group
     lane = lax.broadcasted_iota(jnp.int32, (rows, LANES), 1)
-    lse, mean = stats_ref[0], stats_ref[1]
+    lse, mean = stats_ref[:, : LANES // 2], stats_ref[:, LANES // 2 :]
     small = jnp.zeros((rows, LANES), jnp.float32)
     inverse = []
     for j in range(teachers):
@@ -228,7 +230,7 @@
     for part, (logits_ref, value_ref) in enumerate(((own_ref, student_ref), (other_ref, other_student_ref))):
         place = side if part == 0 else 1 - side
         span = pl.ds(pl.multiple_of(place * group, group), group)
-        norms = stats_ref[0, span]
+        norms = stats_ref[span]
         weights = weight_ref[span]
         target = jnp.where(
             lax.broadcasted_iota(jnp.int32, (group, width), 1) == label_at(place), HARD_SHARE, 0.0
@@ -242,33 +244,50 @@
         residual_ref[span] = (prob - target).astype(jnp.bfloat16)
 
 
-def grad_body(hidden_ref, residual_ref, small_ref, sib_ref, grad_ref, cross_ref, agree_ref, buf, sems):
+def grad_body(hidden_ref, *refs):
+    count = lax.axis_size("teacher")
+    residual_refs, (small_ref, sib_ref, grad_ref, cross_ref, agree_ref) = refs[:-10], refs[-10:-5]
+    buf, rows_ref, cross_buf, agree_buf, sems = refs[-5:]
+    if len(residual_refs) > 1:
+        me = lax.axis_index("teacher")
+        size = rows_ref.shape[0] // count
+        for mask, ref in enumerate(residual_refs):
+            rows_ref[pl.ds(pl.multiple_of((me ^ mask) * size, size), size)] = ref[...]
+    else:
+        rows_ref = residual_refs[0]
     parts, step, _ = buf.shape
     copies = []
+
+    def send(value, ref):
+        copies.append(pltpu.make_async_copy(value, ref, sems.at[len(copies)]))
+        copies[-1].start()
+
     for at in range(parts):
         rows = pl.ds(at * step, step)
-        buf[at] = jnp.dot(hidden_ref[rows], residual_ref[...], preferred_element_type=jnp.float32)
-        copies.append(pltpu.make_async_copy(buf.at[at], grad_ref.at[rows], sems.at[at]))
-        copies[at].start()
-    core = lax.axis_index("teacher") % 2
-    block = cross_ref.shape[1]
-    piece = block // 4
-    source = lax.broadcasted_iota(jnp.int32, (LANES, block), 0)
-    token = lax.broadcasted_iota(jnp.int32, (LANES, block), 1)
-    hit = source == token // (2 * piece) * (2 * piece) + core * piece + token % piece
-    mine = token // piece % 2 == core
-    placed = sum(
-        jnp.dot(
-            ref[...],
-            jnp.where(hit & which, 1.0, 0.0),
-            preferred_element_type=jnp.float32,
-            precision=lax.Precision.HIGHEST,
-        )
-        for ref, which in ((small_ref, mine), (sib_ref, jnp.logical_not(mine)))
-    )
-    count = cross_ref.shape[0]
-    cross_ref[...] = placed[:count]
-    agree_ref[...] = placed[count : count + agree_ref.shape[0]]
+        buf[at] = jnp.dot(hidden_ref[rows], rows_ref[...], preferred_element_type=jnp.float32)
+        send(buf.at[at], grad_ref.at[rows])
+        if at == 0:
+            core = lax.axis_index("teacher") % 2
+            block = cross_buf.shape[1]
+            piece = block // 4
+            source = lax.broadcasted_iota(jnp.int32, (LANES, block), 0)
+            token = lax.broadcasted_iota(jnp.int32, (LANES, block), 1)
+            hit = source == token // (2 * piece) * (2 * piece) + core * piece + token % piece
+            mine = token // piece % 2 == core
+            placed = sum(
+                jnp.dot(
+                    ref[...],
+                    jnp.where(hit & which, 1.0, 0.0),
+                    preferred_element_type=jnp.float32,
+                    precision=lax.Precision.HIGHEST,
+                )
+                for ref, which in ((small_ref, mine), (sib_ref, jnp.logical_not(mine)))
+            )
+            entries = cross_buf.shape[0]
+            cross_buf[...] = placed[:entries]
+            agree_buf[...] = placed[entries : entries + agree_buf.shape[0]]
+            send(cross_buf, cross_ref)
+            send(agree_buf, agree_ref)
     for copy in copies:
         copy.wait()
 
@@ -362,16 +381,16 @@
 
     outs = (flat, shape((group, width), f32))
     logits, mine, first = local(
-        functools.partial(stats_body, 0), (*outs, shape((2, group, LANES), f32)), (kept, far, student, student_far)
+        functools.partial(stats_body, 0), (*outs, shape((group, LANES), f32)), (kept, far, student, student_far)
     )
     other_logits, others, stats = local(
         functools.partial(stats_body, 1),
-        (*outs, shape((2, block, LANES), f32)),
+        (*outs, shape((block, LANES), f32)),
         (other_kept, other_far, student, student_far, first),
     )
     mask = 1
     while mask < shards:
-        stats = merge(stats, swap(stats, "vocab", mask))
+        (stats,) = local(merge_body, (shape((block, LANES), f32),), (stats, swap(stats, "vocab", mask)))
         mask *= 2
 
     entries = teachers * teachers + teachers
@@ -382,15 +401,23 @@
         scratch=[pltpu.VMEM((block, LANES), f32)],
     )
     sib_small = swap(small, "teacher", 1)
-    gathered = lax.all_gather(residual, "teacher", axis=0, tiled=True)
+    sib_residual = swap(residual, "teacher", 1)
+    far_residual = swap(residual, "teacher", 2)
+    residuals = (residual, sib_residual, far_residual, swap(far_residual, "teacher", 1))
     parts = 8 if rows % 8 == 0 else 1
+    squares = shape((teachers * teachers, block), f32), shape((teachers, block), f32)
     grad, cross, agree = call(
         grad_body,
-        (shape((rows, width), f32), shape((teachers * teachers, block), f32), shape((teachers, block), f32)),
-        (turned, gathered, small, sib_small),
-        in_specs=[VMEM] * 4,
-        out_specs=(pl.BlockSpec(memory_space=pl.ANY), VMEM, VMEM),
-        scratch=[pltpu.VMEM((parts, rows // parts, width), f32), pltpu.SemaphoreType.DMA((parts,))],
+        (shape((rows, width), f32), *squares),
+        (turned, *residuals, small, sib_small),
+        in_specs=[VMEM] * (3 + len(residuals)),
+        out_specs=(any_place,) * 3,
+        scratch=[
+            pltpu.VMEM((parts, rows // parts, width), f32),
+            pltpu.VMEM((tokens, width), residual.dtype),
+            *(pltpu.VMEM(square.shape, f32) for square in squares),
+            pltpu.SemaphoreType.DMA((parts + 2,)),
+        ],
     )
     return cross.T.reshape(block, teachers, teachers), agree.T, grad
 

time: 60.9 us -> 58.7 us (0.964)
  blocking collectives: 7.43 us -> 0 us
  waiting for transfers between devices: 24.6 us -> 29.1 us
  starting transfers between devices: 16.8 us -> 17.9 us
    all_gather x1 -> x0, blocking collectives: 7.43 us -> none  [fast(): gathered = lax.all_gather(residual, 'teacher', axis=0, tiled=True)]
    ppermute x20 -> x23, waiting for transfers between devices: 24.6 us -> 29.1 us  [swap(): return lax.ppermute(value, axis, [(i, i ^ mask) for i in range(count)])]
    ppermute x20 -> x23, starting transfers between devices: 16.8 us -> 17.9 us  [swap(): return lax.ppermute(value, axis, [(i, i ^ mask) for i in range(count)])]
    pallas_call x12 -> x15, Pallas kernels: 8.42 us -> 8.23 us  [call(): pl.pallas_call(body, out_shape=outs, scratch_shapes=list(scratch), compil...]
  transfers between devices with their start and end apart: 20 -> 23, of which waited for: 9 -> 11; matrix products, arithmetic and copies ran while one was open for 0% -> 0% of each run, Pallas kernels for 7% -> 7%
where the time goes in v5:
time: 58.7 us; the launch traced here: 58.6 us
  waiting for transfers between devices  29.1 us (50%)
  starting transfers between devices  17.9 us (30%)
  Pallas kernels  8.23 us (14%)
  local copies, waits for them, and re-layouts  2.51 us (4%)
  between operations  0.81 us (1%)
    ppermute x23, waiting for transfers between devices, swap(): return lax.ppermute(value, axis, [(i, i ^ mask) for i in range(count)])  29.1 us
    ppermute x23, starting transfers between devices, swap(): return lax.ppermute(value, axis, [(i, i ^ mask) for i in range(count)])  17.9 us
    pallas_call x15, Pallas kernels, call(): pl.pallas_call(body, out_shape=outs, scratch_shapes=list(scratch), compil...  8.23 us
    unnamed x10, local copies, waits for them, and re-layouts  2.51 us
  transfers between devices with their start and end apart: 23, of which 11 were waited for; matrix products, arithmetic and copies ran while one was open for 0% of the time, Pallas kernels for 7%

profile of v5, /device:TPU:0, one launch (start us, length us, event | category | flops | bytes accessed | tf_op | source)
XLA Modules:
  0.0 58.6 jit_solution(2104074543523157851)
XLA Ops:
  0.6 0.5 collective-permute-start.5
  1.1 2.6 %collective-permute-start = (bf16[16,2048]{1,0:T(8,128)(2,1)}, bf16[16,2048]{1,0:T(8,128)(2,1)S(1)}, u32[]{:S(2)}, u32[]{:S(2)}) collective-permute-start(bf16[16,2048]{1,0:T(8,128)(2,1)} %bitcast.13), channel_id=1, source_target_pairs={{0,16},{8,24},{16,0},{24,8},{1,17},{9,25},{17,1},{25,9},{2,18},{10... | collective-permute-start | bytes 196616 | tf_op jit(solution)/shard_map/ppermute | solution.py:17
  3.7 1.6 %copy-done.1 = bf16[512,2048]{1,0:T(8,128)(2,1)S(1)} copy-done((bf16[512,2048]{1,0:T(8,128)(2,1)S(1)}, bf16[512,2048]{1,0:T(8,128)(2,1)}, u32[]{:S(2)}) %copy-start.1) | copy-done | bytes 2097176
  5.3 0.9 %copy-done.2 = bf16[128,512]{1,0:T(8,128)(2,1)S(1)} copy-done((bf16[128,512]{1,0:T(8,128)(2,1)S(1)}, bf16[128,512]{1,0:T(8,128)(2,1)}, u32[]{:S(2)}) %copy-start.2) | copy-done | bytes 131096
  6.2 0.5 shard_map.76
  6.7 0.0 copy-start
  6.7 0.2 collective-permute-start.7
  6.9 0.3 collective-permute-start.8
  7.3 0.2 collective-permute-start.9
  7.4 0.1 shard_map.77
  7.5 0.4 collective-permute-start.1
  7.9 0.9 %collective-permute-done.1.sib_ref = bf16[2,8,1024]{2,1,0:T(8,128)(2,1)S(1)} collective-permute-done((bf16[2,8,1024]{2,1,0:T(8,128)(2,1)S(1)}, bf16[2,8,1024]{2,1,0:T(8,128)(2,1)S(1)}, u32[]{:S(2)}, u32[]{:S(2)}) %collective-permute-start.1) | collective-permute-done | bytes 32800 | tf_op jit(solution)/shard_map/ppermute | solution.py:17
  8.8 0.3 collective-permute-start.10
  9.1 3.7 %collective-permute-start.4 = (bf16[4,8,1024]{2,1,0:T(8,128)(2,1)S(1)}, bf16[4,8,1024]{2,1,0:T(8,128)(2,1)S(1)}, u32[]{:S(2)}, u32[]{:S(2)}) collective-permute-start(bf16[4,8,1024]{2,1,0:T(8,128)(2,1)S(1)} %shard_map.78.refs_0_), channel_id=1, source_target_pairs={{0,6},{1,7},{2,4},{3,5},{4,2},{5,3},{6,0},{7,1},{8,14},{9,15},{10,... | collective-permute-start | bytes 196616 | tf_op jit(solution)/shard_map/ppermute | solution.py:17
  12.8 0.8 %collective-permute-start.2 = (bf16[4,8,1024]{2,1,0:T(8,128)(2,1)S(1)}, bf16[4,8,1024]{2,1,0:T(8,128)(2,1)S(1)}, u32[]{:S(2)}, u32[]{:S(2)}) collective-permute-start(bf16[4,8,1024]{2,1,0:T(8,128)(2,1)S(1)} %shard_map.78.refs_0_), channel_id=1, source_target_pairs={{0,2},{1,3},{2,0},{3,1},{4,6},{5,7},{6,4},{7,5},{8,10},{9,11},{10,... | collective-permute-start | bytes 196616 | tf_op jit(solution)/shard_map/ppermute | solution.py:17
  13.6 0.2 shard_map.81
  13.8 0.8 %collective-permute-start.12 = (s16[32,2176]{1,0:T(8,128)(2,1)S(1)}, s16[32,2176]{1,0:T(8,128)(2,1)S(1)}, u32[]{:S(2)}, u32[]{:S(2)}) collective-permute-start(s16[32,2176]{1,0:T(8,128)(2,1)S(1)} %get-tuple-element.50), channel_id=1, source_target_pairs={{0,16},{8,24},{16,0},{24,8},{1,17},{9,25},{17,1},{25,9},{2,18},{10... | collective-permute-start | bytes 417800 | tf_op jit(solution)/shard_map/ppermute | solution.py:17
  14.6 0.8 %collective-permute-done.4.refs_3_ = bf16[4,8,1024]{2,1,0:T(8,128)(2,1)S(1)} collective-permute-done((bf16[4,8,1024]{2,1,0:T(8,128)(2,1)S(1)}, bf16[4,8,1024]{2,1,0:T(8,128)(2,1)S(1)}, u32[]{:S(2)}, u32[]{:S(2)}) %collective-permute-start.4) | collective-permute-done | bytes 65568 | tf_op jit(solution)/shard_map/ppermute | solution.py:17
  15.5 3.2 %collective-permute-done.3.refs_2_ = bf16[4,8,1024]{2,1,0:T(8,128)(2,1)S(1)} collective-permute-done((bf16[4,8,1024]{2,1,0:T(8,128)(2,1)S(1)}, bf16[4,8,1024]{2,1,0:T(8,128)(2,1)S(1)}, u32[]{:S(2)}, u32[]{:S(2)}) %collective-permute-start.3) | collective-permute-done | bytes 65568 | tf_op jit(solution)/shard_map/ppermute | solution.py:17
  18.7 0.1 shard_map.79
  18.8 0.9 %shard_map.80 = (s16[4,16,2176]{2,1,0:T(8,128)(2,1)S(1)}, f32[4,16,2048]{2,1,0:T(8,128)S(1)}) custom-call(bf16[64,1024]{1,0:T(8,128)(2,1)S(1)} %bitcast.11, bf16[64,1024]{1,0:T(8,128)(2,1)S(1)} %bitcast.9, bf16[512,2048]{1,0:T(8,128)(2,1)S(1)} %copy-done, bf16[512,2048]{1,0:T(8,128)(2,1)S(1)} %collective-permute-done.5.refs_3_.refs_0_.refs_2_), custom_call_target="tpu_custom_call" | custom-call | flops 1 | bytes 1 | tf_op jit(solution)/shard_map/pallas_call | solution.py:21
  19.7 1.6 %collective-permute-start.11 = (bf16[64,1024]{1,0:T(8,128)(2,1)S(1)}, bf16[64,1024]{1,0:T(8,128)(2,1)S(1)}, u32[]{:S(2)}, u32[]{:S(2)}) collective-permute-start(bf16[64,1024]{1,0:T(8,128)(2,1)S(1)} %bitcast.12), channel_id=1, source_target_pairs={{0,1},{1,0},{2,3},{3,2},{4,5},{5,4},{6,7},{7,6},{8,9},{9,8},{10,11... | collective-permute-start | bytes 393224 | tf_op jit(solution)/shard_map/ppermute | solution.py:17
  21.2 0.8 %collective-permute-start.6 = (s16[4,16,2176]{2,1,0:T(8,128)(2,1)S(1)}, s16[4,16,2176]{2,1,0:T(8,128)(2,1)S(1)}, u32[]{:S(2)}, u32[]{:S(2)}) collective-permute-start(s16[4,16,2176]{2,1,0:T(8,128)(2,1)S(1)} %get-tuple-element.41), channel_id=1, source_target_pairs={{0,16},{8,24},{16,0},{24,8},{1,17},{9,25},{17,1},{25,9},{2,18},{10... | collective-permute-start | bytes 835592 | tf_op jit(solution)/shard_map/ppermute | solution.py:17
  22.1 2.8 %collective-permute-done.11.refs_0_ = bf16[64,1024]{1,0:T(8,128)(2,1)S(1)} collective-permute-done((bf16[64,1024]{1,0:T(8,128)(2,1)S(1)}, bf16[64,1024]{1,0:T(8,128)(2,1)S(1)}, u32[]{:S(2)}, u32[]{:S(2)}) %collective-permute-start.11) | collective-permute-done | bytes 131104 | tf_op jit(solution)/shard_map/ppermute | solution.py:17
  24.8 1.0 %shard_map.84 = s16[4,16,2176]{2,1,0:T(8,128)(2,1)S(1)} custom-call(bf16[64,1024]{1,0:T(8,128)(2,1)S(1)} %collective-permute-done.11.refs_0_, bf16[512,2048]{1,0:T(8,128)(2,1)S(1)} %copy-done, bf16[512,2048]{1,0:T(8,128)(2,1)S(1)} %collective-permute-done.5.refs_3_.refs_0_.refs_2_), custom_call_target="tpu_custom_call" | custom-call | flops 1 | bytes 1 | tf_op jit(solution)/shard_map/pallas_call | solution.py:21
  25.9 0.9 %collective-permute-start.14 = (s16[4,16,2176]{2,1,0:T(8,128)(2,1)S(1)}, s16[4,16,2176]{2,1,0:T(8,128)(2,1)S(1)}, u32[]{:S(2)}, u32[]{:S(2)}) collective-permute-start(s16[4,16,2176]{2,1,0:T(8,128)(2,1)S(1)} %shard_map.84), channel_id=1, source_target_pairs={{0,16},{8,24},{16,0},{24,8},{1,17},{9,25},{17,1},{25,9},{2,18},{10... | collective-permute-start | bytes 835592 | tf_op jit(solution)/shard_map/ppermute | solution.py:17
  26.8 1.5 %collective-permute-start.13 = (bf16[64,1024]{1,0:T(8,128)(2,1)S(1)}, bf16[64,1024]{1,0:T(8,128)(2,1)S(1)}, u32[]{:S(2)}, u32[]{:S(2)}) collective-permute-start(bf16[64,1024]{1,0:T(8,128)(2,1)S(1)} %bitcast.10), channel_id=1, source_target_pairs={{0,1},{1,0},{2,3},{3,2},{4,5},{5,4},{6,7},{7,6},{8,9},{9,8},{10,11... | collective-permute-start | bytes 393224 | tf_op jit(solution)/shard_map/ppermute | solution.py:17
  28.3 3.4 %collective-permute-done.13.refs_0_ = bf16[64,1024]{1,0:T(8,128)(2,1)S(1)} collective-permute-done((bf16[64,1024]{1,0:T(8,128)(2,1)S(1)}, bf16[64,1024]{1,0:T(8,128)(2,1)S(1)}, u32[]{:S(2)}, u32[]{:S(2)}) %collective-permute-start.13) | collective-permute-done | bytes 131104 | tf_op jit(solution)/shard_map/ppermute | solution.py:17
  31.7 0.8 %shard_map.83.kept_ref = f32[4,16,2048]{2,1,0:T(8,128)S(1)} custom-call(bf16[64,1024]{1,0:T(8,128)(2,1)S(1)} %collective-permute-done.13.refs_0_, bf16[512,2048]{1,0:T(8,128)(2,1)S(1)} %copy-done, bf16[512,2048]{1,0:T(8,128)(2,1)S(1)} %collective-permute-done.5.refs_3_.refs_0_.refs_2_), custom_call_target="tpu_custom_call" | custom-call | flops 1 | bytes 1 | tf_op jit(solution)/shard_map/pallas_call | solution.py:21
  32.6 0.0 copy-start.4
  32.6 0.5 shard_map.82
  33.1 2.1 %collective-permute-done.14.came_ref = s16[4,16,2176]{2,1,0:T(8,128)(2,1)S(1)} collective-permute-done((s16[4,16,2176]{2,1,0:T(8,128)(2,1)S(1)}, s16[4,16,2176]{2,1,0:T(8,128)(2,1)S(1)}, u32[]{:S(2)}, u32[]{:S(2)}) %collective-permute-start.14) | collective-permute-done | bytes 278560 | tf_op jit(solution)/shard_map/ppermute | solution.py:17
  35.2 0.5 shard_map.85
  35.7 0.6 collective-permute-start.15
  36.2 3.2 %collective-permute-done.15.two_ref = f32[32,128]{1,0:T(8,128)S(1)} collective-permute-done((f32[32,128]{1,0:T(8,128)S(1)}, f32[32,128]{1,0:T(8,128)S(1)}, u32[]{:S(2)}, u32[]{:S(2)}) %collective-permute-start.15) | collective-permute-done | bytes 16416 | tf_op jit(solution)/shard_map/ppermute | solution.py:17
  39.5 0.1 shard_map.86.one_ref
  39.6 0.8 %collective-permute-start.16 = (f32[32,128]{1,0:T(8,128)S(1)}, f32[32,128]{1,0:T(8,128)S(1)}, u32[]{:S(2)}, u32[]{:S(2)}) collective-permute-start(f32[32,128]{1,0:T(8,128)S(1)} %shard_map.86.one_ref), channel_id=1, source_target_pairs={{0,2},{1,3},{2,0},{3,1},{4,6},{5,7},{6,4},{7,5},{8,10},{9,11},{10,... | collective-permute-start | bytes 49160 | tf_op jit(solution)/shard_map/ppermute | solution.py:17
  40.4 3.2 %collective-permute-done.16.two_ref = f32[32,128]{1,0:T(8,128)S(1)} collective-permute-done((f32[32,128]{1,0:T(8,128)S(1)}, f32[32,128]{1,0:T(8,128)S(1)}, u32[]{:S(2)}, u32[]{:S(2)}) %collective-permute-start.16) | collective-permute-done | bytes 16416 | tf_op jit(solution)/shard_map/ppermute | solution.py:17
  43.6 0.1 shard_map.87.one_ref
  43.7 0.6 %collective-permute-start.17 = (f32[32,128]{1,0:T(8,128)S(1)}, f32[32,128]{1,0:T(8,128)S(1)}, u32[]{:S(2)}, u32[]{:S(2)}) collective-permute-start(f32[32,128]{1,0:T(8,128)S(1)} %shard_map.87.one_ref), channel_id=1, source_target_pairs={{0,4},{1,5},{2,6},{3,7},{4,0},{5,1},{6,2},{7,3},{8,12},{9,13},{10,... | collective-permute-start | bytes 49160 | tf_op jit(solution)/shard_map/ppermute | solution.py:17
  44.3 4.3 %collective-permute-done.17.two_ref = f32[32,128]{1,0:T(8,128)S(1)} collective-permute-done((f32[32,128]{1,0:T(8,128)S(1)}, f32[32,128]{1,0:T(8,128)S(1)}, u32[]{:S(2)}, u32[]{:S(2)}) %collective-permute-start.17) | collective-permute-done | bytes 16416 | tf_op jit(solution)/shard_map/ppermute | solution.py:17
  48.6 0.1 shard_map.88.stats_ref
  48.7 1.1 %shard_map.89 = (f32[24,128]{1,0:T(8,128)S(1)}, bf16[32,2048]{1,0:T(8,128)(2,1)S(1)}) custom-call(f32[4,16,2048]{2,1,0:T(8,128)S(1)} %get-tuple-element.52.own_ref, f32[4,16,2048]{2,1,0:T(8,128)S(1)} %get-tuple-element.56.other_ref, f32[16,2048]{1,0:T(8,128)S(1)} %get-tuple-element.57.student_ref, f32[16,2048]{1,0:T(8,128)S(1)} %get-tuple-element.58.other_student_ref, ...), custom_call_target="tpu_custom_call" | custom-call | flops 1 | bytes 1 | tf_op jit(solution)/shard_map/pallas_call | solution.py:21
  49.8 0.7 %collective-permute-start.20 = (bf16[32,2048]{1,0:T(8,128)(2,1)S(1)}, bf16[32,2048]{1,0:T(8,128)(2,1)S(1)}, u32[]{:S(2)}, u32[]{:S(2)}) collective-permute-start(bf16[32,2048]{1,0:T(8,128)(2,1)S(1)} %get-tuple-element.60.refs_0_), channel_id=1, source_target_pairs={{0,16},{8,24},{16,0},{24,8},{1,17},{9,25},{17,1},{25,9},{2,18},{10... | collective-permute-start | bytes 393224 | tf_op jit(solution)/shard_map/ppermute | solution.py:17
  50.5 4.3 %collective-permute-done.20.refs_2_ = bf16[32,2048]{1,0:T(8,128)(2,1)S(1)} collective-permute-done((bf16[32,2048]{1,0:T(8,128)(2,1)S(1)}, bf16[32,2048]{1,0:T(8,128)(2,1)S(1)}, u32[]{:S(2)}, u32[]{:S(2)}) %collective-permute-start.20) | collective-permute-done | bytes 131104 | tf_op jit(solution)/shard_map/ppermute | solution.py:17
  54.8 0.5 collective-permute-start.22
  55.3 0.9 %collective-permute-done.22.refs_5_ = f32[24,128]{1,0:T(8,128)S(1)} collective-permute-done((f32[24,128]{1,0:T(8,128)S(1)}, f32[24,128]{1,0:T(8,128)S(1)}, u32[]{:S(2)}, u32[]{:S(2)}) %collective-permute-start.22) | collective-permute-done | bytes 12320 | tf_op jit(solution)/shard_map/ppermute | solution.py:17
  56.2 2.4 %shard_map.90 = (f32[512,2048]{1,0:T(8,128)}, f32[16,32]{1,0:T(8,128)}, f32[4,32]{1,0:T(4,128)}) custom-call(bf16[512,128]{1,0:T(8,128)(2,1)S(1)} %get-tuple-element.34.hidden_ref, bf16[32,2048]{1,0:T(8,128)(2,1)S(1)} %get-tuple-element.60.refs_0_, bf16[32,2048]{1,0:T(8,128)(2,1)S(1)} %collective-permute-done.19.refs_1_, ...), custom_call_target="tpu_custom_call" | custom-call | flops 1 | bytes 1 | tf_op jit(solution)/shard_map/pallas_call | solution.py:21
  (23 shorter events, 0.1 us)
Async XLA Ops:
  0.6 13.0 %collective-permute-start.5 = (bf16[512,2048]{1,0:T(8,128)(2,1)}, bf16[512,2048]{1,0:T(8,128)(2,1)S(1)}, u32[]{:S(2)}, u32[]{:S(2)}) collective-permute-start(bf16[512,2048]{1,0:T(8,128)(2,1)} %refs_1_.3), channel_id=1, source_target_pairs={{0,8},{8,0},{16,24},{24,16},{1,9},{9,1},{17,25},{25,17},{2,10},{10... | collective-permute-start | bytes 6291464 | tf_op jit(solution)/shard_map/ppermute | solution.py:17
  1.1 6.3 %collective-permute-start = (bf16[16,2048]{1,0:T(8,128)(2,1)}, bf16[16,2048]{1,0:T(8,128)(2,1)S(1)}, u32[]{:S(2)}, u32[]{:S(2)}) collective-permute-start(bf16[16,2048]{1,0:T(8,128)(2,1)} %bitcast.13), channel_id=1, source_target_pairs={{0,16},{8,24},{16,0},{24,8},{1,17},{9,25},{17,1},{25,9},{2,18},{10... | collective-permute-start | bytes 196616 | tf_op jit(solution)/shard_map/ppermute | solution.py:17
  3.7 1.6 %copy-start.1 = (bf16[512,2048]{1,0:T(8,128)(2,1)S(1)}, bf16[512,2048]{1,0:T(8,128)(2,1)}, u32[]{:S(2)}) copy-start(bf16[512,2048]{1,0:T(8,128)(2,1)} %head_ref.1) | copy-start | bytes 6291460
  5.3 0.9 %copy-start.2 = (bf16[128,512]{1,0:T(8,128)(2,1)S(1)}, bf16[128,512]{1,0:T(8,128)(2,1)}, u32[]{:S(2)}) copy-start(bf16[128,512]{1,0:T(8,128)(2,1)} %hidden_ref.1) | copy-start | bytes 393220
  6.2 1.2 %copy-start.3 = (bf16[1,16,2048]{2,1,0:T(8,128)(2,1)S(1)}, bf16[1,16,2048]{2,1,0:T(8,128)(2,1)}, u32[]{:S(2)}) copy-start(bf16[1,16,2048]{2,1,0:T(8,128)(2,1)} %param.5) | copy-start | bytes 196612
  6.7 12.1 %copy-start = (bf16[512,2048]{1,0:T(8,128)(2,1)S(1)}, bf16[512,2048]{1,0:T(8,128)(2,1)}, u32[]{:S(2)}) copy-start(bf16[512,2048]{1,0:T(8,128)(2,1)} %refs_1_.3) | copy-start | bytes 6291460
  6.7 2.4 %collective-permute-start.7 = (f32[2,32,512]{2,1,0:T(8,128)S(1)}, f32[2,32,512]{2,1,0:T(8,128)S(1)}, u32[]{:S(2)}, u32[]{:S(2)}) collective-permute-start(f32[2,32,512]{2,1,0:T(8,128)S(1)} %get-tuple-element.43), channel_id=1, source_target_pairs={{0,8},{8,0},{16,24},{24,16},{1,9},{9,1},{17,25},{25,17},{2,10},{10... | collective-permute-start | bytes 393224 | tf_op jit(solution)/shard_map/ppermute | solution.py:17
  6.9 5.9 %collective-permute-start.8 = (f32[2,32,512]{2,1,0:T(8,128)S(1)}, f32[2,32,512]{2,1,0:T(8,128)S(1)}, u32[]{:S(2)}, u32[]{:S(2)}) collective-permute-start(f32[2,32,512]{2,1,0:T(8,128)S(1)} %get-tuple-element.44), channel_id=1, source_target_pairs={{0,8},{8,0},{16,24},{24,16},{1,9},{9,1},{17,25},{25,17},{2,10},{10... | collective-permute-start | bytes 393224 | tf_op jit(solution)/shard_map/ppermute | solution.py:17
  7.3 5.5 %collective-permute-start.9 = (f32[2,32,512]{2,1,0:T(8,128)S(1)}, f32[2,32,512]{2,1,0:T(8,128)S(1)}, u32[]{:S(2)}, u32[]{:S(2)}) collective-permute-start(f32[2,32,512]{2,1,0:T(8,128)S(1)} %get-tuple-element.45), channel_id=1, source_target_pairs={{0,8},{8,0},{16,24},{24,16},{1,9},{9,1},{17,25},{25,17},{2,10},{10... | collective-permute-start | bytes 393224 | tf_op jit(solution)/shard_map/ppermute | solution.py:17
  7.5 1.3 %collective-permute-start.1 = (bf16[2,8,1024]{2,1,0:T(8,128)(2,1)S(1)}, bf16[2,8,1024]{2,1,0:T(8,128)(2,1)S(1)}, u32[]{:S(2)}, u32[]{:S(2)}) collective-permute-start(bf16[2,8,1024]{2,1,0:T(8,128)(2,1)S(1)} %get-tuple-element.36), channel_id=1, source_target_pairs={{0,8},{8,0},{16,24},{24,16},{1,9},{9,1},{17,25},{25,17},{2,10},{10... | collective-permute-start | bytes 98312 | tf_op jit(solution)/shard_map/ppermute | solution.py:17
  8.8 4.8 %collective-permute-start.10 = (f32[2,32,512]{2,1,0:T(8,128)S(1)}, f32[2,32,512]{2,1,0:T(8,128)S(1)}, u32[]{:S(2)}, u32[]{:S(2)}) collective-permute-start(f32[2,32,512]{2,1,0:T(8,128)S(1)} %get-tuple-element.46), channel_id=1, source_target_pairs={{0,8},{8,0},{16,24},{24,16},{1,9},{9,1},{17,25},{25,17},{2,10},{10... | collective-permute-start | bytes 393224 | tf_op jit(solution)/shard_map/ppermute | solution.py:17
  9.1 6.3 %collective-permute-start.4 = (bf16[4,8,1024]{2,1,0:T(8,128)(2,1)S(1)}, bf16[4,8,1024]{2,1,0:T(8,128)(2,1)S(1)}, u32[]{:S(2)}, u32[]{:S(2)}) collective-permute-start(bf16[4,8,1024]{2,1,0:T(8,128)(2,1)S(1)} %shard_map.78.refs_0_), channel_id=1, source_target_pairs={{0,6},{1,7},{2,4},{3,5},{4,2},{5,3},{6,0},{7,1},{8,14},{9,15},{10,... | collective-permute-start | bytes 196616 | tf_op jit(solution)/shard_map/ppermute | solution.py:17
  12.8 5.9 %collective-permute-start.3 = (bf16[4,8,1024]{2,1,0:T(8,128)(2,1)S(1)}, bf16[4,8,1024]{2,1,0:T(8,128)(2,1)S(1)}, u32[]{:S(2)}, u32[]{:S(2)}) collective-permute-start(bf16[4,8,1024]{2,1,0:T(8,128)(2,1)S(1)} %shard_map.78.refs_0_), channel_id=1, source_target_pairs={{0,4},{1,5},{2,6},{3,7},{4,0},{5,1},{6,2},{7,3},{8,12},{9,13},{10,... | collective-permute-start | bytes 196616 | tf_op jit(solution)/shard_map/ppermute | solution.py:17
  12.8 5.9 %collective-permute-start.2 = (bf16[4,8,1024]{2,1,0:T(8,128)(2,1)S(1)}, bf16[4,8,1024]{2,1,0:T(8,128)(2,1)S(1)}, u32[]{:S(2)}, u32[]{:S(2)}) collective-permute-start(bf16[4,8,1024]{2,1,0:T(8,128)(2,1)S(1)} %shard_map.78.refs_0_), channel_id=1, source_target_pairs={{0,2},{1,3},{2,0},{3,1},{4,6},{5,7},{6,4},{7,5},{8,10},{9,11},{10,... | collective-permute-start | bytes 196616 | tf_op jit(solution)/shard_map/ppermute | solution.py:17
  13.8 11.0 %collective-permute-start.12 = (s16[32,2176]{1,0:T(8,128)(2,1)S(1)}, s16[32,2176]{1,0:T(8,128)(2,1)S(1)}, u32[]{:S(2)}, u32[]{:S(2)}) collective-permute-start(s16[32,2176]{1,0:T(8,128)(2,1)S(1)} %get-tuple-element.50), channel_id=1, source_target_pairs={{0,16},{8,24},{16,0},{24,8},{1,17},{9,25},{17,1},{25,9},{2,18},{10... | collective-permute-start | bytes 417800 | tf_op jit(solution)/shard_map/ppermute | solution.py:17
  19.7 5.2 %collective-permute-start.11 = (bf16[64,1024]{1,0:T(8,128)(2,1)S(1)}, bf16[64,1024]{1,0:T(8,128)(2,1)S(1)}, u32[]{:S(2)}, u32[]{:S(2)}) collective-permute-start(bf16[64,1024]{1,0:T(8,128)(2,1)S(1)} %bitcast.12), channel_id=1, source_target_pairs={{0,1},{1,0},{2,3},{3,2},{4,5},{5,4},{6,7},{7,6},{8,9},{9,8},{10,11... | collective-permute-start | bytes 393224 | tf_op jit(solution)/shard_map/ppermute | solution.py:17
  21.2 11.3 %collective-permute-start.6 = (s16[4,16,2176]{2,1,0:T(8,128)(2,1)S(1)}, s16[4,16,2176]{2,1,0:T(8,128)(2,1)S(1)}, u32[]{:S(2)}, u32[]{:S(2)}) collective-permute-start(s16[4,16,2176]{2,1,0:T(8,128)(2,1)S(1)} %get-tuple-element.41), channel_id=1, source_target_pairs={{0,16},{8,24},{16,0},{24,8},{1,17},{9,25},{17,1},{25,9},{2,18},{10... | collective-permute-start | bytes 835592 | tf_op jit(solution)/shard_map/ppermute | solution.py:17
  25.9 9.3 %collective-permute-start.14 = (s16[4,16,2176]{2,1,0:T(8,128)(2,1)S(1)}, s16[4,16,2176]{2,1,0:T(8,128)(2,1)S(1)}, u32[]{:S(2)}, u32[]{:S(2)}) collective-permute-start(s16[4,16,2176]{2,1,0:T(8,128)(2,1)S(1)} %shard_map.84), channel_id=1, source_target_pairs={{0,16},{8,24},{16,0},{24,8},{1,17},{9,25},{17,1},{25,9},{2,18},{10... | collective-permute-start | bytes 835592 | tf_op jit(solution)/shard_map/ppermute | solution.py:17
  26.8 5.0 %collective-permute-start.13 = (bf16[64,1024]{1,0:T(8,128)(2,1)S(1)}, bf16[64,1024]{1,0:T(8,128)(2,1)S(1)}, u32[]{:S(2)}, u32[]{:S(2)}) collective-permute-start(bf16[64,1024]{1,0:T(8,128)(2,1)S(1)} %bitcast.10), channel_id=1, source_target_pairs={{0,1},{1,0},{2,3},{3,2},{4,5},{5,4},{6,7},{7,6},{8,9},{9,8},{10,11... | collective-permute-start | bytes 393224 | tf_op jit(solution)/shard_map/ppermute | solution.py:17
  32.6 11.7 %copy-start.4 = (s32[32]{0:T(128)S(1)}, s32[32]{0:T(128)}, u32[]{:S(2)}) copy-start(s32[32]{0:T(128)} %param.9) | copy-start | bytes 388
  35.7 3.8 %collective-permute-start.15 = (f32[32,128]{1,0:T(8,128)S(1)}, f32[32,128]{1,0:T(8,128)S(1)}, u32[]{:S(2)}, u32[]{:S(2)}) collective-permute-start(f32[32,128]{1,0:T(8,128)S(1)} %get-tuple-element.59.one_ref), channel_id=1, source_target_pairs={{0,1},{1,0},{2,3},{3,2},{4,5},{5,4},{6,7},{7,6},{8,9},{9,8},{10,11... | collective-permute-start | bytes 49160 | tf_op jit(solution)/shard_map/ppermute | solution.py:17
  39.6 4.0 %collective-permute-start.16 = (f32[32,128]{1,0:T(8,128)S(1)}, f32[32,128]{1,0:T(8,128)S(1)}, u32[]{:S(2)}, u32[]{:S(2)}) collective-permute-start(f32[32,128]{1,0:T(8,128)S(1)} %shard_map.86.one_ref), channel_id=1, source_target_pairs={{0,2},{1,3},{2,0},{3,1},{4,6},{5,7},{6,4},{7,5},{8,10},{9,11},{10,... | collective-permute-start | bytes 49160 | tf_op jit(solution)/shard_map/ppermute | solution.py:17
  43.7 4.9 %collective-permute-start.17 = (f32[32,128]{1,0:T(8,128)S(1)}, f32[32,128]{1,0:T(8,128)S(1)}, u32[]{:S(2)}, u32[]{:S(2)}) collective-permute-start(f32[32,128]{1,0:T(8,128)S(1)} %shard_map.87.one_ref), channel_id=1, source_target_pairs={{0,4},{1,5},{2,6},{3,7},{4,0},{5,1},{6,2},{7,3},{8,12},{9,13},{10,... | collective-permute-start | bytes 49160 | tf_op jit(solution)/shard_map/ppermute | solution.py:17
  44.3 4.4 %collective-permute-start.18 = (s32[32]{0:T(128)S(1)}, s32[32]{0:T(128)S(1)}, u32[]{:S(2)}, u32[]{:S(2)}) collective-permute-start(s32[32]{0:T(128)S(1)} %copy-done.4), channel_id=1, source_target_pairs={{0,8},{8,0},{16,24},{24,16},{1,9},{9,1},{17,25},{25,17},{2,10},{10... | collective-permute-start | bytes 392 | tf_op jit(solution)/shard_map/ppermute | solution.py:17
  49.8 5.0 %collective-permute-start.20 = (bf16[32,2048]{1,0:T(8,128)(2,1)S(1)}, bf16[32,2048]{1,0:T(8,128)(2,1)S(1)}, u32[]{:S(2)}, u32[]{:S(2)}) collective-permute-start(bf16[32,2048]{1,0:T(8,128)(2,1)S(1)} %get-tuple-element.60.refs_0_), channel_id=1, source_target_pairs={{0,16},{8,24},{16,0},{24,8},{1,17},{9,25},{17,1},{25,9},{2,18},{10... | collective-permute-start | bytes 393224 | tf_op jit(solution)/shard_map/ppermute | solution.py:17
  50.5 5.7 %collective-permute-start.19 = (bf16[32,2048]{1,0:T(8,128)(2,1)S(1)}, bf16[32,2048]{1,0:T(8,128)(2,1)S(1)}, u32[]{:S(2)}, u32[]{:S(2)}) collective-permute-start(bf16[32,2048]{1,0:T(8,128)(2,1)S(1)} %get-tuple-element.60.refs_0_), channel_id=1, source_target_pairs={{0,8},{8,0},{16,24},{24,16},{1,9},{9,1},{17,25},{25,17},{2,10},{10... | collective-permute-start | bytes 393224 | tf_op jit(solution)/shard_map/ppermute | solution.py:17
  54.8 1.4 %collective-permute-start.21 = (bf16[32,2048]{1,0:T(8,128)(2,1)S(1)}, bf16[32,2048]{1,0:T(8,128)(2,1)S(1)}, u32[]{:S(2)}, u32[]{:S(2)}) collective-permute-start(bf16[32,2048]{1,0:T(8,128)(2,1)S(1)} %collective-permute-done.20.refs_2_), channel_id=1, source_target_pairs={{0,8},{8,0},{16,24},{24,16},{1,9},{9,1},{17,25},{25,17},{2,10},{10... | collective-permute-start | bytes 393224 | tf_op jit(solution)/shard_map/ppermute | solution.py:17
  54.8 1.4 %collective-permute-start.22 = (f32[24,128]{1,0:T(8,128)S(1)}, f32[24,128]{1,0:T(8,128)S(1)}, u32[]{:S(2)}, u32[]{:S(2)}) collective-permute-start(f32[24,128]{1,0:T(8,128)S(1)} %get-tuple-element.61.refs_4_), channel_id=1, source_target_pairs={{0,8},{8,0},{16,24},{24,16},{1,9},{9,1},{17,25},{25,17},{2,10},{10... | collective-permute-start | bytes 36872 | tf_op jit(solution)/shard_map/ppermute | solution.py:17

commit v6 on v5

--- a/solution.py
+++ b/solution.py
@@ -373,7 +373,8 @@
     sent, away, stay = lax.optimization_barrier((sent, away, stay))
     far = swap(sent, "teacher", 2)
     other_away = swap(away, "vocab", 1)
-    other_away, stay, student_far = lax.optimization_barrier((other_away, stay, student_far))
+    stay, far = lax.optimization_barrier((stay, far))
+    other_away, student_far = lax.optimization_barrier((other_away, student_far))
     other_stay = swap(stay, "vocab", 1)
     (other_sent,) = partial((code,), other_away)
     other_far = swap(other_sent, "teacher", 2)

time: 58.7 us -> 57.2 us (0.974)
  waiting for transfers between devices: 29.1 us -> 25.2 us
  starting transfers between devices: 17.9 us -> 20.3 us
    ppermute x23, waiting for transfers between devices: 29.1 us -> 25.2 us  [swap(): return lax.ppermute(value, axis, [(i, i ^ mask) for i in range(count)])]
    ppermute x23, starting transfers between devices: 17.9 us -> 20.3 us  [swap(): return lax.ppermute(value, axis, [(i, i ^ mask) for i in range(count)])]
where the time goes in v6:
time: 57.2 us; the launch traced here: 57 us
  waiting for transfers between devices  25.2 us (44%)
  starting transfers between devices  20.3 us (35%)
  Pallas kernels  8.21 us (14%)
  local copies, waits for them, and re-layouts  2.51 us (4%)
  between operations  0.8 us (1%)
    ppermute x23, waiting for transfers between devices, swap(): return lax.ppermute(value, axis, [(i, i ^ mask) for i in range(count)])  25.2 us
    ppermute x23, starting transfers between devices, swap(): return lax.ppermute(value, axis, [(i, i ^ mask) for i in range(count)])  20.3 us
    pallas_call x15, Pallas kernels, call(): pl.pallas_call(body, out_shape=outs, scratch_shapes=list(scratch), compil...  8.21 us
    unnamed x10, local copies, waits for them, and re-layouts  2.51 us
  transfers between devices with their start and end apart: 23, of which 11 were waited for; matrix products, arithmetic and copies ran while one was open for 0% of the time, Pallas kernels for 7%

profile of v6, /device:TPU:0, one launch (start us, length us, event | category | flops | bytes accessed | tf_op | source)
XLA Modules:
  0.0 57.0 jit_solution(4712008677294011146)
XLA Ops:
  0.6 0.5 collective-permute-start.5
  1.1 2.6 %collective-permute-start = (bf16[16,2048]{1,0:T(8,128)(2,1)}, bf16[16,2048]{1,0:T(8,128)(2,1)S(1)}, u32[]{:S(2)}, u32[]{:S(2)}) collective-permute-start(bf16[16,2048]{1,0:T(8,128)(2,1)} %bitcast.13), channel_id=1, source_target_pairs={{0,16},{8,24},{16,0},{24,8},{1,17},{9,25},{17,1},{25,9},{2,18},{10... | collective-permute-start | bytes 196616 | tf_op jit(solution)/shard_map/ppermute | solution.py:17
  3.7 1.6 %copy-done.1 = bf16[512,2048]{1,0:T(8,128)(2,1)S(1)} copy-done((bf16[512,2048]{1,0:T(8,128)(2,1)S(1)}, bf16[512,2048]{1,0:T(8,128)(2,1)}, u32[]{:S(2)}) %copy-start.1) | copy-done | bytes 2097176
  5.3 0.9 %copy-done.2 = bf16[128,512]{1,0:T(8,128)(2,1)S(1)} copy-done((bf16[128,512]{1,0:T(8,128)(2,1)S(1)}, bf16[128,512]{1,0:T(8,128)(2,1)}, u32[]{:S(2)}) %copy-start.2) | copy-done | bytes 131096
  6.2 0.5 shard_map.76
  6.7 0.0 copy-start
  6.7 0.2 collective-permute-start.7
  6.9 0.3 collective-permute-start.8
  7.3 0.2 collective-permute-start.9
  7.4 0.1 shard_map.77
  7.5 0.4 collective-permute-start.1
  7.9 0.9 %collective-permute-done.1.sib_ref = bf16[2,8,1024]{2,1,0:T(8,128)(2,1)S(1)} collective-permute-done((bf16[2,8,1024]{2,1,0:T(8,128)(2,1)S(1)}, bf16[2,8,1024]{2,1,0:T(8,128)(2,1)S(1)}, u32[]{:S(2)}, u32[]{:S(2)}) %collective-permute-start.1) | collective-permute-done | bytes 32800 | tf_op jit(solution)/shard_map/ppermute | solution.py:17
  8.8 0.3 collective-permute-start.10
  9.1 3.7 %collective-permute-start.4 = (bf16[4,8,1024]{2,1,0:T(8,128)(2,1)S(1)}, bf16[4,8,1024]{2,1,0:T(8,128)(2,1)S(1)}, u32[]{:S(2)}, u32[]{:S(2)}) collective-permute-start(bf16[4,8,1024]{2,1,0:T(8,128)(2,1)S(1)} %shard_map.78.refs_0_), channel_id=1, source_target_pairs={{0,6},{1,7},{2,4},{3,5},{4,2},{5,3},{6,0},{7,1},{8,14},{9,15},{10,... | collective-permute-start | bytes 196616 | tf_op jit(solution)/shard_map/ppermute | solution.py:17
  12.8 0.8 %collective-permute-start.2 = (bf16[4,8,1024]{2,1,0:T(8,128)(2,1)S(1)}, bf16[4,8,1024]{2,1,0:T(8,128)(2,1)S(1)}, u32[]{:S(2)}, u32[]{:S(2)}) collective-permute-start(bf16[4,8,1024]{2,1,0:T(8,128)(2,1)S(1)} %shard_map.78.refs_0_), channel_id=1, source_target_pairs={{0,2},{1,3},{2,0},{3,1},{4,6},{5,7},{6,4},{7,5},{8,10},{9,11},{10,... | collective-permute-start | bytes 196616 | tf_op jit(solution)/shard_map/ppermute | solution.py:17
  13.6 0.2 shard_map.81
  13.8 0.8 %collective-permute-start.12 = (s16[32,2176]{1,0:T(8,128)(2,1)S(1)}, s16[32,2176]{1,0:T(8,128)(2,1)S(1)}, u32[]{:S(2)}, u32[]{:S(2)}) collective-permute-start(s16[32,2176]{1,0:T(8,128)(2,1)S(1)} %get-tuple-element.52), channel_id=1, source_target_pairs={{0,16},{8,24},{16,0},{24,8},{1,17},{9,25},{17,1},{25,9},{2,18},{10... | collective-permute-start | bytes 417800 | tf_op jit(solution)/shard_map/ppermute | solution.py:17
  14.6 0.9 %collective-permute-done.4.refs_3_ = bf16[4,8,1024]{2,1,0:T(8,128)(2,1)S(1)} collective-permute-done((bf16[4,8,1024]{2,1,0:T(8,128)(2,1)S(1)}, bf16[4,8,1024]{2,1,0:T(8,128)(2,1)S(1)}, u32[]{:S(2)}, u32[]{:S(2)}) %collective-permute-start.4) | collective-permute-done | bytes 65568 | tf_op jit(solution)/shard_map/ppermute | solution.py:17
  15.5 3.2 %collective-permute-done.3.refs_2_ = bf16[4,8,1024]{2,1,0:T(8,128)(2,1)S(1)} collective-permute-done((bf16[4,8,1024]{2,1,0:T(8,128)(2,1)S(1)}, bf16[4,8,1024]{2,1,0:T(8,128)(2,1)S(1)}, u32[]{:S(2)}, u32[]{:S(2)}) %collective-permute-start.3) | collective-permute-done | bytes 65568 | tf_op jit(solution)/shard_map/ppermute | solution.py:17
  18.7 0.1 shard_map.79
  18.8 0.9 %shard_map.80 = (s16[4,16,2176]{2,1,0:T(8,128)(2,1)S(1)}, f32[4,16,2048]{2,1,0:T(8,128)S(1)}) custom-call(bf16[64,1024]{1,0:T(8,128)(2,1)S(1)} %bitcast.11, bf16[64,1024]{1,0:T(8,128)(2,1)S(1)} %bitcast.9, bf16[512,2048]{1,0:T(8,128)(2,1)S(1)} %copy-done, bf16[512,2048]{1,0:T(8,128)(2,1)S(1)} %collective-permute-done.5.refs_3_.refs_0_.refs_2_), custom_call_target="tpu_custom_call" | custom-call | flops 1 | bytes 1 | tf_op jit(solution)/shard_map/pallas_call | solution.py:21
  19.7 0.9 %collective-permute-start.6 = (s16[4,16,2176]{2,1,0:T(8,128)(2,1)S(1)}, s16[4,16,2176]{2,1,0:T(8,128)(2,1)S(1)}, u32[]{:S(2)}, u32[]{:S(2)}) collective-permute-start(s16[4,16,2176]{2,1,0:T(8,128)(2,1)S(1)} %get-tuple-element.43), channel_id=1, source_target_pairs={{0,16},{8,24},{16,0},{24,8},{1,17},{9,25},{17,1},{25,9},{2,18},{10... | collective-permute-start | bytes 835592 | tf_op jit(solution)/shard_map/ppermute | solution.py:17
  20.6 1.5 %collective-permute-start.11 = (bf16[64,1024]{1,0:T(8,128)(2,1)S(1)}, bf16[64,1024]{1,0:T(8,128)(2,1)S(1)}, u32[]{:S(2)}, u32[]{:S(2)}) collective-permute-start(bf16[64,1024]{1,0:T(8,128)(2,1)S(1)} %bitcast.12), channel_id=1, source_target_pairs={{0,1},{1,0},{2,3},{3,2},{4,5},{5,4},{6,7},{7,6},{8,9},{9,8},{10,11... | collective-permute-start | bytes 393224 | tf_op jit(solution)/shard_map/ppermute | solution.py:17
  22.1 3.5 %collective-permute-done.11.refs_0_ = bf16[64,1024]{1,0:T(8,128)(2,1)S(1)} collective-permute-done((bf16[64,1024]{1,0:T(8,128)(2,1)S(1)}, bf16[64,1024]{1,0:T(8,128)(2,1)S(1)}, u32[]{:S(2)}, u32[]{:S(2)}) %collective-permute-start.11) | collective-permute-done | bytes 131104 | tf_op jit(solution)/shard_map/ppermute | solution.py:17
  25.5 1.0 %shard_map.84 = s16[4,16,2176]{2,1,0:T(8,128)(2,1)S(1)} custom-call(bf16[64,1024]{1,0:T(8,128)(2,1)S(1)} %collective-permute-done.11.refs_0_, bf16[512,2048]{1,0:T(8,128)(2,1)S(1)} %copy-done, bf16[512,2048]{1,0:T(8,128)(2,1)S(1)} %collective-permute-done.5.refs_3_.refs_0_.refs_2_), custom_call_target="tpu_custom_call" | custom-call | flops 1 | bytes 1 | tf_op jit(solution)/shard_map/pallas_call | solution.py:21
  26.6 1.3 %collective-permute-start.14 = (s16[4,16,2176]{2,1,0:T(8,128)(2,1)S(1)}, s16[4,16,2176]{2,1,0:T(8,128)(2,1)S(1)}, u32[]{:S(2)}, u32[]{:S(2)}) collective-permute-start(s16[4,16,2176]{2,1,0:T(8,128)(2,1)S(1)} %shard_map.84), channel_id=1, source_target_pairs={{0,16},{8,24},{16,0},{24,8},{1,17},{9,25},{17,1},{25,9},{2,18},{10... | collective-permute-start | bytes 835592 | tf_op jit(solution)/shard_map/ppermute | solution.py:17
  27.8 0.3 collective-permute-done.6.came_ref
  28.1 1.5 %collective-permute-start.13 = (bf16[64,1024]{1,0:T(8,128)(2,1)S(1)}, bf16[64,1024]{1,0:T(8,128)(2,1)S(1)}, u32[]{:S(2)}, u32[]{:S(2)}) collective-permute-start(bf16[64,1024]{1,0:T(8,128)(2,1)S(1)} %bitcast.10), channel_id=1, source_target_pairs={{0,1},{1,0},{2,3},{3,2},{4,5},{5,4},{6,7},{7,6},{8,9},{9,8},{10,11... | collective-permute-start | bytes 393224 | tf_op jit(solution)/shard_map/ppermute | solution.py:17
  29.7 0.5 shard_map.82
  30.1 3.0 %collective-permute-done.13.refs_0_ = bf16[64,1024]{1,0:T(8,128)(2,1)S(1)} collective-permute-done((bf16[64,1024]{1,0:T(8,128)(2,1)S(1)}, bf16[64,1024]{1,0:T(8,128)(2,1)S(1)}, u32[]{:S(2)}, u32[]{:S(2)}) %collective-permute-start.13) | collective-permute-done | bytes 131104 | tf_op jit(solution)/shard_map/ppermute | solution.py:17
  33.1 0.8 %shard_map.83.kept_ref = f32[4,16,2048]{2,1,0:T(8,128)S(1)} custom-call(bf16[64,1024]{1,0:T(8,128)(2,1)S(1)} %collective-permute-done.13.refs_0_, bf16[512,2048]{1,0:T(8,128)(2,1)S(1)} %copy-done, bf16[512,2048]{1,0:T(8,128)(2,1)S(1)} %collective-permute-done.5.refs_3_.refs_0_.refs_2_), custom_call_target="tpu_custom_call" | custom-call | flops 1 | bytes 1 | tf_op jit(solution)/shard_map/pallas_call | solution.py:21
  33.9 0.0 collective-permute-done.14.came_ref
  34.0 0.5 shard_map.85
  34.4 1.6 %collective-permute-start.15 = (f32[32,128]{1,0:T(8,128)S(1)}, f32[32,128]{1,0:T(8,128)S(1)}, u32[]{:S(2)}, u32[]{:S(2)}) collective-permute-start(f32[32,128]{1,0:T(8,128)S(1)} %get-tuple-element.61.one_ref), channel_id=1, source_target_pairs={{0,1},{1,0},{2,3},{3,2},{4,5},{5,4},{6,7},{7,6},{8,9},{9,8},{10,11... | collective-permute-start | bytes 49160 | tf_op jit(solution)/shard_map/ppermute | solution.py:17
  36.0 2.2 %collective-permute-done.15.two_ref = f32[32,128]{1,0:T(8,128)S(1)} collective-permute-done((f32[32,128]{1,0:T(8,128)S(1)}, f32[32,128]{1,0:T(8,128)S(1)}, u32[]{:S(2)}, u32[]{:S(2)}) %collective-permute-start.15) | collective-permute-done | bytes 16416 | tf_op jit(solution)/shard_map/ppermute | solution.py:17
  38.2 0.1 shard_map.86.one_ref
  38.4 0.9 %collective-permute-start.16 = (f32[32,128]{1,0:T(8,128)S(1)}, f32[32,128]{1,0:T(8,128)S(1)}, u32[]{:S(2)}, u32[]{:S(2)}) collective-permute-start(f32[32,128]{1,0:T(8,128)S(1)} %shard_map.86.one_ref), channel_id=1, source_target_pairs={{0,2},{1,3},{2,0},{3,1},{4,6},{5,7},{6,4},{7,5},{8,10},{9,11},{10,... | collective-permute-start | bytes 49160 | tf_op jit(solution)/shard_map/ppermute | solution.py:17
  39.3 2.9 %collective-permute-done.16.two_ref = f32[32,128]{1,0:T(8,128)S(1)} collective-permute-done((f32[32,128]{1,0:T(8,128)S(1)}, f32[32,128]{1,0:T(8,128)S(1)}, u32[]{:S(2)}, u32[]{:S(2)}) %collective-permute-start.16) | collective-permute-done | bytes 16416 | tf_op jit(solution)/shard_map/ppermute | solution.py:17
  42.2 0.1 shard_map.87.one_ref
  42.3 1.2 %collective-permute-start.17 = (f32[32,128]{1,0:T(8,128)S(1)}, f32[32,128]{1,0:T(8,128)S(1)}, u32[]{:S(2)}, u32[]{:S(2)}) collective-permute-start(f32[32,128]{1,0:T(8,128)S(1)} %shard_map.87.one_ref), channel_id=1, source_target_pairs={{0,4},{1,5},{2,6},{3,7},{4,0},{5,1},{6,2},{7,3},{8,12},{9,13},{10,... | collective-permute-start | bytes 49160 | tf_op jit(solution)/shard_map/ppermute | solution.py:17
  43.4 3.5 %collective-permute-done.17.two_ref = f32[32,128]{1,0:T(8,128)S(1)} collective-permute-done((f32[32,128]{1,0:T(8,128)S(1)}, f32[32,128]{1,0:T(8,128)S(1)}, u32[]{:S(2)}, u32[]{:S(2)}) %collective-permute-start.17) | collective-permute-done | bytes 16416 | tf_op jit(solution)/shard_map/ppermute | solution.py:17
  47.0 0.1 shard_map.88.stats_ref
  47.1 1.1 %shard_map.89 = (f32[24,128]{1,0:T(8,128)S(1)}, bf16[32,2048]{1,0:T(8,128)(2,1)S(1)}) custom-call(f32[4,16,2048]{2,1,0:T(8,128)S(1)} %get-tuple-element.54.own_ref, f32[4,16,2048]{2,1,0:T(8,128)S(1)} %get-tuple-element.58.other_ref, f32[16,2048]{1,0:T(8,128)S(1)} %get-tuple-element.59.student_ref, f32[16,2048]{1,0:T(8,128)S(1)} %get-tuple-element.60.other_student_ref, ...), custom_call_target="tpu_custom_call" | custom-call | flops 1 | bytes 1 | tf_op jit(solution)/shard_map/pallas_call | solution.py:21
  48.2 1.1 %collective-permute-start.20 = (bf16[32,2048]{1,0:T(8,128)(2,1)S(1)}, bf16[32,2048]{1,0:T(8,128)(2,1)S(1)}, u32[]{:S(2)}, u32[]{:S(2)}) collective-permute-start(bf16[32,2048]{1,0:T(8,128)(2,1)S(1)} %get-tuple-element.62.refs_0_), channel_id=1, source_target_pairs={{0,16},{8,24},{16,0},{24,8},{1,17},{9,25},{17,1},{25,9},{2,18},{10... | collective-permute-start | bytes 393224 | tf_op jit(solution)/shard_map/ppermute | solution.py:17
  49.3 4.0 %collective-permute-done.20.refs_2_ = bf16[32,2048]{1,0:T(8,128)(2,1)S(1)} collective-permute-done((bf16[32,2048]{1,0:T(8,128)(2,1)S(1)}, bf16[32,2048]{1,0:T(8,128)(2,1)S(1)}, u32[]{:S(2)}, u32[]{:S(2)}) %collective-permute-start.20) | collective-permute-done | bytes 131104 | tf_op jit(solution)/shard_map/ppermute | solution.py:17
  53.2 0.5 collective-permute-start.22
  53.7 0.9 %collective-permute-done.22.refs_5_ = f32[24,128]{1,0:T(8,128)S(1)} collective-permute-done((f32[24,128]{1,0:T(8,128)S(1)}, f32[24,128]{1,0:T(8,128)S(1)}, u32[]{:S(2)}, u32[]{:S(2)}) %collective-permute-start.22) | collective-permute-done | bytes 12320 | tf_op jit(solution)/shard_map/ppermute | solution.py:17
  54.6 2.4 %shard_map.90 = (f32[512,2048]{1,0:T(8,128)}, f32[16,32]{1,0:T(8,128)}, f32[4,32]{1,0:T(4,128)}) custom-call(bf16[512,128]{1,0:T(8,128)(2,1)S(1)} %get-tuple-element.35.hidden_ref, bf16[32,2048]{1,0:T(8,128)(2,1)S(1)} %get-tuple-element.62.refs_0_, bf16[32,2048]{1,0:T(8,128)(2,1)S(1)} %collective-permute-done.19.refs_1_, ...), custom_call_target="tpu_custom_call" | custom-call | flops 1 | bytes 1 | tf_op jit(solution)/shard_map/pallas_call | solution.py:21
  (23 shorter events, 0.1 us)
Async XLA Ops:
  0.6 13.0 %collective-permute-start.5 = (bf16[512,2048]{1,0:T(8,128)(2,1)}, bf16[512,2048]{1,0:T(8,128)(2,1)S(1)}, u32[]{:S(2)}, u32[]{:S(2)}) collective-permute-start(bf16[512,2048]{1,0:T(8,128)(2,1)} %refs_1_.3), channel_id=1, source_target_pairs={{0,8},{8,0},{16,24},{24,16},{1,9},{9,1},{17,25},{25,17},{2,10},{10... | collective-permute-start | bytes 6291464 | tf_op jit(solution)/shard_map/ppermute | solution.py:17
  1.1 6.3 %collective-permute-start = (bf16[16,2048]{1,0:T(8,128)(2,1)}, bf16[16,2048]{1,0:T(8,128)(2,1)S(1)}, u32[]{:S(2)}, u32[]{:S(2)}) collective-permute-start(bf16[16,2048]{1,0:T(8,128)(2,1)} %bitcast.13), channel_id=1, source_target_pairs={{0,16},{8,24},{16,0},{24,8},{1,17},{9,25},{17,1},{25,9},{2,18},{10... | collective-permute-start | bytes 196616 | tf_op jit(solution)/shard_map/ppermute | solution.py:17
  3.7 1.6 %copy-start.1 = (bf16[512,2048]{1,0:T(8,128)(2,1)S(1)}, bf16[512,2048]{1,0:T(8,128)(2,1)}, u32[]{:S(2)}) copy-start(bf16[512,2048]{1,0:T(8,128)(2,1)} %head_ref.1) | copy-start | bytes 6291460
  5.3 0.9 %copy-start.2 = (bf16[128,512]{1,0:T(8,128)(2,1)S(1)}, bf16[128,512]{1,0:T(8,128)(2,1)}, u32[]{:S(2)}) copy-start(bf16[128,512]{1,0:T(8,128)(2,1)} %hidden_ref.1) | copy-start | bytes 393220
  6.2 1.2 %copy-start.3 = (bf16[1,16,2048]{2,1,0:T(8,128)(2,1)S(1)}, bf16[1,16,2048]{2,1,0:T(8,128)(2,1)}, u32[]{:S(2)}) copy-start(bf16[1,16,2048]{2,1,0:T(8,128)(2,1)} %param.5) | copy-start | bytes 196612
  6.7 12.1 %copy-start = (bf16[512,2048]{1,0:T(8,128)(2,1)S(1)}, bf16[512,2048]{1,0:T(8,128)(2,1)}, u32[]{:S(2)}) copy-start(bf16[512,2048]{1,0:T(8,128)(2,1)} %refs_1_.3) | copy-start | bytes 6291460
  6.7 2.4 %collective-permute-start.7 = (f32[2,32,512]{2,1,0:T(8,128)S(1)}, f32[2,32,512]{2,1,0:T(8,128)S(1)}, u32[]{:S(2)}, u32[]{:S(2)}) collective-permute-start(f32[2,32,512]{2,1,0:T(8,128)S(1)} %get-tuple-element.46), channel_id=1, source_target_pairs={{0,8},{8,0},{16,24},{24,16},{1,9},{9,1},{17,25},{25,17},{2,10},{10... | collective-permute-start | bytes 393224 | tf_op jit(solution)/shard_map/ppermute | solution.py:17
  6.9 5.9 %collective-permute-start.8 = (f32[2,32,512]{2,1,0:T(8,128)S(1)}, f32[2,32,512]{2,1,0:T(8,128)S(1)}, u32[]{:S(2)}, u32[]{:S(2)}) collective-permute-start(f32[2,32,512]{2,1,0:T(8,128)S(1)} %get-tuple-element.47), channel_id=1, source_target_pairs={{0,8},{8,0},{16,24},{24,16},{1,9},{9,1},{17,25},{25,17},{2,10},{10... | collective-permute-start | bytes 393224 | tf_op jit(solution)/shard_map/ppermute | solution.py:17
  7.3 5.5 %collective-permute-start.9 = (f32[2,32,512]{2,1,0:T(8,128)S(1)}, f32[2,32,512]{2,1,0:T(8,128)S(1)}, u32[]{:S(2)}, u32[]{:S(2)}) collective-permute-start(f32[2,32,512]{2,1,0:T(8,128)S(1)} %get-tuple-element.48), channel_id=1, source_target_pairs={{0,8},{8,0},{16,24},{24,16},{1,9},{9,1},{17,25},{25,17},{2,10},{10... | collective-permute-start | bytes 393224 | tf_op jit(solution)/shard_map/ppermute | solution.py:17
  7.5 1.3 %collective-permute-start.1 = (bf16[2,8,1024]{2,1,0:T(8,128)(2,1)S(1)}, bf16[2,8,1024]{2,1,0:T(8,128)(2,1)S(1)}, u32[]{:S(2)}, u32[]{:S(2)}) collective-permute-start(bf16[2,8,1024]{2,1,0:T(8,128)(2,1)S(1)} %get-tuple-element.37), channel_id=1, source_target_pairs={{0,8},{8,0},{16,24},{24,16},{1,9},{9,1},{17,25},{25,17},{2,10},{10... | collective-permute-start | bytes 98312 | tf_op jit(solution)/shard_map/ppermute | solution.py:17
  8.8 4.8 %collective-permute-start.10 = (f32[2,32,512]{2,1,0:T(8,128)S(1)}, f32[2,32,512]{2,1,0:T(8,128)S(1)}, u32[]{:S(2)}, u32[]{:S(2)}) collective-permute-start(f32[2,32,512]{2,1,0:T(8,128)S(1)} %get-tuple-element.49), channel_id=1, source_target_pairs={{0,8},{8,0},{16,24},{24,16},{1,9},{9,1},{17,25},{25,17},{2,10},{10... | collective-permute-start | bytes 393224 | tf_op jit(solution)/shard_map/ppermute | solution.py:17
  9.1 6.3 %collective-permute-start.4 = (bf16[4,8,1024]{2,1,0:T(8,128)(2,1)S(1)}, bf16[4,8,1024]{2,1,0:T(8,128)(2,1)S(1)}, u32[]{:S(2)}, u32[]{:S(2)}) collective-permute-start(bf16[4,8,1024]{2,1,0:T(8,128)(2,1)S(1)} %shard_map.78.refs_0_), channel_id=1, source_target_pairs={{0,6},{1,7},{2,4},{3,5},{4,2},{5,3},{6,0},{7,1},{8,14},{9,15},{10,... | collective-permute-start | bytes 196616 | tf_op jit(solution)/shard_map/ppermute | solution.py:17
  12.8 5.9 %collective-permute-start.3 = (bf16[4,8,1024]{2,1,0:T(8,128)(2,1)S(1)}, bf16[4,8,1024]{2,1,0:T(8,128)(2,1)S(1)}, u32[]{:S(2)}, u32[]{:S(2)}) collective-permute-start(bf16[4,8,1024]{2,1,0:T(8,128)(2,1)S(1)} %shard_map.78.refs_0_), channel_id=1, source_target_pairs={{0,4},{1,5},{2,6},{3,7},{4,0},{5,1},{6,2},{7,3},{8,12},{9,13},{10,... | collective-permute-start | bytes 196616 | tf_op jit(solution)/shard_map/ppermute | solution.py:17
  12.8 5.9 %collective-permute-start.2 = (bf16[4,8,1024]{2,1,0:T(8,128)(2,1)S(1)}, bf16[4,8,1024]{2,1,0:T(8,128)(2,1)S(1)}, u32[]{:S(2)}, u32[]{:S(2)}) collective-permute-start(bf16[4,8,1024]{2,1,0:T(8,128)(2,1)S(1)} %shard_map.78.refs_0_), channel_id=1, source_target_pairs={{0,2},{1,3},{2,0},{3,1},{4,6},{5,7},{6,4},{7,5},{8,10},{9,11},{10,... | collective-permute-start | bytes 196616 | tf_op jit(solution)/shard_map/ppermute | solution.py:17
  13.8 11.7 %collective-permute-start.12 = (s16[32,2176]{1,0:T(8,128)(2,1)S(1)}, s16[32,2176]{1,0:T(8,128)(2,1)S(1)}, u32[]{:S(2)}, u32[]{:S(2)}) collective-permute-start(s16[32,2176]{1,0:T(8,128)(2,1)S(1)} %get-tuple-element.52), channel_id=1, source_target_pairs={{0,16},{8,24},{16,0},{24,8},{1,17},{9,25},{17,1},{25,9},{2,18},{10... | collective-permute-start | bytes 417800 | tf_op jit(solution)/shard_map/ppermute | solution.py:17
  19.7 8.5 %collective-permute-start.6 = (s16[4,16,2176]{2,1,0:T(8,128)(2,1)S(1)}, s16[4,16,2176]{2,1,0:T(8,128)(2,1)S(1)}, u32[]{:S(2)}, u32[]{:S(2)}) collective-permute-start(s16[4,16,2176]{2,1,0:T(8,128)(2,1)S(1)} %get-tuple-element.43), channel_id=1, source_target_pairs={{0,16},{8,24},{16,0},{24,8},{1,17},{9,25},{17,1},{25,9},{2,18},{10... | collective-permute-start | bytes 835592 | tf_op jit(solution)/shard_map/ppermute | solution.py:17
  20.6 5.0 %collective-permute-start.11 = (bf16[64,1024]{1,0:T(8,128)(2,1)S(1)}, bf16[64,1024]{1,0:T(8,128)(2,1)S(1)}, u32[]{:S(2)}, u32[]{:S(2)}) collective-permute-start(bf16[64,1024]{1,0:T(8,128)(2,1)S(1)} %bitcast.12), channel_id=1, source_target_pairs={{0,1},{1,0},{2,3},{3,2},{4,5},{5,4},{6,7},{7,6},{8,9},{9,8},{10,11... | collective-permute-start | bytes 393224 | tf_op jit(solution)/shard_map/ppermute | solution.py:17
  26.6 7.4 %collective-permute-start.14 = (s16[4,16,2176]{2,1,0:T(8,128)(2,1)S(1)}, s16[4,16,2176]{2,1,0:T(8,128)(2,1)S(1)}, u32[]{:S(2)}, u32[]{:S(2)}) collective-permute-start(s16[4,16,2176]{2,1,0:T(8,128)(2,1)S(1)} %shard_map.84), channel_id=1, source_target_pairs={{0,16},{8,24},{16,0},{24,8},{1,17},{9,25},{17,1},{25,9},{2,18},{10... | collective-permute-start | bytes 835592 | tf_op jit(solution)/shard_map/ppermute | solution.py:17
  28.1 5.0 %collective-permute-start.13 = (bf16[64,1024]{1,0:T(8,128)(2,1)S(1)}, bf16[64,1024]{1,0:T(8,128)(2,1)S(1)}, u32[]{:S(2)}, u32[]{:S(2)}) collective-permute-start(bf16[64,1024]{1,0:T(8,128)(2,1)S(1)} %bitcast.10), channel_id=1, source_target_pairs={{0,1},{1,0},{2,3},{3,2},{4,5},{5,4},{6,7},{7,6},{8,9},{9,8},{10,11... | collective-permute-start | bytes 393224 | tf_op jit(solution)/shard_map/ppermute | solution.py:17
  30.1 13.3 %copy-start.4 = (s32[32]{0:T(128)S(1)}, s32[32]{0:T(128)}, u32[]{:S(2)}) copy-start(s32[32]{0:T(128)} %param.9) | copy-start | bytes 388
  34.4 3.8 %collective-permute-start.15 = (f32[32,128]{1,0:T(8,128)S(1)}, f32[32,128]{1,0:T(8,128)S(1)}, u32[]{:S(2)}, u32[]{:S(2)}) collective-permute-start(f32[32,128]{1,0:T(8,128)S(1)} %get-tuple-element.61.one_ref), channel_id=1, source_target_pairs={{0,1},{1,0},{2,3},{3,2},{4,5},{5,4},{6,7},{7,6},{8,9},{9,8},{10,11... | collective-permute-start | bytes 49160 | tf_op jit(solution)/shard_map/ppermute | solution.py:17
  38.4 3.8 %collective-permute-start.16 = (f32[32,128]{1,0:T(8,128)S(1)}, f32[32,128]{1,0:T(8,128)S(1)}, u32[]{:S(2)}, u32[]{:S(2)}) collective-permute-start(f32[32,128]{1,0:T(8,128)S(1)} %shard_map.86.one_ref), channel_id=1, source_target_pairs={{0,2},{1,3},{2,0},{3,1},{4,6},{5,7},{6,4},{7,5},{8,10},{9,11},{10,... | collective-permute-start | bytes 49160 | tf_op jit(solution)/shard_map/ppermute | solution.py:17
  42.3 4.7 %collective-permute-start.17 = (f32[32,128]{1,0:T(8,128)S(1)}, f32[32,128]{1,0:T(8,128)S(1)}, u32[]{:S(2)}, u32[]{:S(2)}) collective-permute-start(f32[32,128]{1,0:T(8,128)S(1)} %shard_map.87.one_ref), channel_id=1, source_target_pairs={{0,4},{1,5},{2,6},{3,7},{4,0},{5,1},{6,2},{7,3},{8,12},{9,13},{10,... | collective-permute-start | bytes 49160 | tf_op jit(solution)/shard_map/ppermute | solution.py:17
  43.4 3.7 %collective-permute-start.18 = (s32[32]{0:T(128)S(1)}, s32[32]{0:T(128)S(1)}, u32[]{:S(2)}, u32[]{:S(2)}) collective-permute-start(s32[32]{0:T(128)S(1)} %copy-done.4), channel_id=1, source_target_pairs={{0,8},{8,0},{16,24},{24,16},{1,9},{9,1},{17,25},{25,17},{2,10},{10... | collective-permute-start | bytes 392 | tf_op jit(solution)/shard_map/ppermute | solution.py:17
  48.2 5.0 %collective-permute-start.20 = (bf16[32,2048]{1,0:T(8,128)(2,1)S(1)}, bf16[32,2048]{1,0:T(8,128)(2,1)S(1)}, u32[]{:S(2)}, u32[]{:S(2)}) collective-permute-start(bf16[32,2048]{1,0:T(8,128)(2,1)S(1)} %get-tuple-element.62.refs_0_), channel_id=1, source_target_pairs={{0,16},{8,24},{16,0},{24,8},{1,17},{9,25},{17,1},{25,9},{2,18},{10... | collective-permute-start | bytes 393224 | tf_op jit(solution)/shard_map/ppermute | solution.py:17
  49.2 5.4 %collective-permute-start.19 = (bf16[32,2048]{1,0:T(8,128)(2,1)S(1)}, bf16[32,2048]{1,0:T(8,128)(2,1)S(1)}, u32[]{:S(2)}, u32[]{:S(2)}) collective-permute-start(bf16[32,2048]{1,0:T(8,128)(2,1)S(1)} %get-tuple-element.62.refs_0_), channel_id=1, source_target_pairs={{0,8},{8,0},{16,24},{24,16},{1,9},{9,1},{17,25},{25,17},{2,10},{10... | collective-permute-start | bytes 393224 | tf_op jit(solution)/shard_map/ppermute | solution.py:17
  53.2 1.4 %collective-permute-start.21 = (bf16[32,2048]{1,0:T(8,128)(2,1)S(1)}, bf16[32,2048]{1,0:T(8,128)(2,1)S(1)}, u32[]{:S(2)}, u32[]{:S(2)}) collective-permute-start(bf16[32,2048]{1,0:T(8,128)(2,1)S(1)} %collective-permute-done.20.refs_2_), channel_id=1, source_target_pairs={{0,8},{8,0},{16,24},{24,16},{1,9},{9,1},{17,25},{25,17},{2,10},{10... | collective-permute-start | bytes 393224 | tf_op jit(solution)/shard_map/ppermute | solution.py:17
  53.2 1.4 %collective-permute-start.22 = (f32[24,128]{1,0:T(8,128)S(1)}, f32[24,128]{1,0:T(8,128)S(1)}, u32[]{:S(2)}, u32[]{:S(2)}) collective-permute-start(f32[24,128]{1,0:T(8,128)S(1)} %get-tuple-element.63.refs_4_), channel_id=1, source_target_pairs={{0,8},{8,0},{16,24},{24,16},{1,9},{9,1},{17,25},{25,17},{2,10},{10... | collective-permute-start | bytes 36872 | tf_op jit(solution)/shard_map/ppermute | solution.py:17

commit v7 on v6

--- a/solution.py
+++ b/solution.py
@@ -145,37 +145,51 @@
     encode(own_ref[1 - x] + jnp.concatenate([ref[1 - x] for ref in sib_refs], axis=1), give_ref, ())
 
 
-def stats_body(part, kept_ref, came_ref, student_ref, far_ref, *refs):
-    logits_ref, student_out_ref, stats_ref = refs[-3:]
+def stats_body(part, kept_ref, came_ref, *refs):
+    if part == 0:
+        student_ref, far_ref, weight_ref, student_out_ref, stats_ref, tops_ref, logits_ref = refs
+    else:
+        first_stats_ref, first_tops_ref, weight_ref, stats_ref, tops_ref, logits_ref = refs
     side = lax.axis_index("vocab") % 2
     teachers, rows, _ = logits_ref.shape
-    for i in range(teachers):
-        logits_ref[i] = kept_ref[i] + decode(came_ref[i])
     lane = lax.broadcasted_iota(jnp.int32, (rows, LANES), 1)
     lse = jnp.zeros((rows, LANES), jnp.float32)
     mean = jnp.zeros((rows, LANES), jnp.float32)
-    tops = [jnp.max(logits_ref[i], axis=1, keepdims=True) for i in range(teachers)]
+    peak = jnp.zeros((rows, LANES), jnp.float32)
+    tops = []
     for i in range(teachers):
-        weight = jnp.exp(logits_ref[i] - tops[i])
+        value = kept_ref[i] + decode(came_ref[i])
+        tops.append(jnp.max(value, axis=1, keepdims=True))
+        logits_ref[i] = value - tops[i]
+    for i in range(teachers):
+        weight = jnp.exp(logits_ref[i])
+        weight_ref[i] = weight
         total = jnp.sum(weight, axis=1, keepdims=True)
         group = (lane >= i * teachers) & (lane < (i + 1) * teachers)
         lse = jnp.where(group, tops[i] + jnp.log(total), lse)
+        peak = jnp.where(group, tops[i], peak)
         for j in range(teachers):
-            local = jnp.sum(weight * (logits_ref[j] - tops[j]), axis=1, keepdims=True) / total + tops[j]
+            local = jnp.sum(weight * logits_ref[j], axis=1, keepdims=True) / total + tops[j]
             mean = jnp.where(lane == LANES // 2 + i * teachers + j, local, mean)
-    place = side if part == 0 else 1 - side
-    span = pl.ds(pl.multiple_of(place * rows, rows), rows)
-    value = student_ref[span] + decode(far_ref[span])
-    student_out_ref[...] = value
-    top = jnp.max(value, axis=1, keepdims=True)
-    total = jnp.sum(jnp.exp(value - top), axis=1, keepdims=True)
-    lse = jnp.where(lane == teachers * teachers, top + jnp.log(total), lse)
     value = jnp.where(lane < LANES // 2, lse, mean)
+    student_lane = lane == teachers * teachers
+    own = pl.ds(pl.multiple_of(side * rows, rows), rows)
+    other = pl.ds(pl.multiple_of((1 - side) * rows, rows), rows)
     if part == 0:
-        stats_ref[...] = value
+        student = student_ref[...] + decode(far_ref[...])
+        top = jnp.max(student, axis=1, keepdims=True)
+        weight = jnp.exp(student - top)
+        student_out_ref[...] = weight
+        wide = jnp.broadcast_to(top + jnp.log(jnp.sum(weight, axis=1, keepdims=True)), stats_ref.shape)
+        stats_ref[...] = wide
+        tops_ref[...] = jnp.broadcast_to(top, tops_ref.shape)
+        stats_ref[own] = jnp.where(student_lane, stats_ref[own], value)
+        tops_ref[own] = jnp.where(student_lane, tops_ref[own], peak)
     else:
-        stats_ref[pl.ds(pl.multiple_of(side * rows, rows), rows)] = refs[0][...]
-        stats_ref[span] = value
+        stats_ref[own] = first_stats_ref[own]
+        tops_ref[own] = first_tops_ref[own]
+        stats_ref[other] = jnp.where(student_lane, first_stats_ref[other], value)
+        tops_ref[other] = jnp.where(student_lane, first_tops_ref[other], peak)
 
 
 def merge_body(one_ref, two_ref, out_ref):
@@ -191,7 +205,7 @@
 
 
 def residual_body(
-    own_ref, other_ref, student_ref, other_student_ref, stats_ref, label_ref, sib_label_ref, small_ref, residual_ref, weight_ref
+    own_ref, other_ref, student_ref, tops_ref, stats_ref, label_ref, sib_label_ref, small_ref, residual_ref, weight_ref, scale_ref
 ):
     side = lax.axis_index("vocab") % 2
     core = lax.axis_index("teacher") % 2
@@ -227,20 +241,20 @@
     label = jnp.where(hit, jnp.where(mine, label_ref[...], sib_label_ref[...]), 0)
     label = jnp.sum(label, axis=1, keepdims=True) - lax.axis_index("vocab") * width
     label_at = lambda place: jnp.where(place == 0, label[:group], label[group:])
-    for part, (logits_ref, value_ref) in enumerate(((own_ref, student_ref), (other_ref, other_student_ref))):
+    scale = jnp.where(lane <= at, jnp.exp(jnp.minimum(tops_ref[...] - stats_ref[...], 0.0)), 0.0)
+    scale_ref[...] = scale
+    for part, exp_ref in enumerate((own_ref, other_ref)):
         place = side if part == 0 else 1 - side
         span = pl.ds(pl.multiple_of(place * group, group), group)
-        norms = stats_ref[span]
+        scales = scale_ref[span]
         weights = weight_ref[span]
         target = jnp.where(
             lax.broadcasted_iota(jnp.int32, (group, width), 1) == label_at(place), HARD_SHARE, 0.0
         )
         for i in range(teachers):
-            norm = norms[:, i * teachers : i * teachers + 1]
-            log_prob = (logits_ref[i] - norm).astype(jnp.bfloat16).astype(jnp.float32)
-            prob = jnp.exp(log_prob).astype(jnp.bfloat16).astype(jnp.float32)
-            target = target + ((1.0 - HARD_SHARE) / teachers * weights[:, at + i : at + i + 1]) * prob
-        prob = jnp.exp(value_ref[...] - norms[:, at : at + 1])
+            share = (1.0 - HARD_SHARE) / teachers * weights[:, at + i : at + i + 1]
+            target = target + share * scales[:, i * teachers : i * teachers + 1] * exp_ref[i]
+        prob = student_ref[span] * scales[:, at : at + 1]
         residual_ref[span] = (prob - target).astype(jnp.bfloat16)
 
 
@@ -380,14 +394,16 @@
     other_far = swap(other_sent, "teacher", 2)
     (other_kept,) = partial((flat,), other_stay)
 
-    outs = (flat, shape((group, width), f32))
-    logits, mine, first = local(
-        functools.partial(stats_body, 0), (*outs, shape((group, LANES), f32)), (kept, far, student, student_far)
-    )
-    other_logits, others, stats = local(
-        functools.partial(stats_body, 1),
-        (*outs, shape((block, LANES), f32)),
-        (other_kept, other_far, student, student_far, first),
+    lists = (shape((block, LANES), f32),) * 2
+    scratch = [pltpu.VMEM(flat.shape, f32)]
+    weights, student_weights, *firsts = local(
+        functools.partial(stats_body, 0),
+        (flat, shape((block, width), f32), *lists),
+        (kept, far, student, student_far),
+        scratch=scratch,
+    )
+    other_weights, stats, tops = local(
+        functools.partial(stats_body, 1), (flat, *lists), (other_kept, other_far, *firsts), scratch=scratch
     )
     mask = 1
     while mask < shards:
@@ -398,8 +414,8 @@
     small, residual = local(
         residual_body,
         (shape((-(-entries // 8) * 8, LANES), f32), shape((block, width), jnp.bfloat16)),
-        (logits, other_logits, mine, others, stats, labels.reshape(1, block), sib_labels.reshape(1, block)),
-        scratch=[pltpu.VMEM((block, LANES), f32)],
+        (weights, other_weights, student_weights, tops, stats, labels.reshape(1, block), sib_labels.reshape(1, block)),
+        scratch=[pltpu.VMEM((block, LANES), f32)] * 2,
     )
     sib_small = swap(small, "teacher", 1)
     sib_residual = swap(residual, "teacher", 1)

time: 57.2 us -> 56.8 us (level)
  no operation moved by 1% of the time
where the time goes in v7:
time: 56.8 us; the launch traced here: 56.7 us
  waiting for transfers between devices  25.2 us (44%)
  starting transfers between devices  20.2 us (36%)
  Pallas kernels  7.98 us (14%)
  local copies, waits for them, and re-layouts  2.51 us (4%)
  between operations  0.79 us (1%)
    ppermute x23, waiting for transfers between devices, swap(): return lax.ppermute(value, axis, [(i, i ^ mask) for i in range(count)])  25.2 us
    ppermute x23, starting transfers between devices, swap(): return lax.ppermute(value, axis, [(i, i ^ mask) for i in range(count)])  20.2 us
    pallas_call x15, Pallas kernels, call(): pl.pallas_call(body, out_shape=outs, scratch_shapes=list(scratch), compil...  7.98 us
    unnamed x10, local copies, waits for them, and re-layouts  2.51 us
  transfers between devices with their start and end apart: 23, of which 11 were waited for; matrix products, arithmetic and copies ran while one was open for 0% of the time, Pallas kernels for 7%

profile of v7, /device:TPU:0, one launch (start us, length us, event | category | flops | bytes accessed | tf_op | source)
XLA Modules:
  0.0 56.7 jit_solution(3362996599964695734)
XLA Ops:
  0.6 0.5 collective-permute-start.5
  1.1 2.6 %collective-permute-start = (bf16[16,2048]{1,0:T(8,128)(2,1)}, bf16[16,2048]{1,0:T(8,128)(2,1)S(1)}, u32[]{:S(2)}, u32[]{:S(2)}) collective-permute-start(bf16[16,2048]{1,0:T(8,128)(2,1)} %bitcast.13), channel_id=1, source_target_pairs={{0,16},{8,24},{16,0},{24,8},{1,17},{9,25},{17,1},{25,9},{2,18},{10... | collective-permute-start | bytes 196616 | tf_op jit(solution)/shard_map/ppermute | solution.py:17
  3.7 1.6 %copy-done.1 = bf16[512,2048]{1,0:T(8,128)(2,1)S(1)} copy-done((bf16[512,2048]{1,0:T(8,128)(2,1)S(1)}, bf16[512,2048]{1,0:T(8,128)(2,1)}, u32[]{:S(2)}) %copy-start.1) | copy-done | bytes 2097176
  5.3 0.9 %copy-done.2 = bf16[128,512]{1,0:T(8,128)(2,1)S(1)} copy-done((bf16[128,512]{1,0:T(8,128)(2,1)S(1)}, bf16[128,512]{1,0:T(8,128)(2,1)}, u32[]{:S(2)}) %copy-start.2) | copy-done | bytes 131096
  6.2 0.5 shard_map.76
  6.7 0.0 copy-start
  6.7 0.2 collective-permute-start.7
  6.9 0.3 collective-permute-start.8
  7.3 0.2 collective-permute-start.9
  7.4 0.1 shard_map.77
  7.5 0.4 collective-permute-start.1
  7.9 0.9 %collective-permute-done.1.sib_ref = bf16[2,8,1024]{2,1,0:T(8,128)(2,1)S(1)} collective-permute-done((bf16[2,8,1024]{2,1,0:T(8,128)(2,1)S(1)}, bf16[2,8,1024]{2,1,0:T(8,128)(2,1)S(1)}, u32[]{:S(2)}, u32[]{:S(2)}) %collective-permute-start.1) | collective-permute-done | bytes 32800 | tf_op jit(solution)/shard_map/ppermute | solution.py:17
  8.8 0.3 collective-permute-start.10
  9.1 3.7 %collective-permute-start.4 = (bf16[4,8,1024]{2,1,0:T(8,128)(2,1)S(1)}, bf16[4,8,1024]{2,1,0:T(8,128)(2,1)S(1)}, u32[]{:S(2)}, u32[]{:S(2)}) collective-permute-start(bf16[4,8,1024]{2,1,0:T(8,128)(2,1)S(1)} %shard_map.78.refs_0_), channel_id=1, source_target_pairs={{0,6},{1,7},{2,4},{3,5},{4,2},{5,3},{6,0},{7,1},{8,14},{9,15},{10,... | collective-permute-start | bytes 196616 | tf_op jit(solution)/shard_map/ppermute | solution.py:17
  12.8 0.8 %collective-permute-start.2 = (bf16[4,8,1024]{2,1,0:T(8,128)(2,1)S(1)}, bf16[4,8,1024]{2,1,0:T(8,128)(2,1)S(1)}, u32[]{:S(2)}, u32[]{:S(2)}) collective-permute-start(bf16[4,8,1024]{2,1,0:T(8,128)(2,1)S(1)} %shard_map.78.refs_0_), channel_id=1, source_target_pairs={{0,2},{1,3},{2,0},{3,1},{4,6},{5,7},{6,4},{7,5},{8,10},{9,11},{10,... | collective-permute-start | bytes 196616 | tf_op jit(solution)/shard_map/ppermute | solution.py:17
  13.6 0.2 shard_map.81
  13.8 0.8 %collective-permute-start.12 = (s16[32,2176]{1,0:T(8,128)(2,1)S(1)}, s16[32,2176]{1,0:T(8,128)(2,1)S(1)}, u32[]{:S(2)}, u32[]{:S(2)}) collective-permute-start(s16[32,2176]{1,0:T(8,128)(2,1)S(1)} %get-tuple-element.53), channel_id=1, source_target_pairs={{0,16},{8,24},{16,0},{24,8},{1,17},{9,25},{17,1},{25,9},{2,18},{10... | collective-permute-start | bytes 417800 | tf_op jit(solution)/shard_map/ppermute | solution.py:17
  14.6 0.9 %collective-permute-done.4.refs_3_ = bf16[4,8,1024]{2,1,0:T(8,128)(2,1)S(1)} collective-permute-done((bf16[4,8,1024]{2,1,0:T(8,128)(2,1)S(1)}, bf16[4,8,1024]{2,1,0:T(8,128)(2,1)S(1)}, u32[]{:S(2)}, u32[]{:S(2)}) %collective-permute-start.4) | collective-permute-done | bytes 65568 | tf_op jit(solution)/shard_map/ppermute | solution.py:17
  15.5 3.2 %collective-permute-done.3.refs_2_ = bf16[4,8,1024]{2,1,0:T(8,128)(2,1)S(1)} collective-permute-done((bf16[4,8,1024]{2,1,0:T(8,128)(2,1)S(1)}, bf16[4,8,1024]{2,1,0:T(8,128)(2,1)S(1)}, u32[]{:S(2)}, u32[]{:S(2)}) %collective-permute-start.3) | collective-permute-done | bytes 65568 | tf_op jit(solution)/shard_map/ppermute | solution.py:17
  18.7 0.1 shard_map.79
  18.8 0.9 %shard_map.80 = (s16[4,16,2176]{2,1,0:T(8,128)(2,1)S(1)}, f32[4,16,2048]{2,1,0:T(8,128)S(1)}) custom-call(bf16[64,1024]{1,0:T(8,128)(2,1)S(1)} %bitcast.11, bf16[64,1024]{1,0:T(8,128)(2,1)S(1)} %bitcast.9, bf16[512,2048]{1,0:T(8,128)(2,1)S(1)} %copy-done, bf16[512,2048]{1,0:T(8,128)(2,1)S(1)} %collective-permute-done.5.refs_3_.refs_0_.refs_2_), custom_call_target="tpu_custom_call" | custom-call | flops 1 | bytes 1 | tf_op jit(solution)/shard_map/pallas_call | solution.py:21
  19.7 0.9 %collective-permute-start.6 = (s16[4,16,2176]{2,1,0:T(8,128)(2,1)S(1)}, s16[4,16,2176]{2,1,0:T(8,128)(2,1)S(1)}, u32[]{:S(2)}, u32[]{:S(2)}) collective-permute-start(s16[4,16,2176]{2,1,0:T(8,128)(2,1)S(1)} %get-tuple-element.44), channel_id=1, source_target_pairs={{0,16},{8,24},{16,0},{24,8},{1,17},{9,25},{17,1},{25,9},{2,18},{10... | collective-permute-start | bytes 835592 | tf_op jit(solution)/shard_map/ppermute | solution.py:17
  20.6 1.5 %collective-permute-start.11 = (bf16[64,1024]{1,0:T(8,128)(2,1)S(1)}, bf16[64,1024]{1,0:T(8,128)(2,1)S(1)}, u32[]{:S(2)}, u32[]{:S(2)}) collective-permute-start(bf16[64,1024]{1,0:T(8,128)(2,1)S(1)} %bitcast.12), channel_id=1, source_target_pairs={{0,1},{1,0},{2,3},{3,2},{4,5},{5,4},{6,7},{7,6},{8,9},{9,8},{10,11... | collective-permute-start | bytes 393224 | tf_op jit(solution)/shard_map/ppermute | solution.py:17
  22.1 3.5 %collective-permute-done.11.refs_0_ = bf16[64,1024]{1,0:T(8,128)(2,1)S(1)} collective-permute-done((bf16[64,1024]{1,0:T(8,128)(2,1)S(1)}, bf16[64,1024]{1,0:T(8,128)(2,1)S(1)}, u32[]{:S(2)}, u32[]{:S(2)}) %collective-permute-start.11) | collective-permute-done | bytes 131104 | tf_op jit(solution)/shard_map/ppermute | solution.py:17
  25.5 1.0 %shard_map.84 = s16[4,16,2176]{2,1,0:T(8,128)(2,1)S(1)} custom-call(bf16[64,1024]{1,0:T(8,128)(2,1)S(1)} %collective-permute-done.11.refs_0_, bf16[512,2048]{1,0:T(8,128)(2,1)S(1)} %copy-done, bf16[512,2048]{1,0:T(8,128)(2,1)S(1)} %collective-permute-done.5.refs_3_.refs_0_.refs_2_), custom_call_target="tpu_custom_call" | custom-call | flops 1 | bytes 1 | tf_op jit(solution)/shard_map/pallas_call | solution.py:21
  26.6 1.3 %collective-permute-start.14 = (s16[4,16,2176]{2,1,0:T(8,128)(2,1)S(1)}, s16[4,16,2176]{2,1,0:T(8,128)(2,1)S(1)}, u32[]{:S(2)}, u32[]{:S(2)}) collective-permute-start(s16[4,16,2176]{2,1,0:T(8,128)(2,1)S(1)} %shard_map.84), channel_id=1, source_target_pairs={{0,16},{8,24},{16,0},{24,8},{1,17},{9,25},{17,1},{25,9},{2,18},{10... | collective-permute-start | bytes 835592 | tf_op jit(solution)/shard_map/ppermute | solution.py:17
  27.8 0.3 collective-permute-done.6.came_ref
  28.1 1.5 %collective-permute-start.13 = (bf16[64,1024]{1,0:T(8,128)(2,1)S(1)}, bf16[64,1024]{1,0:T(8,128)(2,1)S(1)}, u32[]{:S(2)}, u32[]{:S(2)}) collective-permute-start(bf16[64,1024]{1,0:T(8,128)(2,1)S(1)} %bitcast.10), channel_id=1, source_target_pairs={{0,1},{1,0},{2,3},{3,2},{4,5},{5,4},{6,7},{7,6},{8,9},{9,8},{10,11... | collective-permute-start | bytes 393224 | tf_op jit(solution)/shard_map/ppermute | solution.py:17
  29.7 0.5 shard_map.82
  30.2 2.9 %collective-permute-done.13.refs_0_ = bf16[64,1024]{1,0:T(8,128)(2,1)S(1)} collective-permute-done((bf16[64,1024]{1,0:T(8,128)(2,1)S(1)}, bf16[64,1024]{1,0:T(8,128)(2,1)S(1)}, u32[]{:S(2)}, u32[]{:S(2)}) %collective-permute-start.13) | collective-permute-done | bytes 131104 | tf_op jit(solution)/shard_map/ppermute | solution.py:17
  33.1 0.8 %shard_map.83.kept_ref = f32[4,16,2048]{2,1,0:T(8,128)S(1)} custom-call(bf16[64,1024]{1,0:T(8,128)(2,1)S(1)} %collective-permute-done.13.refs_0_, bf16[512,2048]{1,0:T(8,128)(2,1)S(1)} %copy-done, bf16[512,2048]{1,0:T(8,128)(2,1)S(1)} %collective-permute-done.5.refs_3_.refs_0_.refs_2_), custom_call_target="tpu_custom_call" | custom-call | flops 1 | bytes 1 | tf_op jit(solution)/shard_map/pallas_call | solution.py:21
  33.9 0.0 collective-permute-done.14.came_ref
  34.0 0.5 shard_map.85
  34.5 1.6 %collective-permute-start.15 = (f32[32,128]{1,0:T(8,128)S(1)}, f32[32,128]{1,0:T(8,128)S(1)}, u32[]{:S(2)}, u32[]{:S(2)}) collective-permute-start(f32[32,128]{1,0:T(8,128)S(1)} %get-tuple-element.63.one_ref), channel_id=1, source_target_pairs={{0,1},{1,0},{2,3},{3,2},{4,5},{5,4},{6,7},{7,6},{8,9},{9,8},{10,11... | collective-permute-start | bytes 49160 | tf_op jit(solution)/shard_map/ppermute | solution.py:17
  36.0 2.2 %collective-permute-done.15.two_ref = f32[32,128]{1,0:T(8,128)S(1)} collective-permute-done((f32[32,128]{1,0:T(8,128)S(1)}, f32[32,128]{1,0:T(8,128)S(1)}, u32[]{:S(2)}, u32[]{:S(2)}) %collective-permute-start.15) | collective-permute-done | bytes 16416 | tf_op jit(solution)/shard_map/ppermute | solution.py:17
  38.3 0.1 shard_map.86.one_ref
  38.4 0.9 %collective-permute-start.16 = (f32[32,128]{1,0:T(8,128)S(1)}, f32[32,128]{1,0:T(8,128)S(1)}, u32[]{:S(2)}, u32[]{:S(2)}) collective-permute-start(f32[32,128]{1,0:T(8,128)S(1)} %shard_map.86.one_ref), channel_id=1, source_target_pairs={{0,2},{1,3},{2,0},{3,1},{4,6},{5,7},{6,4},{7,5},{8,10},{9,11},{10,... | collective-permute-start | bytes 49160 | tf_op jit(solution)/shard_map/ppermute | solution.py:17
  39.3 2.9 %collective-permute-done.16.two_ref = f32[32,128]{1,0:T(8,128)S(1)} collective-permute-done((f32[32,128]{1,0:T(8,128)S(1)}, f32[32,128]{1,0:T(8,128)S(1)}, u32[]{:S(2)}, u32[]{:S(2)}) %collective-permute-start.16) | collective-permute-done | bytes 16416 | tf_op jit(solution)/shard_map/ppermute | solution.py:17
  42.2 0.1 shard_map.87.one_ref
  42.3 1.1 %collective-permute-start.17 = (f32[32,128]{1,0:T(8,128)S(1)}, f32[32,128]{1,0:T(8,128)S(1)}, u32[]{:S(2)}, u32[]{:S(2)}) collective-permute-start(f32[32,128]{1,0:T(8,128)S(1)} %shard_map.87.one_ref), channel_id=1, source_target_pairs={{0,4},{1,5},{2,6},{3,7},{4,0},{5,1},{6,2},{7,3},{8,12},{9,13},{10,... | collective-permute-start | bytes 49160 | tf_op jit(solution)/shard_map/ppermute | solution.py:17
  43.4 3.6 %collective-permute-done.17.two_ref = f32[32,128]{1,0:T(8,128)S(1)} collective-permute-done((f32[32,128]{1,0:T(8,128)S(1)}, f32[32,128]{1,0:T(8,128)S(1)}, u32[]{:S(2)}, u32[]{:S(2)}) %collective-permute-start.17) | collective-permute-done | bytes 16416 | tf_op jit(solution)/shard_map/ppermute | solution.py:17
  47.0 0.1 shard_map.88.stats_ref
  47.1 0.8 %shard_map.89 = (f32[24,128]{1,0:T(8,128)S(1)}, bf16[32,2048]{1,0:T(8,128)(2,1)S(1)}) custom-call(f32[4,16,2048]{2,1,0:T(8,128)S(1)} %get-tuple-element.55.own_ref, f32[4,16,2048]{2,1,0:T(8,128)S(1)} %get-tuple-element.60.other_ref, f32[32,2048]{1,0:T(8,128)S(1)} %get-tuple-element.61.student_ref, f32[32,128]{1,0:T(8,128)S(1)} %get-tuple-element.62.tops_ref, ...), custom_call_target="tpu_custom_call" | custom-call | flops 1 | bytes 1 | tf_op jit(solution)/shard_map/pallas_call | solution.py:21
  47.9 1.1 %collective-permute-start.20 = (bf16[32,2048]{1,0:T(8,128)(2,1)S(1)}, bf16[32,2048]{1,0:T(8,128)(2,1)S(1)}, u32[]{:S(2)}, u32[]{:S(2)}) collective-permute-start(bf16[32,2048]{1,0:T(8,128)(2,1)S(1)} %get-tuple-element.64.refs_0_), channel_id=1, source_target_pairs={{0,16},{8,24},{16,0},{24,8},{1,17},{9,25},{17,1},{25,9},{2,18},{10... | collective-permute-start | bytes 393224 | tf_op jit(solution)/shard_map/ppermute | solution.py:17
  48.9 4.0 %collective-permute-done.20.refs_2_ = bf16[32,2048]{1,0:T(8,128)(2,1)S(1)} collective-permute-done((bf16[32,2048]{1,0:T(8,128)(2,1)S(1)}, bf16[32,2048]{1,0:T(8,128)(2,1)S(1)}, u32[]{:S(2)}, u32[]{:S(2)}) %collective-permute-start.20) | collective-permute-done | bytes 131104 | tf_op jit(solution)/shard_map/ppermute | solution.py:17
  52.9 0.5 collective-permute-start.22
  53.4 0.9 %collective-permute-done.22.refs_5_ = f32[24,128]{1,0:T(8,128)S(1)} collective-permute-done((f32[24,128]{1,0:T(8,128)S(1)}, f32[24,128]{1,0:T(8,128)S(1)}, u32[]{:S(2)}, u32[]{:S(2)}) %collective-permute-start.22) | collective-permute-done | bytes 12320 | tf_op jit(solution)/shard_map/ppermute | solution.py:17
  54.3 2.4 %shard_map.90 = (f32[512,2048]{1,0:T(8,128)}, f32[16,32]{1,0:T(8,128)}, f32[4,32]{1,0:T(4,128)}) custom-call(bf16[512,128]{1,0:T(8,128)(2,1)S(1)} %get-tuple-element.36.hidden_ref, bf16[32,2048]{1,0:T(8,128)(2,1)S(1)} %get-tuple-element.64.refs_0_, bf16[32,2048]{1,0:T(8,128)(2,1)S(1)} %collective-permute-done.19.refs_1_, ...), custom_call_target="tpu_custom_call" | custom-call | flops 1 | bytes 1 | tf_op jit(solution)/shard_map/pallas_call | solution.py:21
  (23 shorter events, 0.1 us)
Async XLA Ops:
  0.6 13.0 %collective-permute-start.5 = (bf16[512,2048]{1,0:T(8,128)(2,1)}, bf16[512,2048]{1,0:T(8,128)(2,1)S(1)}, u32[]{:S(2)}, u32[]{:S(2)}) collective-permute-start(bf16[512,2048]{1,0:T(8,128)(2,1)} %refs_1_.3), channel_id=1, source_target_pairs={{0,8},{8,0},{16,24},{24,16},{1,9},{9,1},{17,25},{25,17},{2,10},{10... | collective-permute-start | bytes 6291464 | tf_op jit(solution)/shard_map/ppermute | solution.py:17
  1.1 6.3 %collective-permute-start = (bf16[16,2048]{1,0:T(8,128)(2,1)}, bf16[16,2048]{1,0:T(8,128)(2,1)S(1)}, u32[]{:S(2)}, u32[]{:S(2)}) collective-permute-start(bf16[16,2048]{1,0:T(8,128)(2,1)} %bitcast.13), channel_id=1, source_target_pairs={{0,16},{8,24},{16,0},{24,8},{1,17},{9,25},{17,1},{25,9},{2,18},{10... | collective-permute-start | bytes 196616 | tf_op jit(solution)/shard_map/ppermute | solution.py:17
  3.7 1.6 %copy-start.1 = (bf16[512,2048]{1,0:T(8,128)(2,1)S(1)}, bf16[512,2048]{1,0:T(8,128)(2,1)}, u32[]{:S(2)}) copy-start(bf16[512,2048]{1,0:T(8,128)(2,1)} %head_ref.1) | copy-start | bytes 6291460
  5.3 0.9 %copy-start.2 = (bf16[128,512]{1,0:T(8,128)(2,1)S(1)}, bf16[128,512]{1,0:T(8,128)(2,1)}, u32[]{:S(2)}) copy-start(bf16[128,512]{1,0:T(8,128)(2,1)} %hidden_ref.1) | copy-start | bytes 393220
  6.2 1.2 %copy-start.3 = (bf16[1,16,2048]{2,1,0:T(8,128)(2,1)S(1)}, bf16[1,16,2048]{2,1,0:T(8,128)(2,1)}, u32[]{:S(2)}) copy-start(bf16[1,16,2048]{2,1,0:T(8,128)(2,1)} %param.5) | copy-start | bytes 196612
  6.7 12.1 %copy-start = (bf16[512,2048]{1,0:T(8,128)(2,1)S(1)}, bf16[512,2048]{1,0:T(8,128)(2,1)}, u32[]{:S(2)}) copy-start(bf16[512,2048]{1,0:T(8,128)(2,1)} %refs_1_.3) | copy-start | bytes 6291460
  6.7 2.4 %collective-permute-start.7 = (f32[2,32,512]{2,1,0:T(8,128)S(1)}, f32[2,32,512]{2,1,0:T(8,128)S(1)}, u32[]{:S(2)}, u32[]{:S(2)}) collective-permute-start(f32[2,32,512]{2,1,0:T(8,128)S(1)} %get-tuple-element.47), channel_id=1, source_target_pairs={{0,8},{8,0},{16,24},{24,16},{1,9},{9,1},{17,25},{25,17},{2,10},{10... | collective-permute-start | bytes 393224 | tf_op jit(solution)/shard_map/ppermute | solution.py:17
  6.9 5.9 %collective-permute-start.8 = (f32[2,32,512]{2,1,0:T(8,128)S(1)}, f32[2,32,512]{2,1,0:T(8,128)S(1)}, u32[]{:S(2)}, u32[]{:S(2)}) collective-permute-start(f32[2,32,512]{2,1,0:T(8,128)S(1)} %get-tuple-element.48), channel_id=1, source_target_pairs={{0,8},{8,0},{16,24},{24,16},{1,9},{9,1},{17,25},{25,17},{2,10},{10... | collective-permute-start | bytes 393224 | tf_op jit(solution)/shard_map/ppermute | solution.py:17
  7.3 5.5 %collective-permute-start.9 = (f32[2,32,512]{2,1,0:T(8,128)S(1)}, f32[2,32,512]{2,1,0:T(8,128)S(1)}, u32[]{:S(2)}, u32[]{:S(2)}) collective-permute-start(f32[2,32,512]{2,1,0:T(8,128)S(1)} %get-tuple-element.49), channel_id=1, source_target_pairs={{0,8},{8,0},{16,24},{24,16},{1,9},{9,1},{17,25},{25,17},{2,10},{10... | collective-permute-start | bytes 393224 | tf_op jit(solution)/shard_map/ppermute | solution.py:17
  7.5 1.3 %collective-permute-start.1 = (bf16[2,8,1024]{2,1,0:T(8,128)(2,1)S(1)}, bf16[2,8,1024]{2,1,0:T(8,128)(2,1)S(1)}, u32[]{:S(2)}, u32[]{:S(2)}) collective-permute-start(bf16[2,8,1024]{2,1,0:T(8,128)(2,1)S(1)} %get-tuple-element.38), channel_id=1, source_target_pairs={{0,8},{8,0},{16,24},{24,16},{1,9},{9,1},{17,25},{25,17},{2,10},{10... | collective-permute-start | bytes 98312 | tf_op jit(solution)/shard_map/ppermute | solution.py:17
  8.8 4.8 %collective-permute-start.10 = (f32[2,32,512]{2,1,0:T(8,128)S(1)}, f32[2,32,512]{2,1,0:T(8,128)S(1)}, u32[]{:S(2)}, u32[]{:S(2)}) collective-permute-start(f32[2,32,512]{2,1,0:T(8,128)S(1)} %get-tuple-element.50), channel_id=1, source_target_pairs={{0,8},{8,0},{16,24},{24,16},{1,9},{9,1},{17,25},{25,17},{2,10},{10... | collective-permute-start | bytes 393224 | tf_op jit(solution)/shard_map/ppermute | solution.py:17
  9.1 6.3 %collective-permute-start.4 = (bf16[4,8,1024]{2,1,0:T(8,128)(2,1)S(1)}, bf16[4,8,1024]{2,1,0:T(8,128)(2,1)S(1)}, u32[]{:S(2)}, u32[]{:S(2)}) collective-permute-start(bf16[4,8,1024]{2,1,0:T(8,128)(2,1)S(1)} %shard_map.78.refs_0_), channel_id=1, source_target_pairs={{0,6},{1,7},{2,4},{3,5},{4,2},{5,3},{6,0},{7,1},{8,14},{9,15},{10,... | collective-permute-start | bytes 196616 | tf_op jit(solution)/shard_map/ppermute | solution.py:17
  12.8 5.9 %collective-permute-start.3 = (bf16[4,8,1024]{2,1,0:T(8,128)(2,1)S(1)}, bf16[4,8,1024]{2,1,0:T(8,128)(2,1)S(1)}, u32[]{:S(2)}, u32[]{:S(2)}) collective-permute-start(bf16[4,8,1024]{2,1,0:T(8,128)(2,1)S(1)} %shard_map.78.refs_0_), channel_id=1, source_target_pairs={{0,4},{1,5},{2,6},{3,7},{4,0},{5,1},{6,2},{7,3},{8,12},{9,13},{10,... | collective-permute-start | bytes 196616 | tf_op jit(solution)/shard_map/ppermute | solution.py:17
  12.8 5.9 %collective-permute-start.2 = (bf16[4,8,1024]{2,1,0:T(8,128)(2,1)S(1)}, bf16[4,8,1024]{2,1,0:T(8,128)(2,1)S(1)}, u32[]{:S(2)}, u32[]{:S(2)}) collective-permute-start(bf16[4,8,1024]{2,1,0:T(8,128)(2,1)S(1)} %shard_map.78.refs_0_), channel_id=1, source_target_pairs={{0,2},{1,3},{2,0},{3,1},{4,6},{5,7},{6,4},{7,5},{8,10},{9,11},{10,... | collective-permute-start | bytes 196616 | tf_op jit(solution)/shard_map/ppermute | solution.py:17
  13.8 11.7 %collective-permute-start.12 = (s16[32,2176]{1,0:T(8,128)(2,1)S(1)}, s16[32,2176]{1,0:T(8,128)(2,1)S(1)}, u32[]{:S(2)}, u32[]{:S(2)}) collective-permute-start(s16[32,2176]{1,0:T(8,128)(2,1)S(1)} %get-tuple-element.53), channel_id=1, source_target_pairs={{0,16},{8,24},{16,0},{24,8},{1,17},{9,25},{17,1},{25,9},{2,18},{10... | collective-permute-start | bytes 417800 | tf_op jit(solution)/shard_map/ppermute | solution.py:17
  19.7 8.5 %collective-permute-start.6 = (s16[4,16,2176]{2,1,0:T(8,128)(2,1)S(1)}, s16[4,16,2176]{2,1,0:T(8,128)(2,1)S(1)}, u32[]{:S(2)}, u32[]{:S(2)}) collective-permute-start(s16[4,16,2176]{2,1,0:T(8,128)(2,1)S(1)} %get-tuple-element.44), channel_id=1, source_target_pairs={{0,16},{8,24},{16,0},{24,8},{1,17},{9,25},{17,1},{25,9},{2,18},{10... | collective-permute-start | bytes 835592 | tf_op jit(solution)/shard_map/ppermute | solution.py:17
  20.6 5.0 %collective-permute-start.11 = (bf16[64,1024]{1,0:T(8,128)(2,1)S(1)}, bf16[64,1024]{1,0:T(8,128)(2,1)S(1)}, u32[]{:S(2)}, u32[]{:S(2)}) collective-permute-start(bf16[64,1024]{1,0:T(8,128)(2,1)S(1)} %bitcast.12), channel_id=1, source_target_pairs={{0,1},{1,0},{2,3},{3,2},{4,5},{5,4},{6,7},{7,6},{8,9},{9,8},{10,11... | collective-permute-start | bytes 393224 | tf_op jit(solution)/shard_map/ppermute | solution.py:17
  26.6 7.4 %collective-permute-start.14 = (s16[4,16,2176]{2,1,0:T(8,128)(2,1)S(1)}, s16[4,16,2176]{2,1,0:T(8,128)(2,1)S(1)}, u32[]{:S(2)}, u32[]{:S(2)}) collective-permute-start(s16[4,16,2176]{2,1,0:T(8,128)(2,1)S(1)} %shard_map.84), channel_id=1, source_target_pairs={{0,16},{8,24},{16,0},{24,8},{1,17},{9,25},{17,1},{25,9},{2,18},{10... | collective-permute-start | bytes 835592 | tf_op jit(solution)/shard_map/ppermute | solution.py:17
  28.1 5.0 %collective-permute-start.13 = (bf16[64,1024]{1,0:T(8,128)(2,1)S(1)}, bf16[64,1024]{1,0:T(8,128)(2,1)S(1)}, u32[]{:S(2)}, u32[]{:S(2)}) collective-permute-start(bf16[64,1024]{1,0:T(8,128)(2,1)S(1)} %bitcast.10), channel_id=1, source_target_pairs={{0,1},{1,0},{2,3},{3,2},{4,5},{5,4},{6,7},{7,6},{8,9},{9,8},{10,11... | collective-permute-start | bytes 393224 | tf_op jit(solution)/shard_map/ppermute | solution.py:17
  30.2 13.2 %copy-start.4 = (s32[32]{0:T(128)S(1)}, s32[32]{0:T(128)}, u32[]{:S(2)}) copy-start(s32[32]{0:T(128)} %param.9) | copy-start | bytes 388
  34.5 3.8 %collective-permute-start.15 = (f32[32,128]{1,0:T(8,128)S(1)}, f32[32,128]{1,0:T(8,128)S(1)}, u32[]{:S(2)}, u32[]{:S(2)}) collective-permute-start(f32[32,128]{1,0:T(8,128)S(1)} %get-tuple-element.63.one_ref), channel_id=1, source_target_pairs={{0,1},{1,0},{2,3},{3,2},{4,5},{5,4},{6,7},{7,6},{8,9},{9,8},{10,11... | collective-permute-start | bytes 49160 | tf_op jit(solution)/shard_map/ppermute | solution.py:17
  38.4 3.8 %collective-permute-start.16 = (f32[32,128]{1,0:T(8,128)S(1)}, f32[32,128]{1,0:T(8,128)S(1)}, u32[]{:S(2)}, u32[]{:S(2)}) collective-permute-start(f32[32,128]{1,0:T(8,128)S(1)} %shard_map.86.one_ref), channel_id=1, source_target_pairs={{0,2},{1,3},{2,0},{3,1},{4,6},{5,7},{6,4},{7,5},{8,10},{9,11},{10,... | collective-permute-start | bytes 49160 | tf_op jit(solution)/shard_map/ppermute | solution.py:17
  42.3 4.7 %collective-permute-start.17 = (f32[32,128]{1,0:T(8,128)S(1)}, f32[32,128]{1,0:T(8,128)S(1)}, u32[]{:S(2)}, u32[]{:S(2)}) collective-permute-start(f32[32,128]{1,0:T(8,128)S(1)} %shard_map.87.one_ref), channel_id=1, source_target_pairs={{0,4},{1,5},{2,6},{3,7},{4,0},{5,1},{6,2},{7,3},{8,12},{9,13},{10,... | collective-permute-start | bytes 49160 | tf_op jit(solution)/shard_map/ppermute | solution.py:17
  43.4 3.7 %collective-permute-start.18 = (s32[32]{0:T(128)S(1)}, s32[32]{0:T(128)S(1)}, u32[]{:S(2)}, u32[]{:S(2)}) collective-permute-start(s32[32]{0:T(128)S(1)} %copy-done.4), channel_id=1, source_target_pairs={{0,8},{8,0},{16,24},{24,16},{1,9},{9,1},{17,25},{25,17},{2,10},{10... | collective-permute-start | bytes 392 | tf_op jit(solution)/shard_map/ppermute | solution.py:17
  47.9 5.0 %collective-permute-start.20 = (bf16[32,2048]{1,0:T(8,128)(2,1)S(1)}, bf16[32,2048]{1,0:T(8,128)(2,1)S(1)}, u32[]{:S(2)}, u32[]{:S(2)}) collective-permute-start(bf16[32,2048]{1,0:T(8,128)(2,1)S(1)} %get-tuple-element.64.refs_0_), channel_id=1, source_target_pairs={{0,16},{8,24},{16,0},{24,8},{1,17},{9,25},{17,1},{25,9},{2,18},{10... | collective-permute-start | bytes 393224 | tf_op jit(solution)/shard_map/ppermute | solution.py:17
  48.9 5.4 %collective-permute-start.19 = (bf16[32,2048]{1,0:T(8,128)(2,1)S(1)}, bf16[32,2048]{1,0:T(8,128)(2,1)S(1)}, u32[]{:S(2)}, u32[]{:S(2)}) collective-permute-start(bf16[32,2048]{1,0:T(8,128)(2,1)S(1)} %get-tuple-element.64.refs_0_), channel_id=1, source_target_pairs={{0,8},{8,0},{16,24},{24,16},{1,9},{9,1},{17,25},{25,17},{2,10},{10... | collective-permute-start | bytes 393224 | tf_op jit(solution)/shard_map/ppermute | solution.py:17
  52.9 1.4 %collective-permute-start.21 = (bf16[32,2048]{1,0:T(8,128)(2,1)S(1)}, bf16[32,2048]{1,0:T(8,128)(2,1)S(1)}, u32[]{:S(2)}, u32[]{:S(2)}) collective-permute-start(bf16[32,2048]{1,0:T(8,128)(2,1)S(1)} %collective-permute-done.20.refs_2_), channel_id=1, source_target_pairs={{0,8},{8,0},{16,24},{24,16},{1,9},{9,1},{17,25},{25,17},{2,10},{10... | collective-permute-start | bytes 393224 | tf_op jit(solution)/shard_map/ppermute | solution.py:17
  52.9 1.4 %collective-permute-start.22 = (f32[24,128]{1,0:T(8,128)S(1)}, f32[24,128]{1,0:T(8,128)S(1)}, u32[]{:S(2)}, u32[]{:S(2)}) collective-permute-start(f32[24,128]{1,0:T(8,128)S(1)} %get-tuple-element.65.refs_4_), channel_id=1, source_target_pairs={{0,8},{8,0},{16,24},{24,16},{1,9},{9,1},{17,25},{25,17},{2,10},{10... | collective-permute-start | bytes 36872 | tf_op jit(solution)/shard_map/ppermute | solution.py:17

commit v8 on v7

--- a/solution.py
+++ b/solution.py
@@ -359,7 +359,7 @@
         functools.partial(sum_body, cuts),
         (shape((block, width), f32), coded((block, width + LANES))),
         (mine, *others),
-        after=(sib_head,),
+        after=(part,),
     )
     student_far = swap(give, "teacher", 2)
     away, stay = local(

time: 56.8 us -> 56.8 us (level)
  no operation moved by 1% of the time
where the time goes in v8:
time: 56.8 us; the launch traced here: 56.7 us
  waiting for transfers between devices  25.1 us (44%)
  starting transfers between devices  20.3 us (36%)
  Pallas kernels  7.98 us (14%)
  local copies, waits for them, and re-layouts  2.51 us (4%)
  between operations  0.79 us (1%)
    ppermute x23, waiting for transfers between devices, swap(): return lax.ppermute(value, axis, [(i, i ^ mask) for i in range(count)])  25.1 us
    ppermute x23, starting transfers between devices, swap(): return lax.ppermute(value, axis, [(i, i ^ mask) for i in range(count)])  20.3 us
    pallas_call x15, Pallas kernels, call(): pl.pallas_call(body, out_shape=outs, scratch_shapes=list(scratch), compil...  7.98 us
    unnamed x10, local copies, waits for them, and re-layouts  2.51 us
  transfers between devices with their start and end apart: 23, of which 11 were waited for; matrix products, arithmetic and copies ran while one was open for 0% of the time, Pallas kernels for 7%

profile of v8, /device:TPU:0, one launch (start us, length us, event | category | flops | bytes accessed | tf_op | source)
XLA Modules:
  0.0 56.7 jit_solution(8387110013895305020)
XLA Ops:
  0.6 0.5 collective-permute-start.5
  1.2 2.6 %collective-permute-start = (bf16[16,2048]{1,0:T(8,128)(2,1)}, bf16[16,2048]{1,0:T(8,128)(2,1)S(1)}, u32[]{:S(2)}, u32[]{:S(2)}) collective-permute-start(bf16[16,2048]{1,0:T(8,128)(2,1)} %bitcast.13), channel_id=1, source_target_pairs={{0,16},{8,24},{16,0},{24,8},{1,17},{9,25},{17,1},{25,9},{2,18},{10... | collective-permute-start | bytes 196616 | tf_op jit(solution)/shard_map/ppermute | solution.py:17
  3.7 1.6 %copy-done.1 = bf16[512,2048]{1,0:T(8,128)(2,1)S(1)} copy-done((bf16[512,2048]{1,0:T(8,128)(2,1)S(1)}, bf16[512,2048]{1,0:T(8,128)(2,1)}, u32[]{:S(2)}) %copy-start.1) | copy-done | bytes 2097176
  5.3 0.9 %copy-done.2 = bf16[128,512]{1,0:T(8,128)(2,1)S(1)} copy-done((bf16[128,512]{1,0:T(8,128)(2,1)S(1)}, bf16[128,512]{1,0:T(8,128)(2,1)}, u32[]{:S(2)}) %copy-start.2) | copy-done | bytes 131096
  6.2 0.5 shard_map.76
  6.7 0.2 collective-permute-start.7
  6.9 0.3 collective-permute-start.8
  7.3 0.2 collective-permute-start.9
  7.4 0.1 shard_map.77
  7.5 0.4 collective-permute-start.1
  7.9 0.9 %collective-permute-done.1.sib_ref = bf16[2,8,1024]{2,1,0:T(8,128)(2,1)S(1)} collective-permute-done((bf16[2,8,1024]{2,1,0:T(8,128)(2,1)S(1)}, bf16[2,8,1024]{2,1,0:T(8,128)(2,1)S(1)}, u32[]{:S(2)}, u32[]{:S(2)}) %collective-permute-start.1) | collective-permute-done | bytes 32800 | tf_op jit(solution)/shard_map/ppermute | solution.py:17
  8.8 0.3 collective-permute-start.10
  9.1 0.0 collective-permute-done.7.refs_2_
  9.1 3.7 %collective-permute-start.4 = (bf16[4,8,1024]{2,1,0:T(8,128)(2,1)S(1)}, bf16[4,8,1024]{2,1,0:T(8,128)(2,1)S(1)}, u32[]{:S(2)}, u32[]{:S(2)}) collective-permute-start(bf16[4,8,1024]{2,1,0:T(8,128)(2,1)S(1)} %shard_map.78.refs_0_), channel_id=1, source_target_pairs={{0,6},{1,7},{2,4},{3,5},{4,2},{5,3},{6,0},{7,1},{8,14},{9,15},{10,... | collective-permute-start | bytes 196616 | tf_op jit(solution)/shard_map/ppermute | solution.py:17
  12.8 0.8 %collective-permute-start.2 = (bf16[4,8,1024]{2,1,0:T(8,128)(2,1)S(1)}, bf16[4,8,1024]{2,1,0:T(8,128)(2,1)S(1)}, u32[]{:S(2)}, u32[]{:S(2)}) collective-permute-start(bf16[4,8,1024]{2,1,0:T(8,128)(2,1)S(1)} %shard_map.78.refs_0_), channel_id=1, source_target_pairs={{0,2},{1,3},{2,0},{3,1},{4,6},{5,7},{6,4},{7,5},{8,10},{9,11},{10,... | collective-permute-start | bytes 196616 | tf_op jit(solution)/shard_map/ppermute | solution.py:17
  13.6 0.2 shard_map.81
  13.8 0.8 %collective-permute-start.12 = (s16[32,2176]{1,0:T(8,128)(2,1)S(1)}, s16[32,2176]{1,0:T(8,128)(2,1)S(1)}, u32[]{:S(2)}, u32[]{:S(2)}) collective-permute-start(s16[32,2176]{1,0:T(8,128)(2,1)S(1)} %get-tuple-element.53), channel_id=1, source_target_pairs={{0,16},{8,24},{16,0},{24,8},{1,17},{9,25},{17,1},{25,9},{2,18},{10... | collective-permute-start | bytes 417800 | tf_op jit(solution)/shard_map/ppermute | solution.py:17
  14.6 0.8 %collective-permute-done.4.refs_3_ = bf16[4,8,1024]{2,1,0:T(8,128)(2,1)S(1)} collective-permute-done((bf16[4,8,1024]{2,1,0:T(8,128)(2,1)S(1)}, bf16[4,8,1024]{2,1,0:T(8,128)(2,1)S(1)}, u32[]{:S(2)}, u32[]{:S(2)}) %collective-permute-start.4) | collective-permute-done | bytes 65568 | tf_op jit(solution)/shard_map/ppermute | solution.py:17
  15.5 3.2 %collective-permute-done.3.refs_2_ = bf16[4,8,1024]{2,1,0:T(8,128)(2,1)S(1)} collective-permute-done((bf16[4,8,1024]{2,1,0:T(8,128)(2,1)S(1)}, bf16[4,8,1024]{2,1,0:T(8,128)(2,1)S(1)}, u32[]{:S(2)}, u32[]{:S(2)}) %collective-permute-start.3) | collective-permute-done | bytes 65568 | tf_op jit(solution)/shard_map/ppermute | solution.py:17
  18.7 0.1 shard_map.79
  18.8 0.9 %shard_map.80 = (s16[4,16,2176]{2,1,0:T(8,128)(2,1)S(1)}, f32[4,16,2048]{2,1,0:T(8,128)S(1)}) custom-call(bf16[64,1024]{1,0:T(8,128)(2,1)S(1)} %bitcast.11, bf16[64,1024]{1,0:T(8,128)(2,1)S(1)} %bitcast.9, bf16[512,2048]{1,0:T(8,128)(2,1)S(1)} %copy-done, bf16[512,2048]{1,0:T(8,128)(2,1)S(1)} %collective-permute-done.5.refs_3_.refs_2_), custom_call_target="tpu_custom_call" | custom-call | flops 1 | bytes 1 | tf_op jit(solution)/shard_map/pallas_call | solution.py:21
  19.7 0.9 %collective-permute-start.6 = (s16[4,16,2176]{2,1,0:T(8,128)(2,1)S(1)}, s16[4,16,2176]{2,1,0:T(8,128)(2,1)S(1)}, u32[]{:S(2)}, u32[]{:S(2)}) collective-permute-start(s16[4,16,2176]{2,1,0:T(8,128)(2,1)S(1)} %get-tuple-element.44), channel_id=1, source_target_pairs={{0,16},{8,24},{16,0},{24,8},{1,17},{9,25},{17,1},{25,9},{2,18},{10... | collective-permute-start | bytes 835592 | tf_op jit(solution)/shard_map/ppermute | solution.py:17
  20.6 1.5 %collective-permute-start.11 = (bf16[64,1024]{1,0:T(8,128)(2,1)S(1)}, bf16[64,1024]{1,0:T(8,128)(2,1)S(1)}, u32[]{:S(2)}, u32[]{:S(2)}) collective-permute-start(bf16[64,1024]{1,0:T(8,128)(2,1)S(1)} %bitcast.12), channel_id=1, source_target_pairs={{0,1},{1,0},{2,3},{3,2},{4,5},{5,4},{6,7},{7,6},{8,9},{9,8},{10,11... | collective-permute-start | bytes 393224 | tf_op jit(solution)/shard_map/ppermute | solution.py:17
  22.1 3.4 %collective-permute-done.11.refs_0_ = bf16[64,1024]{1,0:T(8,128)(2,1)S(1)} collective-permute-done((bf16[64,1024]{1,0:T(8,128)(2,1)S(1)}, bf16[64,1024]{1,0:T(8,128)(2,1)S(1)}, u32[]{:S(2)}, u32[]{:S(2)}) %collective-permute-start.11) | collective-permute-done | bytes 131104 | tf_op jit(solution)/shard_map/ppermute | solution.py:17
  25.5 1.0 %shard_map.84 = s16[4,16,2176]{2,1,0:T(8,128)(2,1)S(1)} custom-call(bf16[64,1024]{1,0:T(8,128)(2,1)S(1)} %collective-permute-done.11.refs_0_, bf16[512,2048]{1,0:T(8,128)(2,1)S(1)} %copy-done, bf16[512,2048]{1,0:T(8,128)(2,1)S(1)} %collective-permute-done.5.refs_3_.refs_2_), custom_call_target="tpu_custom_call" | custom-call | flops 1 | bytes 1 | tf_op jit(solution)/shard_map/pallas_call | solution.py:21
  26.6 1.2 %collective-permute-start.14 = (s16[4,16,2176]{2,1,0:T(8,128)(2,1)S(1)}, s16[4,16,2176]{2,1,0:T(8,128)(2,1)S(1)}, u32[]{:S(2)}, u32[]{:S(2)}) collective-permute-start(s16[4,16,2176]{2,1,0:T(8,128)(2,1)S(1)} %shard_map.84), channel_id=1, source_target_pairs={{0,16},{8,24},{16,0},{24,8},{1,17},{9,25},{17,1},{25,9},{2,18},{10... | collective-permute-start | bytes 835592 | tf_op jit(solution)/shard_map/ppermute | solution.py:17
  27.8 0.3 collective-permute-done.6.came_ref
  28.1 1.5 %collective-permute-start.13 = (bf16[64,1024]{1,0:T(8,128)(2,1)S(1)}, bf16[64,1024]{1,0:T(8,128)(2,1)S(1)}, u32[]{:S(2)}, u32[]{:S(2)}) collective-permute-start(bf16[64,1024]{1,0:T(8,128)(2,1)S(1)} %bitcast.10), channel_id=1, source_target_pairs={{0,1},{1,0},{2,3},{3,2},{4,5},{5,4},{6,7},{7,6},{8,9},{9,8},{10,11... | collective-permute-start | bytes 393224 | tf_op jit(solution)/shard_map/ppermute | solution.py:17
  29.7 0.5 shard_map.82
  30.2 2.9 %collective-permute-done.13.refs_0_ = bf16[64,1024]{1,0:T(8,128)(2,1)S(1)} collective-permute-done((bf16[64,1024]{1,0:T(8,128)(2,1)S(1)}, bf16[64,1024]{1,0:T(8,128)(2,1)S(1)}, u32[]{:S(2)}, u32[]{:S(2)}) %collective-permute-start.13) | collective-permute-done | bytes 131104 | tf_op jit(solution)/shard_map/ppermute | solution.py:17
  33.1 0.8 %shard_map.83.kept_ref = f32[4,16,2048]{2,1,0:T(8,128)S(1)} custom-call(bf16[64,1024]{1,0:T(8,128)(2,1)S(1)} %collective-permute-done.13.refs_0_, bf16[512,2048]{1,0:T(8,128)(2,1)S(1)} %copy-done, bf16[512,2048]{1,0:T(8,128)(2,1)S(1)} %collective-permute-done.5.refs_3_.refs_2_), custom_call_target="tpu_custom_call" | custom-call | flops 1 | bytes 1 | tf_op jit(solution)/shard_map/pallas_call | solution.py:21
  33.9 0.0 collective-permute-done.14.came_ref
  34.0 0.5 shard_map.85
  34.5 1.6 %collective-permute-start.15 = (f32[32,128]{1,0:T(8,128)S(1)}, f32[32,128]{1,0:T(8,128)S(1)}, u32[]{:S(2)}, u32[]{:S(2)}) collective-permute-start(f32[32,128]{1,0:T(8,128)S(1)} %get-tuple-element.63.one_ref), channel_id=1, source_target_pairs={{0,1},{1,0},{2,3},{3,2},{4,5},{5,4},{6,7},{7,6},{8,9},{9,8},{10,11... | collective-permute-start | bytes 49160 | tf_op jit(solution)/shard_map/ppermute | solution.py:17
  36.0 2.2 %collective-permute-done.15.two_ref = f32[32,128]{1,0:T(8,128)S(1)} collective-permute-done((f32[32,128]{1,0:T(8,128)S(1)}, f32[32,128]{1,0:T(8,128)S(1)}, u32[]{:S(2)}, u32[]{:S(2)}) %collective-permute-start.15) | collective-permute-done | bytes 16416 | tf_op jit(solution)/shard_map/ppermute | solution.py:17
  38.3 0.1 shard_map.86.one_ref
  38.4 0.9 %collective-permute-start.16 = (f32[32,128]{1,0:T(8,128)S(1)}, f32[32,128]{1,0:T(8,128)S(1)}, u32[]{:S(2)}, u32[]{:S(2)}) collective-permute-start(f32[32,128]{1,0:T(8,128)S(1)} %shard_map.86.one_ref), channel_id=1, source_target_pairs={{0,2},{1,3},{2,0},{3,1},{4,6},{5,7},{6,4},{7,5},{8,10},{9,11},{10,... | collective-permute-start | bytes 49160 | tf_op jit(solution)/shard_map/ppermute | solution.py:17
  39.3 2.9 %collective-permute-done.16.two_ref = f32[32,128]{1,0:T(8,128)S(1)} collective-permute-done((f32[32,128]{1,0:T(8,128)S(1)}, f32[32,128]{1,0:T(8,128)S(1)}, u32[]{:S(2)}, u32[]{:S(2)}) %collective-permute-start.16) | collective-permute-done | bytes 16416 | tf_op jit(solution)/shard_map/ppermute | solution.py:17
  42.2 0.1 shard_map.87.one_ref
  42.3 1.1 %collective-permute-start.17 = (f32[32,128]{1,0:T(8,128)S(1)}, f32[32,128]{1,0:T(8,128)S(1)}, u32[]{:S(2)}, u32[]{:S(2)}) collective-permute-start(f32[32,128]{1,0:T(8,128)S(1)} %shard_map.87.one_ref), channel_id=1, source_target_pairs={{0,4},{1,5},{2,6},{3,7},{4,0},{5,1},{6,2},{7,3},{8,12},{9,13},{10,... | collective-permute-start | bytes 49160 | tf_op jit(solution)/shard_map/ppermute | solution.py:17
  43.4 3.6 %collective-permute-done.17.two_ref = f32[32,128]{1,0:T(8,128)S(1)} collective-permute-done((f32[32,128]{1,0:T(8,128)S(1)}, f32[32,128]{1,0:T(8,128)S(1)}, u32[]{:S(2)}, u32[]{:S(2)}) %collective-permute-start.17) | collective-permute-done | bytes 16416 | tf_op jit(solution)/shard_map/ppermute | solution.py:17
  47.0 0.1 shard_map.88.stats_ref
  47.1 0.8 %shard_map.89 = (f32[24,128]{1,0:T(8,128)S(1)}, bf16[32,2048]{1,0:T(8,128)(2,1)S(1)}) custom-call(f32[4,16,2048]{2,1,0:T(8,128)S(1)} %get-tuple-element.55.own_ref, f32[4,16,2048]{2,1,0:T(8,128)S(1)} %get-tuple-element.60.other_ref, f32[32,2048]{1,0:T(8,128)S(1)} %get-tuple-element.61.student_ref, f32[32,128]{1,0:T(8,128)S(1)} %get-tuple-element.62.tops_ref, ...), custom_call_target="tpu_custom_call" | custom-call | flops 1 | bytes 1 | tf_op jit(solution)/shard_map/pallas_call | solution.py:21
  47.9 1.0 %collective-permute-start.20 = (bf16[32,2048]{1,0:T(8,128)(2,1)S(1)}, bf16[32,2048]{1,0:T(8,128)(2,1)S(1)}, u32[]{:S(2)}, u32[]{:S(2)}) collective-permute-start(bf16[32,2048]{1,0:T(8,128)(2,1)S(1)} %get-tuple-element.64.refs_0_), channel_id=1, source_target_pairs={{0,16},{8,24},{16,0},{24,8},{1,17},{9,25},{17,1},{25,9},{2,18},{10... | collective-permute-start | bytes 393224 | tf_op jit(solution)/shard_map/ppermute | solution.py:17
  48.9 4.0 %collective-permute-done.20.refs_2_ = bf16[32,2048]{1,0:T(8,128)(2,1)S(1)} collective-permute-done((bf16[32,2048]{1,0:T(8,128)(2,1)S(1)}, bf16[32,2048]{1,0:T(8,128)(2,1)S(1)}, u32[]{:S(2)}, u32[]{:S(2)}) %collective-permute-start.20) | collective-permute-done | bytes 131104 | tf_op jit(solution)/shard_map/ppermute | solution.py:17
  52.9 0.5 collective-permute-start.22
  53.4 0.9 %collective-permute-done.22.refs_5_ = f32[24,128]{1,0:T(8,128)S(1)} collective-permute-done((f32[24,128]{1,0:T(8,128)S(1)}, f32[24,128]{1,0:T(8,128)S(1)}, u32[]{:S(2)}, u32[]{:S(2)}) %collective-permute-start.22) | collective-permute-done | bytes 12320 | tf_op jit(solution)/shard_map/ppermute | solution.py:17
  54.3 2.4 %shard_map.90 = (f32[512,2048]{1,0:T(8,128)}, f32[16,32]{1,0:T(8,128)}, f32[4,32]{1,0:T(4,128)}) custom-call(bf16[512,128]{1,0:T(8,128)(2,1)S(1)} %get-tuple-element.36.hidden_ref, bf16[32,2048]{1,0:T(8,128)(2,1)S(1)} %get-tuple-element.64.refs_0_, bf16[32,2048]{1,0:T(8,128)(2,1)S(1)} %collective-permute-done.19.refs_1_, ...), custom_call_target="tpu_custom_call" | custom-call | flops 1 | bytes 1 | tf_op jit(solution)/shard_map/pallas_call | solution.py:21
  (23 shorter events, 0.1 us)
Async XLA Ops:
  0.6 18.1 %copy-start = (bf16[512,2048]{1,0:T(8,128)(2,1)S(1)}, bf16[512,2048]{1,0:T(8,128)(2,1)}, u32[]{:S(2)}) copy-start(bf16[512,2048]{1,0:T(8,128)(2,1)} %refs_1_.3) | copy-start | bytes 6291460
  0.6 18.1 %collective-permute-start.5 = (bf16[512,2048]{1,0:T(8,128)(2,1)}, bf16[512,2048]{1,0:T(8,128)(2,1)S(1)}, u32[]{:S(2)}, u32[]{:S(2)}) collective-permute-start(bf16[512,2048]{1,0:T(8,128)(2,1)} %refs_1_.3), channel_id=1, source_target_pairs={{0,8},{8,0},{16,24},{24,16},{1,9},{9,1},{17,25},{25,17},{2,10},{10... | collective-permute-start | bytes 6291464 | tf_op jit(solution)/shard_map/ppermute | solution.py:17
  1.2 6.3 %collective-permute-start = (bf16[16,2048]{1,0:T(8,128)(2,1)}, bf16[16,2048]{1,0:T(8,128)(2,1)S(1)}, u32[]{:S(2)}, u32[]{:S(2)}) collective-permute-start(bf16[16,2048]{1,0:T(8,128)(2,1)} %bitcast.13), channel_id=1, source_target_pairs={{0,16},{8,24},{16,0},{24,8},{1,17},{9,25},{17,1},{25,9},{2,18},{10... | collective-permute-start | bytes 196616 | tf_op jit(solution)/shard_map/ppermute | solution.py:17
  3.7 1.6 %copy-start.1 = (bf16[512,2048]{1,0:T(8,128)(2,1)S(1)}, bf16[512,2048]{1,0:T(8,128)(2,1)}, u32[]{:S(2)}) copy-start(bf16[512,2048]{1,0:T(8,128)(2,1)} %head_ref.1) | copy-start | bytes 6291460
  5.3 0.9 %copy-start.2 = (bf16[128,512]{1,0:T(8,128)(2,1)S(1)}, bf16[128,512]{1,0:T(8,128)(2,1)}, u32[]{:S(2)}) copy-start(bf16[128,512]{1,0:T(8,128)(2,1)} %hidden_ref.1) | copy-start | bytes 393220
  6.2 1.2 %copy-start.3 = (bf16[1,16,2048]{2,1,0:T(8,128)(2,1)S(1)}, bf16[1,16,2048]{2,1,0:T(8,128)(2,1)}, u32[]{:S(2)}) copy-start(bf16[1,16,2048]{2,1,0:T(8,128)(2,1)} %param.5) | copy-start | bytes 196612
  6.7 2.4 %collective-permute-start.7 = (f32[2,32,512]{2,1,0:T(8,128)S(1)}, f32[2,32,512]{2,1,0:T(8,128)S(1)}, u32[]{:S(2)}, u32[]{:S(2)}) collective-permute-start(f32[2,32,512]{2,1,0:T(8,128)S(1)} %get-tuple-element.47), channel_id=1, source_target_pairs={{0,8},{8,0},{16,24},{24,16},{1,9},{9,1},{17,25},{25,17},{2,10},{10... | collective-permute-start | bytes 393224 | tf_op jit(solution)/shard_map/ppermute | solution.py:17
  6.9 5.9 %collective-permute-start.8 = (f32[2,32,512]{2,1,0:T(8,128)S(1)}, f32[2,32,512]{2,1,0:T(8,128)S(1)}, u32[]{:S(2)}, u32[]{:S(2)}) collective-permute-start(f32[2,32,512]{2,1,0:T(8,128)S(1)} %get-tuple-element.48), channel_id=1, source_target_pairs={{0,8},{8,0},{16,24},{24,16},{1,9},{9,1},{17,25},{25,17},{2,10},{10... | collective-permute-start | bytes 393224 | tf_op jit(solution)/shard_map/ppermute | solution.py:17
  7.3 5.5 %collective-permute-start.9 = (f32[2,32,512]{2,1,0:T(8,128)S(1)}, f32[2,32,512]{2,1,0:T(8,128)S(1)}, u32[]{:S(2)}, u32[]{:S(2)}) collective-permute-start(f32[2,32,512]{2,1,0:T(8,128)S(1)} %get-tuple-element.49), channel_id=1, source_target_pairs={{0,8},{8,0},{16,24},{24,16},{1,9},{9,1},{17,25},{25,17},{2,10},{10... | collective-permute-start | bytes 393224 | tf_op jit(solution)/shard_map/ppermute | solution.py:17
  7.5 1.3 %collective-permute-start.1 = (bf16[2,8,1024]{2,1,0:T(8,128)(2,1)S(1)}, bf16[2,8,1024]{2,1,0:T(8,128)(2,1)S(1)}, u32[]{:S(2)}, u32[]{:S(2)}) collective-permute-start(bf16[2,8,1024]{2,1,0:T(8,128)(2,1)S(1)} %get-tuple-element.38), channel_id=1, source_target_pairs={{0,8},{8,0},{16,24},{24,16},{1,9},{9,1},{17,25},{25,17},{2,10},{10... | collective-permute-start | bytes 98312 | tf_op jit(solution)/shard_map/ppermute | solution.py:17
  8.8 4.8 %collective-permute-start.10 = (f32[2,32,512]{2,1,0:T(8,128)S(1)}, f32[2,32,512]{2,1,0:T(8,128)S(1)}, u32[]{:S(2)}, u32[]{:S(2)}) collective-permute-start(f32[2,32,512]{2,1,0:T(8,128)S(1)} %get-tuple-element.50), channel_id=1, source_target_pairs={{0,8},{8,0},{16,24},{24,16},{1,9},{9,1},{17,25},{25,17},{2,10},{10... | collective-permute-start | bytes 393224 | tf_op jit(solution)/shard_map/ppermute | solution.py:17
  9.1 6.3 %collective-permute-start.4 = (bf16[4,8,1024]{2,1,0:T(8,128)(2,1)S(1)}, bf16[4,8,1024]{2,1,0:T(8,128)(2,1)S(1)}, u32[]{:S(2)}, u32[]{:S(2)}) collective-permute-start(bf16[4,8,1024]{2,1,0:T(8,128)(2,1)S(1)} %shard_map.78.refs_0_), channel_id=1, source_target_pairs={{0,6},{1,7},{2,4},{3,5},{4,2},{5,3},{6,0},{7,1},{8,14},{9,15},{10,... | collective-permute-start | bytes 196616 | tf_op jit(solution)/shard_map/ppermute | solution.py:17
  12.8 5.9 %collective-permute-start.3 = (bf16[4,8,1024]{2,1,0:T(8,128)(2,1)S(1)}, bf16[4,8,1024]{2,1,0:T(8,128)(2,1)S(1)}, u32[]{:S(2)}, u32[]{:S(2)}) collective-permute-start(bf16[4,8,1024]{2,1,0:T(8,128)(2,1)S(1)} %shard_map.78.refs_0_), channel_id=1, source_target_pairs={{0,4},{1,5},{2,6},{3,7},{4,0},{5,1},{6,2},{7,3},{8,12},{9,13},{10,... | collective-permute-start | bytes 196616 | tf_op jit(solution)/shard_map/ppermute | solution.py:17
  12.8 5.9 %collective-permute-start.2 = (bf16[4,8,1024]{2,1,0:T(8,128)(2,1)S(1)}, bf16[4,8,1024]{2,1,0:T(8,128)(2,1)S(1)}, u32[]{:S(2)}, u32[]{:S(2)}) collective-permute-start(bf16[4,8,1024]{2,1,0:T(8,128)(2,1)S(1)} %shard_map.78.refs_0_), channel_id=1, source_target_pairs={{0,2},{1,3},{2,0},{3,1},{4,6},{5,7},{6,4},{7,5},{8,10},{9,11},{10,... | collective-permute-start | bytes 196616 | tf_op jit(solution)/shard_map/ppermute | solution.py:17
  13.8 8.3 %collective-permute-start.12 = (s16[32,2176]{1,0:T(8,128)(2,1)S(1)}, s16[32,2176]{1,0:T(8,128)(2,1)S(1)}, u32[]{:S(2)}, u32[]{:S(2)}) collective-permute-start(s16[32,2176]{1,0:T(8,128)(2,1)S(1)} %get-tuple-element.53), channel_id=1, source_target_pairs={{0,16},{8,24},{16,0},{24,8},{1,17},{9,25},{17,1},{25,9},{2,18},{10... | collective-permute-start | bytes 417800 | tf_op jit(solution)/shard_map/ppermute | solution.py:17
  19.7 8.4 %collective-permute-start.6 = (s16[4,16,2176]{2,1,0:T(8,128)(2,1)S(1)}, s16[4,16,2176]{2,1,0:T(8,128)(2,1)S(1)}, u32[]{:S(2)}, u32[]{:S(2)}) collective-permute-start(s16[4,16,2176]{2,1,0:T(8,128)(2,1)S(1)} %get-tuple-element.44), channel_id=1, source_target_pairs={{0,16},{8,24},{16,0},{24,8},{1,17},{9,25},{17,1},{25,9},{2,18},{10... | collective-permute-start | bytes 835592 | tf_op jit(solution)/shard_map/ppermute | solution.py:17
  20.6 5.0 %collective-permute-start.11 = (bf16[64,1024]{1,0:T(8,128)(2,1)S(1)}, bf16[64,1024]{1,0:T(8,128)(2,1)S(1)}, u32[]{:S(2)}, u32[]{:S(2)}) collective-permute-start(bf16[64,1024]{1,0:T(8,128)(2,1)S(1)} %bitcast.12), channel_id=1, source_target_pairs={{0,1},{1,0},{2,3},{3,2},{4,5},{5,4},{6,7},{7,6},{8,9},{9,8},{10,11... | collective-permute-start | bytes 393224 | tf_op jit(solution)/shard_map/ppermute | solution.py:17
  26.6 7.4 %collective-permute-start.14 = (s16[4,16,2176]{2,1,0:T(8,128)(2,1)S(1)}, s16[4,16,2176]{2,1,0:T(8,128)(2,1)S(1)}, u32[]{:S(2)}, u32[]{:S(2)}) collective-permute-start(s16[4,16,2176]{2,1,0:T(8,128)(2,1)S(1)} %shard_map.84), channel_id=1, source_target_pairs={{0,16},{8,24},{16,0},{24,8},{1,17},{9,25},{17,1},{25,9},{2,18},{10... | collective-permute-start | bytes 835592 | tf_op jit(solution)/shard_map/ppermute | solution.py:17
  28.1 5.0 %collective-permute-start.13 = (bf16[64,1024]{1,0:T(8,128)(2,1)S(1)}, bf16[64,1024]{1,0:T(8,128)(2,1)S(1)}, u32[]{:S(2)}, u32[]{:S(2)}) collective-permute-start(bf16[64,1024]{1,0:T(8,128)(2,1)S(1)} %bitcast.10), channel_id=1, source_target_pairs={{0,1},{1,0},{2,3},{3,2},{4,5},{5,4},{6,7},{7,6},{8,9},{9,8},{10,11... | collective-permute-start | bytes 393224 | tf_op jit(solution)/shard_map/ppermute | solution.py:17
  30.2 13.2 %copy-start.4 = (s32[32]{0:T(128)S(1)}, s32[32]{0:T(128)}, u32[]{:S(2)}) copy-start(s32[32]{0:T(128)} %param.9) | copy-start | bytes 388
  34.5 3.8 %collective-permute-start.15 = (f32[32,128]{1,0:T(8,128)S(1)}, f32[32,128]{1,0:T(8,128)S(1)}, u32[]{:S(2)}, u32[]{:S(2)}) collective-permute-start(f32[32,128]{1,0:T(8,128)S(1)} %get-tuple-element.63.one_ref), channel_id=1, source_target_pairs={{0,1},{1,0},{2,3},{3,2},{4,5},{5,4},{6,7},{7,6},{8,9},{9,8},{10,11... | collective-permute-start | bytes 49160 | tf_op jit(solution)/shard_map/ppermute | solution.py:17
  38.4 3.8 %collective-permute-start.16 = (f32[32,128]{1,0:T(8,128)S(1)}, f32[32,128]{1,0:T(8,128)S(1)}, u32[]{:S(2)}, u32[]{:S(2)}) collective-permute-start(f32[32,128]{1,0:T(8,128)S(1)} %shard_map.86.one_ref), channel_id=1, source_target_pairs={{0,2},{1,3},{2,0},{3,1},{4,6},{5,7},{6,4},{7,5},{8,10},{9,11},{10,... | collective-permute-start | bytes 49160 | tf_op jit(solution)/shard_map/ppermute | solution.py:17
  42.3 4.7 %collective-permute-start.17 = (f32[32,128]{1,0:T(8,128)S(1)}, f32[32,128]{1,0:T(8,128)S(1)}, u32[]{:S(2)}, u32[]{:S(2)}) collective-permute-start(f32[32,128]{1,0:T(8,128)S(1)} %shard_map.87.one_ref), channel_id=1, source_target_pairs={{0,4},{1,5},{2,6},{3,7},{4,0},{5,1},{6,2},{7,3},{8,12},{9,13},{10,... | collective-permute-start | bytes 49160 | tf_op jit(solution)/shard_map/ppermute | solution.py:17
  43.4 3.7 %collective-permute-start.18 = (s32[32]{0:T(128)S(1)}, s32[32]{0:T(128)S(1)}, u32[]{:S(2)}, u32[]{:S(2)}) collective-permute-start(s32[32]{0:T(128)S(1)} %copy-done.4), channel_id=1, source_target_pairs={{0,8},{8,0},{16,24},{24,16},{1,9},{9,1},{17,25},{25,17},{2,10},{10... | collective-permute-start | bytes 392 | tf_op jit(solution)/shard_map/ppermute | solution.py:17
  47.9 5.0 %collective-permute-start.20 = (bf16[32,2048]{1,0:T(8,128)(2,1)S(1)}, bf16[32,2048]{1,0:T(8,128)(2,1)S(1)}, u32[]{:S(2)}, u32[]{:S(2)}) collective-permute-start(bf16[32,2048]{1,0:T(8,128)(2,1)S(1)} %get-tuple-element.64.refs_0_), channel_id=1, source_target_pairs={{0,16},{8,24},{16,0},{24,8},{1,17},{9,25},{17,1},{25,9},{2,18},{10... | collective-permute-start | bytes 393224 | tf_op jit(solution)/shard_map/ppermute | solution.py:17
  48.9 5.4 %collective-permute-start.19 = (bf16[32,2048]{1,0:T(8,128)(2,1)S(1)}, bf16[32,2048]{1,0:T(8,128)(2,1)S(1)}, u32[]{:S(2)}, u32[]{:S(2)}) collective-permute-start(bf16[32,2048]{1,0:T(8,128)(2,1)S(1)} %get-tuple-element.64.refs_0_), channel_id=1, source_target_pairs={{0,8},{8,0},{16,24},{24,16},{1,9},{9,1},{17,25},{25,17},{2,10},{10... | collective-permute-start | bytes 393224 | tf_op jit(solution)/shard_map/ppermute | solution.py:17
  52.9 1.4 %collective-permute-start.21 = (bf16[32,2048]{1,0:T(8,128)(2,1)S(1)}, bf16[32,2048]{1,0:T(8,128)(2,1)S(1)}, u32[]{:S(2)}, u32[]{:S(2)}) collective-permute-start(bf16[32,2048]{1,0:T(8,128)(2,1)S(1)} %collective-permute-done.20.refs_2_), channel_id=1, source_target_pairs={{0,8},{8,0},{16,24},{24,16},{1,9},{9,1},{17,25},{25,17},{2,10},{10... | collective-permute-start | bytes 393224 | tf_op jit(solution)/shard_map/ppermute | solution.py:17
  52.9 1.4 %collective-permute-start.22 = (f32[24,128]{1,0:T(8,128)S(1)}, f32[24,128]{1,0:T(8,128)S(1)}, u32[]{:S(2)}, u32[]{:S(2)}) collective-permute-start(f32[24,128]{1,0:T(8,128)S(1)} %get-tuple-element.65.refs_4_), channel_id=1, source_target_pairs={{0,8},{8,0},{16,24},{24,16},{1,9},{9,1},{17,25},{25,17},{2,10},{10... | collective-permute-start | bytes 36872 | tf_op jit(solution)/shard_map/ppermute | solution.py:17
